TPU v7x, 512 devices: a whole 4x8x8 slice. The times are simulated.
512 devices in a mesh: row: 32 (over z, x), col: 16 (over y, core).
Axes of the slice: x: 4, y: 8, z: 8, core: 2. Of those that a mesh axis runs over, the one named last changes fastest.
Arguments:
- transfer: float32 [32768, 2048], P('row', 'col'), may hold values from -0.125 to 0.125
- emissions: float32 [2048, 4096], P('row', 'col'), may hold values from -6 to 6
Outputs:
- deposit: float32 [32768, 4096], P('row', 'col')
- checksum_rows: float32 [2, 4096], P(None, 'col')
- checksum_cols: float32 [2, 32768], P(None, 'row')
All inputs are finite; a program needn't handle non-finite values.
Results may differ from a plain program's by a relative error of at most 0.00011.
Values sent between devices are 32-bit elements; how exact they have to be, the bound alone decides.
No kernel may reach another device: no remote copies, remote signals or barrier semaphores. Data moves between devices by JAX's collectives and lax.ppermute only.
A program may use at most 64 MiB of HBM per device.

v0:
```python
import jax
import jax.numpy as jnp
from jax import lax
from jax.sharding import PartitionSpec as P


def check_weights(total, start, count):
    index = (start + jnp.arange(count, dtype=jnp.int32)).astype(jnp.float32)
    flat = jnp.full((count,), 1.0, jnp.float32) / jnp.sqrt(jnp.float32(total))
    ramp = (index + 0.5) / total * jnp.sqrt(jnp.float32(3.0) / total)
    return jnp.stack([flat, ramp], 0)


def on_device(transfer, emissions):
    m_local = transfer.shape[0]
    s_local = emissions.shape[1]
    total_rows = m_local * lax.axis_size("row")
    total_cols = s_local * lax.axis_size("col")
    receptor_local = check_weights(total_rows, lax.axis_index("row") * m_local, m_local)
    scenario_local = check_weights(total_cols, lax.axis_index("col") * s_local, s_local)
    highest = lax.Precision.HIGHEST
    whole_right = lax.all_gather(emissions, "row", axis=0, tiled=True)
    main = jnp.dot(
        lax.all_gather(transfer, "col", axis=1, tiled=True),
        whole_right,
        precision=highest,
        preferred_element_type=jnp.float32,
    )
    local_rows = jnp.dot(
        receptor_local, main, precision=highest, preferred_element_type=jnp.float32
    )
    checksum_rows = lax.psum(local_rows, "row")
    local_cols = jnp.einsum(
        "js,ms->jm", scenario_local, main, precision=highest, preferred_element_type=jnp.float32
    )
    checksum_cols = lax.psum(local_cols, "col")
    return (main, checksum_rows, checksum_cols)


def solution(mesh):
    placed = (P("row", "col"), P("row", "col"))
    return jax.shard_map(
        on_device,
        mesh=mesh,
        in_specs=placed,
        out_specs=(P("row", "col"), P(None, "col"), P(None, "row")),
        check_vma=False,
    )
```

profile of v0, /device:TPU:32, one launch (start us, length us, event | category | flops | bytes accessed | tf_op | source)
XLA Modules:
  0.0 282.8 jit_solution(683051703549750667)
XLA Ops:
  7.2 0.0 all-gather.5.cloned.1.call-start
  7.2 0.7 all-gather.5.cloned.1.call-update
  7.9 0.0 all-gather.3.cloned.1.call-start
  7.9 0.7 all-gather.3.cloned.1.call-update
  8.7 90.8 %all-gather.5.cloned.1.call-done = f32[2048,256]{1,0:T(8,128)} async-done(((f32[64,256]{1,0:T(8,128)}), f32[2048,256]{1,0:T(8,128)}) %all-gather.5.cloned.1.call-update) | async-done | bytes 2097168 | tf_op jit(solution)/shard_map/all_gather | solution.py:22
  99.5 62.9 %all-gather.3.cloned.1.call-done = f32[1024,2048]{1,0:T(8,128)} async-done(((f32[1024,128]{1,0:T(8,128)}), f32[1024,2048]{1,0:T(8,128)}) %all-gather.3.cloned.1.call-update) | async-done | bytes 8388624 | tf_op jit(solution)/shard_map/all_gather | solution.py:24
  162.4 9.3 %fusion.6 = f32[1024,256]{1,0:T(8,128)S(1)} fusion(f32[1024,2048]{1,0:T(8,128)} %all-gather.3.cloned.1.call-done, f32[2048,256]{1,0:T(8,128)} %all-gather.5.cloned.1.call-done), kind=kOutput, calls=%fused_computation.8 | convolution fusion | flops 6442450944 | bytes 11534336 | tf_op jit(solution)/shard_map/dot_general | solution.py:23
  171.8 0.0 copy-start
  171.8 1.0 fusion.2
  172.8 26.6 %psum.15 = f32[2,1024]{1,0:T(2,128)} all-reduce(f32[2,1024]{1,0:T(2,128)S(1)} %fusion.2), channel_id=1, replica_groups=mesh['row'=32,'col'=16] {'col'}, use_global_device_ids=true, to_apply=%region_1.0 | all-reduce | flops 2048 | bytes 16384 | tf_op jit(solution)/shard_map/psum | solution.py:36
  199.3 0.5 fusion
  199.9 76.1 %psum.14 = f32[2,256]{1,0:T(2,128)} all-reduce(f32[2,256]{1,0:T(2,128)S(1)} %fusion), channel_id=1, replica_groups=mesh['row'=32,'col'=16] {'row'}, use_global_device_ids=true, to_apply=%region_0.0 | all-reduce | flops 512 | bytes 4096 | tf_op jit(solution)/shard_map/psum | solution.py:32
  276.0 0.0 copy-done
  (2 shorter events, 0.0 us)
Async XLA Ops:
  7.2 92.3 %all-gather.5.cloned.1.call-start = ((), (), s32[]{:S(2)}) async-start(), calls=%async_computation.1 | async-start | bytes 2162688 | tf_op jit(solution)/shard_map/all_gather | solution.py:22
  7.9 154.5 %all-gather.3.cloned.1.call-start = ((), (), s32[]{:S(2)}) async-start(), calls=%async_computation | async-start | bytes 8912896 | tf_op jit(solution)/shard_map/all_gather | solution.py:24
  171.8 104.2 %copy-start = (f32[1024,256]{1,0:T(8,128)}, f32[1024,256]{1,0:T(8,128)S(1)}, u32[]{:S(2)}) copy-start(f32[1024,256]{1,0:T(8,128)S(1)} %fusion.6) | copy-start | bytes 3145732
Sparse Core Ops, SparseCore 0:
  11.2 88.2 all-gather.4
  101.5 60.8 all-gather.2
where the time goes:
time: 283 us
  waiting for transfers between devices  155 us (55%)
  blocking collectives  103 us (36%)
  between operations  14.1 us (5%)
  matrix products  10.8 us (4%)
    all_gather x1, waiting for transfers between devices, on_device(): whole_right = lax.all_gather(emissions, 'row', axis=0, tiled=True)  90.8 us
    psum x1, blocking collectives, on_device(): checksum_rows = lax.psum(local_rows, 'row')  76.1 us
    all_gather x1, waiting for transfers between devices, on_device(): lax.all_gather(transfer, 'col', axis=1, tiled=True)  62.9 us
    psum x1, blocking collectives, on_device(): checksum_cols = lax.psum(local_cols, 'col')  26.6 us
    dot_general x1, matrix products, on_device(): jnp.dot(lax.all_gather(transfer, 'col', axis=1, tiled=True), whole_right,...  9.35 us
  transfers between devices with their start and end apart: 2, of which 2 were waited for; matrix products, arithmetic and copies ran while one was open for 0% of the time, Pallas kernels for 0%

commit v1 on v0

v1 whole, which is shorter than its diff:
```python
import jax
import jax.numpy as jnp
from jax import lax
from jax.experimental import pallas as pl
from jax.experimental.pallas import tpu as pltpu
from jax.sharding import PartitionSpec as P

NX, NY, NZ = 4, 8, 8
STEP = 256
EXTRA = 8
VMEM = 48 * 1024 * 1024

Y_GROUPS = [[2 * y + c for y in range(NY)] for c in range(2)]
Z_GROUPS = [[NX * z + x for z in range(NZ)] for x in range(NX)]
SIBLING = [(j, j ^ 1) for j in range(2 * NY)]


def along_y(shift):
    return [(2 * y + c, 2 * ((y + shift) % NY) + c) for y in range(NY) for c in range(2)]


def spread(j):
    pairs = []
    for z in range(NZ):
        for x in range(NX):
            for y in range(NY):
                for c in range(2):
                    to = (2 * (x % 2) + c + j) % NX
                    pairs.append(((NX * z + x) * 2 * NY + 2 * y + c, (NX * z + to) * 2 * NY + 2 * y + x // 2))
    return pairs


def check_weights(total, start, count):
    index = (start + jnp.arange(count, dtype=jnp.int32)).astype(jnp.float32)
    flat = jnp.full((count,), 1.0, jnp.float32) / jnp.sqrt(jnp.float32(total))
    ramp = (index + 0.5) / total * jnp.sqrt(jnp.float32(3.0) / total)
    return jnp.stack([flat, ramp], 0)


def halves(value):
    high = value.astype(jnp.bfloat16)
    return high, (value - high.astype(jnp.float32)).astype(jnp.bfloat16)


def dot(left, right, contract=((1,), (0,))):
    return lax.dot_general(left, right, (contract, ((), ())), preferred_element_type=jnp.float32)


def product_kernel(place, *refs):
    blocks, (p4, m4, e, u, v, own, send, eh, el, vh, vl, sums) = refs[:7], refs[7:]
    y, c, i = place[0], place[1], pl.program_id(0)
    first = c == 0

    @pl.when(i == 0)
    def _():
        us = jnp.concatenate([u[k] for k in range(NY)], 1)
        sums[...] = lax.dot_general(
            us, e[...], (((1,), (0,)), ((), ())),
            precision=lax.Precision.HIGHEST, preferred_element_type=jnp.float32,
        )
        vs = []
        for k, shift in enumerate((0, -1, 1, -2, 2, -3, 3, 4)):
            at = lax.rem(y + shift + NY, NY)
            block = e[pl.ds(pl.multiple_of(at * 128, 128), 128), :]
            left, right = block[:, :256], block[:, 256:]
            block = jnp.concatenate([jnp.where(first, left, right), jnp.where(first, right, left)], 1)
            eh[k * 128 : (k + 1) * 128, :], el[k * 128 : (k + 1) * 128, :] = halves(block)
            vs.append(v[at])
        vh[...], vl[...] = halves(jnp.concatenate(vs, 1))

    last = jnp.where(i < 2, p4[...], m4[...])
    th, tl = halves(jnp.concatenate([b[...] for b in blocks] + [last], 1))
    out = dot(th, eh[...]) + (dot(tl, eh[...]) + dot(th, el[...]))
    lanes = ((1,), (1,))
    cols = dot(vh[...], th, lanes) + (dot(vl[...], th, lanes) + dot(vh[...], tl, lanes))
    own[:STEP, :] = out[:, :256]
    send[:STEP, :] = out[:, 256:]
    rows = sums[...]
    left, right = rows[:, :256], rows[:, 256:]
    zeros = jnp.zeros((EXTRA - 4, 256), jnp.float32)
    own[STEP:, :] = jnp.concatenate([cols, jnp.where(first, left, right), zeros], 0)
    send[STEP:, :] = jnp.concatenate([cols, jnp.where(first, right, left), zeros], 0)


def product(place, blocks, p4, m4, e, u, v):
    steps = blocks[0].shape[0] // STEP
    half = steps // 2
    whole = lambda a: pl.BlockSpec(a.shape, lambda i, s: (0,) * a.ndim)
    tall = STEP + EXTRA
    shape = jax.ShapeDtypeStruct((steps * tall, 256), jnp.float32)
    depth = e.shape[0]
    return pl.pallas_call(
        product_kernel,
        out_shape=(shape, shape),
        grid_spec=pltpu.PrefetchScalarGridSpec(
            num_scalar_prefetch=1,
            grid=(steps,),
            in_specs=[pl.BlockSpec((STEP, 128), lambda i, s: (i, 0))] * 7
            + [
                pl.BlockSpec((STEP, 128), lambda i, s: (jnp.minimum(i, half - 1), 0)),
                pl.BlockSpec((STEP, 128), lambda i, s: (jnp.maximum(i - half, 0), 0)),
                whole(e), whole(u), whole(v),
            ],
            out_specs=[pl.BlockSpec((tall, 256), lambda i, s: (i, 0))] * 2,
            scratch_shapes=[
                pltpu.VMEM((depth, 512), jnp.bfloat16),
                pltpu.VMEM((depth, 512), jnp.bfloat16),
                pltpu.VMEM((2, depth), jnp.bfloat16),
                pltpu.VMEM((2, depth), jnp.bfloat16),
                pltpu.VMEM((2, 512), jnp.float32),
            ],
        ),
        compiler_params=pltpu.CompilerParams(vmem_limit_bytes=VMEM),
    )(place, *blocks, p4, m4, e, u, v)


def join_kernel(own, other, main, rows, cols):
    total = own[...] + other[...]
    main[...] = total[:STEP]
    cols[...] = total[STEP : STEP + 2]
    rows[...] = total[STEP + 2 : STEP + 4]


def join(own, other):
    tall = STEP + EXTRA
    steps = own.shape[0] // tall
    return pl.pallas_call(
        join_kernel,
        out_shape=(
            jax.ShapeDtypeStruct((steps * STEP, 256), jnp.float32),
            jax.ShapeDtypeStruct((2, 256), jnp.float32),
            jax.ShapeDtypeStruct((2, steps * STEP), jnp.float32),
        ),
        grid=(steps,),
        in_specs=[pl.BlockSpec((tall, 256), lambda i: (i, 0))] * 2,
        out_specs=[
            pl.BlockSpec((STEP, 256), lambda i: (i, 0)),
            pl.BlockSpec((2, 256), lambda i: (0, 0)),
            pl.BlockSpec((2, STEP), lambda i: (0, i)),
        ],
    )(own, other)


def to_all(value, axis, count, groups=None):
    copies = jnp.broadcast_to(value[None], (count,) + value.shape)
    return lax.all_to_all(copies, axis, split_axis=0, concat_axis=0, axis_index_groups=groups)


def on_device(transfer, emissions):
    highest = lax.Precision.HIGHEST
    row, col = lax.axis_index("row"), lax.axis_index("col")
    x, y, c = lax.rem(row, NX), col // 2, lax.rem(col, 2)
    m_local = transfer.shape[0]
    up = lambda a: lax.ppermute(a, "col", along_y(1))
    down = lambda a: lax.ppermute(a, "col", along_y(-1))

    p1, m1 = up(transfer), down(transfer)
    p2, m2 = up(p1), down(m1)
    p3, m3 = up(p2), down(m2)
    p4, m4 = up(p3[: m_local // 2]), down(m3[m_local // 2 :])

    got = jnp.stack([lax.ppermute(emissions, ("row", "col"), spread(j)) for j in range(NX)])
    pick = [lax.dynamic_index_in_dim(got, lax.rem(x - s + NX, NX), keepdims=False) for s in range(NX)]
    near = jnp.concatenate(
        [jnp.concatenate(pick[:2], 1), jnp.concatenate(pick[2:], 1)], 0
    )
    whole = lax.all_gather(near, "row", axis=0, tiled=True, axis_index_groups=Z_GROUPS)

    receptor = check_weights(m_local * lax.axis_size("row"), row * m_local, m_local)
    u = jnp.dot(receptor, transfer, precision=highest, preferred_element_type=jnp.float32)
    u = to_all(u, "row", NX * NZ).sum(0)
    u = to_all(u, "col", NY, Y_GROUPS)

    scenario = check_weights(256 * lax.axis_size("col"), y * 512, 512)
    v = jnp.einsum("js,ks->jk", scenario, near, precision=highest, preferred_element_type=jnp.float32)
    v = to_all(v, "col", NY, Y_GROUPS).sum(0)
    v = to_all(v, "row", NZ, Z_GROUPS)

    place = jnp.stack([y, c]).astype(jnp.int32)
    own, send = product(place, [transfer, p1, m1, p2, m2, p3, m3], p4, m4, whole, u, v)
    other = lax.ppermute(send, "col", SIBLING)
    return join(own, other)


def solution(mesh):
    placed = (P("row", "col"), P("row", "col"))
    return jax.shard_map(
        on_device,
        mesh=mesh,
        in_specs=placed,
        out_specs=(P("row", "col"), P(None, "col"), P(None, "row")),
        check_vma=False,
    )
```

time: 283 us -> 157 us (0.55)
  the two profiles are of different devices: /device:TPU:32 before, /device:TPU:1 now
where the time goes in v1:
time: 157 us; the launch traced here: 156 us
  starting transfers between devices  76.8 us (49%)
  waiting for transfers between devices  41.6 us (26%)
  between operations  14.3 us (9%)
  Pallas kernels  13.5 us (9%)
  local copies, waits for them, and re-layouts  6.59 us (4%)
  other arithmetic  1.66 us (1%)
    all_to_all x4, starting transfers between devices, to_all(): lax.all_to_all(copies, axis, split_axis=0, concat_axis=0, axis_index_grou...  24.8 us
    all_to_all x4, waiting for transfers between devices, to_all(): lax.all_to_all(copies, axis, split_axis=0, concat_axis=0, axis_index_grou...  18.8 us
    ppermute x4, starting transfers between devices, on_device(): lax.ppermute(emissions, ('row', 'col'), spread(j))  18.7 us
    ppermute x4, waiting for transfers between devices, on_device(): down = lambda a: lax.ppermute(a, 'col', along_y(-1))  18.2 us
    ppermute x4, starting transfers between devices, on_device(): down = lambda a: lax.ppermute(a, 'col', along_y(-1))  15.1 us
    pallas_call x1, Pallas kernels, product(): pl.pallas_call(product_kernel, out_shape=(shape, shape), grid_spec=pltpu....  9.95 us
    ppermute x4, starting transfers between devices, on_device(): up = lambda a: lax.ppermute(a, 'col', along_y(1))  9.11 us
    ppermute x1, starting transfers between devices, on_device(): other = lax.ppermute(send, 'col', SIBLING)  9.04 us
  transfers between devices with their start and end apart: 18, of which 7 were waited for; matrix products, arithmetic and copies ran while one was open for 4% of the time, Pallas kernels for 0%

profile of v1, /device:TPU:1, one launch (start us, length us, event | category | flops | bytes accessed | tf_op | source)
XLA Modules:
  0.0 156.1 jit_solution(18436303690476202199)
XLA Ops:
  7.2 6.2 %collective-permute-start.9 = (f32[64,256]{1,0:T(8,128)}, f32[64,256]{1,0:T(8,128)S(1)}, u32[]{:S(2)}, u32[]{:S(2)}) collective-permute-start(f32[64,256]{1,0:T(8,128)} %param.3), channel_id=1, source_target_pairs={{0,16},{1,32},{2,18},{3,34},{4,20},{5,36},{6,22},{7,38},{8,24},{9,... | collective-permute-start | bytes 196616 | tf_op jit(solution)/shard_map/ppermute | solution.py:162
  13.4 2.5 %collective-permute-start.8 = (f32[64,256]{1,0:T(8,128)}, f32[64,256]{1,0:T(8,128)S(1)}, u32[]{:S(2)}, u32[]{:S(2)}) collective-permute-start(f32[64,256]{1,0:T(8,128)} %param.3), channel_id=1, source_target_pairs={{0,0},{1,16},{2,2},{3,18},{4,4},{5,20},{6,6},{7,22},{8,8},{9,24},{... | collective-permute-start | bytes 196616 | tf_op jit(solution)/shard_map/ppermute | solution.py:162
  15.9 3.6 %collective-permute-start.11 = (f32[64,256]{1,0:T(8,128)}, f32[64,256]{1,0:T(8,128)S(1)}, u32[]{:S(2)}, u32[]{:S(2)}) collective-permute-start(f32[64,256]{1,0:T(8,128)} %param.3), channel_id=1, source_target_pairs={{0,48},{1,0},{2,50},{3,2},{4,52},{5,4},{6,54},{7,6},{8,56},{9,8},{... | collective-permute-start | bytes 196616 | tf_op jit(solution)/shard_map/ppermute | solution.py:162
  19.6 6.4 %collective-permute-start.10 = (f32[64,256]{1,0:T(8,128)}, f32[64,256]{1,0:T(8,128)S(1)}, u32[]{:S(2)}, u32[]{:S(2)}) collective-permute-start(f32[64,256]{1,0:T(8,128)} %param.3), channel_id=1, source_target_pairs={{0,32},{1,48},{2,34},{3,50},{4,36},{5,52},{6,38},{7,54},{8,40},{9,... | collective-permute-start | bytes 196616 | tf_op jit(solution)/shard_map/ppermute | solution.py:162
  26.0 2.1 %collective-permute-done.10 = f32[64,256]{1,0:T(8,128)S(1)} collective-permute-done((f32[64,256]{1,0:T(8,128)}, f32[64,256]{1,0:T(8,128)S(1)}, u32[]{:S(2)}, u32[]{:S(2)}) %collective-permute-start.10) | collective-permute-done | bytes 65568 | tf_op jit(solution)/shard_map/ppermute | solution.py:162
  28.8 0.7 maximum_maximum_fusion
  29.5 1.9 %collective-permute-start.1 = (f32[1024,128]{1,0:T(8,128)S(1)}, f32[1024,128]{1,0:T(8,128)S(1)}, u32[]{:S(2)}, u32[]{:S(2)}) collective-permute-start(f32[1024,128]{1,0:T(8,128)S(1)} %copy-done), channel_id=1, source_target_pairs={{0,14},{1,15},{2,0},{3,1},{4,2},{5,3},{6,4},{7,5},{8,6},{9,7},{10,... | collective-permute-start | bytes 1572872 | tf_op jit(solution)/shard_map/ppermute | solution.py:155
  31.5 3.4 %collective-permute-start = (f32[1024,128]{1,0:T(8,128)S(1)}, f32[1024,128]{1,0:T(8,128)S(1)}, u32[]{:S(2)}, u32[]{:S(2)}) collective-permute-start(f32[1024,128]{1,0:T(8,128)S(1)} %copy-done), channel_id=1, source_target_pairs={{0,2},{1,3},{2,4},{3,5},{4,6},{5,7},{6,8},{7,9},{8,10},{9,11},{10,... | collective-permute-start | bytes 1572872 | tf_op jit(solution)/shard_map/ppermute | solution.py:154
  34.8 8.9 %collective-permute-done.1.refs_2_ = f32[1024,128]{1,0:T(8,128)S(1)} collective-permute-done((f32[1024,128]{1,0:T(8,128)S(1)}, f32[1024,128]{1,0:T(8,128)S(1)}, u32[]{:S(2)}, u32[]{:S(2)}) %collective-permute-start.1) | collective-permute-done | bytes 524320 | tf_op jit(solution)/shard_map/ppermute | solution.py:155
  43.7 4.3 %collective-permute-start.3 = (f32[1024,128]{1,0:T(8,128)S(1)}, f32[1024,128]{1,0:T(8,128)S(1)}, u32[]{:S(2)}, u32[]{:S(2)}) collective-permute-start(f32[1024,128]{1,0:T(8,128)S(1)} %collective-permute-done.1.refs_2_), channel_id=1, source_target_pairs={{0,14},{1,15},{2,0},{3,1},{4,2},{5,3},{6,4},{7,5},{8,6},{9,7},{10,... | collective-permute-start | bytes 1572872 | tf_op jit(solution)/shard_map/ppermute | solution.py:155
  48.0 1.9 %collective-permute-start.2 = (f32[1024,128]{1,0:T(8,128)S(1)}, f32[1024,128]{1,0:T(8,128)}, u32[]{:S(2)}, u32[]{:S(2)}) collective-permute-start(f32[1024,128]{1,0:T(8,128)S(1)} %collective-permute-done.refs_1_), channel_id=1, source_target_pairs={{0,2},{1,3},{2,4},{3,5},{4,6},{5,7},{6,8},{7,9},{8,10},{9,11},{10,... | collective-permute-start | bytes 1572872 | tf_op jit(solution)/shard_map/ppermute | solution.py:154
  49.9 9.4 %collective-permute-done.3.refs_4_ = f32[1024,128]{1,0:T(8,128)S(1)} collective-permute-done((f32[1024,128]{1,0:T(8,128)S(1)}, f32[1024,128]{1,0:T(8,128)S(1)}, u32[]{:S(2)}, u32[]{:S(2)}) %collective-permute-start.3) | collective-permute-done | bytes 524320 | tf_op jit(solution)/shard_map/ppermute | solution.py:155
  59.3 4.4 %collective-permute-start.5 = (f32[1024,128]{1,0:T(8,128)S(1)}, f32[1024,128]{1,0:T(8,128)S(1)}, u32[]{:S(2)}, u32[]{:S(2)}) collective-permute-start(f32[1024,128]{1,0:T(8,128)S(1)} %collective-permute-done.3.refs_4_), channel_id=1, source_target_pairs={{0,14},{1,15},{2,0},{3,1},{4,2},{5,3},{6,4},{7,5},{8,6},{9,7},{10,... | collective-permute-start | bytes 1572872 | tf_op jit(solution)/shard_map/ppermute | solution.py:155
  63.7 1.9 %collective-permute-start.4 = (f32[1024,128]{1,0:T(8,128)}, f32[1024,128]{1,0:T(8,128)S(1)}, u32[]{:S(2)}, u32[]{:S(2)}) collective-permute-start(f32[1024,128]{1,0:T(8,128)} %collective-permute-done.2.refs_3_), channel_id=1, source_target_pairs={{0,2},{1,3},{2,4},{3,5},{4,6},{5,7},{6,8},{7,9},{8,10},{9,11},{10,... | collective-permute-start | bytes 1572872 | tf_op jit(solution)/shard_map/ppermute | solution.py:154
  66.6 10.4 %all-to-all-start = ((f32[32,2,128]{2,1,0:T(2,128)}), f32[32,2,128]{2,1,0:T(2,128)}, u32[]{:S(2)}, u32[]{:S(2)}) async-start(f32[32,2,128]{2,1,0:T(2,128)} %broadcast_in_dim.8), calls=%async_computation | async-start | bytes 65536 | tf_op jit(solution)/shard_map/all_to_all | solution.py:146
  77.1 0.7 slice.9
  77.8 4.6 %collective-permute-start.7 = (f32[512,128]{1,0:T(8,128)}, f32[512,128]{1,0:T(8,128)S(1)}, u32[]{:S(2)}, u32[]{:S(2)}) collective-permute-start(f32[512,128]{1,0:T(8,128)} %slice.9), channel_id=1, source_target_pairs={{0,14},{1,15},{2,0},{3,1},{4,2},{5,3},{6,4},{7,5},{8,6},{9,7},{10,... | collective-permute-start | bytes 786440 | tf_op jit(solution)/shard_map/ppermute | solution.py:155
  83.1 1.9 %collective-permute-start.6 = (f32[512,128]{1,0:T(8,128)}, f32[512,128]{1,0:T(8,128)}, u32[]{:S(2)}, u32[]{:S(2)}) collective-permute-start(f32[512,128]{1,0:T(8,128)} %slice.8), channel_id=1, source_target_pairs={{0,2},{1,3},{2,4},{3,5},{4,6},{5,7},{6,8},{7,9},{8,10},{9,11},{10,... | collective-permute-start | bytes 786440 | tf_op jit(solution)/shard_map/ppermute | solution.py:154
  85.0 1.1 fusion.2
  86.8 4.3 %all-to-all-start.2 = ((f32[8,2,128]{2,1,0:T(2,128)}), f32[8,2,128]{2,1,0:T(2,128)S(1)}, u32[]{:S(2)}, u32[]{:S(2)}) async-start(f32[8,2,128]{2,1,0:T(2,128)} %broadcast_in_dim.10), calls=%async_computation.2 | async-start | bytes 16384 | tf_op jit(solution)/shard_map/all_to_all | solution.py:146
  91.1 0.8 reduce_sum.18
  91.9 5.8 %all-to-all-done.2 = f32[8,2,128]{2,1,0:T(2,128)S(1)} async-done(((f32[8,2,128]{2,1,0:T(2,128)}), f32[8,2,128]{2,1,0:T(2,128)S(1)}, u32[]{:S(2)}, u32[]{:S(2)}) %all-to-all-start.2) | async-done | bytes 8224 | tf_op jit(solution)/shard_map/all_to_all | solution.py:146
  98.3 3.3 %all-to-all-start.1 = ((f32[8,2,128]{2,1,0:T(2,128)}), f32[8,2,128]{2,1,0:T(2,128)S(1)}, u32[]{:S(2)}, u32[]{:S(2)}) async-start(f32[8,2,128]{2,1,0:T(2,128)} %broadcast_in_dim.9), calls=%async_computation.1 | async-start | bytes 16384 | tf_op jit(solution)/shard_map/all_to_all | solution.py:146
  101.7 6.5 %all-to-all-done.1.refs_10_ = f32[8,2,128]{2,1,0:T(2,128)S(1)} async-done(((f32[8,2,128]{2,1,0:T(2,128)}), f32[8,2,128]{2,1,0:T(2,128)S(1)}, u32[]{:S(2)}, u32[]{:S(2)}) %all-to-all-start.1) | async-done | bytes 8224 | tf_op jit(solution)/shard_map/all_to_all | solution.py:146
  108.8 6.8 %all-to-all-start.3 = ((f32[8,2,128]{2,1,0:T(2,128)}), f32[8,2,128]{2,1,0:T(2,128)S(1)}, u32[]{:S(2)}, u32[]{:S(2)}) async-start(f32[8,2,128]{2,1,0:T(2,128)} %broadcast_in_dim.11), calls=%async_computation.3 | async-start | bytes 16384 | tf_op jit(solution)/shard_map/all_to_all | solution.py:146
  115.6 6.5 %all-to-all-done.3.refs_11_ = f32[8,2,128]{2,1,0:T(2,128)S(1)} async-done(((f32[8,2,128]{2,1,0:T(2,128)}), f32[8,2,128]{2,1,0:T(2,128)S(1)}, u32[]{:S(2)}, u32[]{:S(2)}) %all-to-all-start.3) | async-done | bytes 8224 | tf_op jit(solution)/shard_map/all_to_all | solution.py:146
  122.2 9.9 %shard_map.49 = (f32[1056,256]{1,0:T(8,128)S(1)}, f32[1056,256]{1,0:T(8,128)}) custom-call(s32[2]{0:T(128)S(1)} %pad_add_fusion.place, f32[1024,128]{1,0:T(8,128)S(1)} %copy-done, f32[1024,128]{1,0:T(8,128)S(1)} %collective-permute-done.refs_1_, f32[1024,128]{1,0:T(8,128)S(1)} %collective-permute-done.1.refs_2_, f32[1024,128]{1,0:T(8,128)} %collective-permute-done.2.refs_3_, ...), custom_call_target="tpu_custom_call" | custom-call | tf_op jit(solution)/shard_map/pallas_call | solution.py:92
  132.1 1.0 copy-done.1
  133.1 9.0 %collective-permute-start.12 = (f32[1056,256]{1,0:T(8,128)}, f32[1056,256]{1,0:T(8,128)S(1)}, u32[]{:S(2)}, u32[]{:S(2)}) collective-permute-start(f32[1056,256]{1,0:T(8,128)} %get-tuple-element.6), channel_id=1, source_target_pairs={{0,1},{1,0},{2,3},{3,2},{4,5},{5,4},{6,7},{7,6},{8,9},{9,8},{10,11... | collective-permute-start | bytes 3244040 | tf_op jit(solution)/shard_map/ppermute | solution.py:181
  142.2 2.5 %collective-permute-done.12.other = f32[1056,256]{1,0:T(8,128)S(1)} collective-permute-done((f32[1056,256]{1,0:T(8,128)}, f32[1056,256]{1,0:T(8,128)S(1)}, u32[]{:S(2)}, u32[]{:S(2)}) %collective-permute-start.12) | collective-permute-done | bytes 1081376 | tf_op jit(solution)/shard_map/ppermute | solution.py:181
  144.7 1.0 copy-done.2
  145.7 3.6 %shard_map.50 = (f32[1024,256]{1,0:T(8,128)}, f32[2,256]{1,0:T(2,128)}, f32[2,1024]{1,0:T(2,128)}) custom-call(f32[1056,256]{1,0:T(8,128)} %copy-done.1, f32[1056,256]{1,0:T(8,128)} %copy-done.2), custom_call_target="tpu_custom_call" | custom-call | tf_op jit(solution)/shard_map/pallas_call | solution.py:127
  (33 shorter events, 4.5 us)
Async XLA Ops:
  7.2 22.4 %copy-start = (f32[1024,128]{1,0:T(8,128)S(1)}, f32[1024,128]{1,0:T(8,128)}, u32[]{:S(2)}) copy-start(f32[1024,128]{1,0:T(8,128)} %refs_0_.1) | copy-start | bytes 1572868
  7.2 115.0 %all-gather.2.cloned.1.call-start = ((), (), s32[]{:S(2)}) async-start(), calls=%async_computation.4 | async-start | bytes 2359296 | tf_op jit(solution)/shard_map/all_gather | solution.py:167
  7.2 18.8 %collective-permute-start.9 = (f32[64,256]{1,0:T(8,128)}, f32[64,256]{1,0:T(8,128)S(1)}, u32[]{:S(2)}, u32[]{:S(2)}) collective-permute-start(f32[64,256]{1,0:T(8,128)} %param.3), channel_id=1, source_target_pairs={{0,16},{1,32},{2,18},{3,34},{4,20},{5,36},{6,22},{7,38},{8,24},{9,... | collective-permute-start | bytes 196616 | tf_op jit(solution)/shard_map/ppermute | solution.py:162
  13.4 12.6 %collective-permute-start.8 = (f32[64,256]{1,0:T(8,128)}, f32[64,256]{1,0:T(8,128)S(1)}, u32[]{:S(2)}, u32[]{:S(2)}) collective-permute-start(f32[64,256]{1,0:T(8,128)} %param.3), channel_id=1, source_target_pairs={{0,0},{1,16},{2,2},{3,18},{4,4},{5,20},{6,6},{7,22},{8,8},{9,24},{... | collective-permute-start | bytes 196616 | tf_op jit(solution)/shard_map/ppermute | solution.py:162
  15.9 10.1 %collective-permute-start.11 = (f32[64,256]{1,0:T(8,128)}, f32[64,256]{1,0:T(8,128)S(1)}, u32[]{:S(2)}, u32[]{:S(2)}) collective-permute-start(f32[64,256]{1,0:T(8,128)} %param.3), channel_id=1, source_target_pairs={{0,48},{1,0},{2,50},{3,2},{4,52},{5,4},{6,54},{7,6},{8,56},{9,8},{... | collective-permute-start | bytes 196616 | tf_op jit(solution)/shard_map/ppermute | solution.py:162
  19.6 8.5 %collective-permute-start.10 = (f32[64,256]{1,0:T(8,128)}, f32[64,256]{1,0:T(8,128)S(1)}, u32[]{:S(2)}, u32[]{:S(2)}) collective-permute-start(f32[64,256]{1,0:T(8,128)} %param.3), channel_id=1, source_target_pairs={{0,32},{1,48},{2,34},{3,50},{4,36},{5,52},{6,38},{7,54},{8,40},{9,... | collective-permute-start | bytes 196616 | tf_op jit(solution)/shard_map/ppermute | solution.py:162
  28.1 0.6 copy-start.3
  28.1 0.6 copy-start.4
  29.5 14.2 %collective-permute-start.1 = (f32[1024,128]{1,0:T(8,128)S(1)}, f32[1024,128]{1,0:T(8,128)S(1)}, u32[]{:S(2)}, u32[]{:S(2)}) collective-permute-start(f32[1024,128]{1,0:T(8,128)S(1)} %copy-done), channel_id=1, source_target_pairs={{0,14},{1,15},{2,0},{3,1},{4,2},{5,3},{6,4},{7,5},{8,6},{9,7},{10,... | collective-permute-start | bytes 1572872 | tf_op jit(solution)/shard_map/ppermute | solution.py:155
  31.5 16.5 %collective-permute-start = (f32[1024,128]{1,0:T(8,128)S(1)}, f32[1024,128]{1,0:T(8,128)S(1)}, u32[]{:S(2)}, u32[]{:S(2)}) collective-permute-start(f32[1024,128]{1,0:T(8,128)S(1)} %copy-done), channel_id=1, source_target_pairs={{0,2},{1,3},{2,4},{3,5},{4,6},{5,7},{6,8},{7,9},{8,10},{9,11},{10,... | collective-permute-start | bytes 1572872 | tf_op jit(solution)/shard_map/ppermute | solution.py:154
  43.7 15.6 %collective-permute-start.3 = (f32[1024,128]{1,0:T(8,128)S(1)}, f32[1024,128]{1,0:T(8,128)S(1)}, u32[]{:S(2)}, u32[]{:S(2)}) collective-permute-start(f32[1024,128]{1,0:T(8,128)S(1)} %collective-permute-done.1.refs_2_), channel_id=1, source_target_pairs={{0,14},{1,15},{2,0},{3,1},{4,2},{5,3},{6,4},{7,5},{8,6},{9,7},{10,... | collective-permute-start | bytes 1572872 | tf_op jit(solution)/shard_map/ppermute | solution.py:155
  48.0 15.7 %collective-permute-start.2 = (f32[1024,128]{1,0:T(8,128)S(1)}, f32[1024,128]{1,0:T(8,128)}, u32[]{:S(2)}, u32[]{:S(2)}) collective-permute-start(f32[1024,128]{1,0:T(8,128)S(1)} %collective-permute-done.refs_1_), channel_id=1, source_target_pairs={{0,2},{1,3},{2,4},{3,5},{4,6},{5,7},{6,8},{7,9},{8,10},{9,11},{10,... | collective-permute-start | bytes 1572872 | tf_op jit(solution)/shard_map/ppermute | solution.py:154
  59.3 17.7 %collective-permute-start.5 = (f32[1024,128]{1,0:T(8,128)S(1)}, f32[1024,128]{1,0:T(8,128)S(1)}, u32[]{:S(2)}, u32[]{:S(2)}) collective-permute-start(f32[1024,128]{1,0:T(8,128)S(1)} %collective-permute-done.3.refs_4_), channel_id=1, source_target_pairs={{0,14},{1,15},{2,0},{3,1},{4,2},{5,3},{6,4},{7,5},{8,6},{9,7},{10,... | collective-permute-start | bytes 1572872 | tf_op jit(solution)/shard_map/ppermute | solution.py:155
  63.7 18.6 %collective-permute-start.4 = (f32[1024,128]{1,0:T(8,128)}, f32[1024,128]{1,0:T(8,128)S(1)}, u32[]{:S(2)}, u32[]{:S(2)}) collective-permute-start(f32[1024,128]{1,0:T(8,128)} %collective-permute-done.2.refs_3_), channel_id=1, source_target_pairs={{0,2},{1,3},{2,4},{3,5},{4,6},{5,7},{6,8},{7,9},{8,10},{9,11},{10,... | collective-permute-start | bytes 1572872 | tf_op jit(solution)/shard_map/ppermute | solution.py:154
  66.6 19.5 %all-to-all-start = ((f32[32,2,128]{2,1,0:T(2,128)}), f32[32,2,128]{2,1,0:T(2,128)}, u32[]{:S(2)}, u32[]{:S(2)}) async-start(f32[32,2,128]{2,1,0:T(2,128)} %broadcast_in_dim.8), calls=%async_computation | async-start | bytes 65536 | tf_op jit(solution)/shard_map/all_to_all | solution.py:146
  77.8 44.4 %collective-permute-start.7 = (f32[512,128]{1,0:T(8,128)}, f32[512,128]{1,0:T(8,128)S(1)}, u32[]{:S(2)}, u32[]{:S(2)}) collective-permute-start(f32[512,128]{1,0:T(8,128)} %slice.9), channel_id=1, source_target_pairs={{0,14},{1,15},{2,0},{3,1},{4,2},{5,3},{6,4},{7,5},{8,6},{9,7},{10,... | collective-permute-start | bytes 786440 | tf_op jit(solution)/shard_map/ppermute | solution.py:155
  83.1 39.1 %collective-permute-start.6 = (f32[512,128]{1,0:T(8,128)}, f32[512,128]{1,0:T(8,128)}, u32[]{:S(2)}, u32[]{:S(2)}) collective-permute-start(f32[512,128]{1,0:T(8,128)} %slice.8), channel_id=1, source_target_pairs={{0,2},{1,3},{2,4},{3,5},{4,6},{5,7},{6,8},{7,9},{8,10},{9,11},{10,... | collective-permute-start | bytes 786440 | tf_op jit(solution)/shard_map/ppermute | solution.py:154
  86.8 10.9 %all-to-all-start.2 = ((f32[8,2,128]{2,1,0:T(2,128)}), f32[8,2,128]{2,1,0:T(2,128)S(1)}, u32[]{:S(2)}, u32[]{:S(2)}) async-start(f32[8,2,128]{2,1,0:T(2,128)} %broadcast_in_dim.10), calls=%async_computation.2 | async-start | bytes 16384 | tf_op jit(solution)/shard_map/all_to_all | solution.py:146
  98.3 9.9 %all-to-all-start.1 = ((f32[8,2,128]{2,1,0:T(2,128)}), f32[8,2,128]{2,1,0:T(2,128)S(1)}, u32[]{:S(2)}, u32[]{:S(2)}) async-start(f32[8,2,128]{2,1,0:T(2,128)} %broadcast_in_dim.9), calls=%async_computation.1 | async-start | bytes 16384 | tf_op jit(solution)/shard_map/all_to_all | solution.py:146
  108.8 13.4 %all-to-all-start.3 = ((f32[8,2,128]{2,1,0:T(2,128)}), f32[8,2,128]{2,1,0:T(2,128)S(1)}, u32[]{:S(2)}, u32[]{:S(2)}) async-start(f32[8,2,128]{2,1,0:T(2,128)} %broadcast_in_dim.11), calls=%async_computation.3 | async-start | bytes 16384 | tf_op jit(solution)/shard_map/all_to_all | solution.py:146
  132.1 1.0 copy-start.1
  133.1 11.6 %collective-permute-start.12 = (f32[1056,256]{1,0:T(8,128)}, f32[1056,256]{1,0:T(8,128)S(1)}, u32[]{:S(2)}, u32[]{:S(2)}) collective-permute-start(f32[1056,256]{1,0:T(8,128)} %get-tuple-element.6), channel_id=1, source_target_pairs={{0,1},{1,0},{2,3},{3,2},{4,5},{5,4},{6,7},{7,6},{8,9},{9,8},{10,11... | collective-permute-start | bytes 3244040 | tf_op jit(solution)/shard_map/ppermute | solution.py:181
  144.7 1.0 copy-start.2
Sparse Core Ops, SparseCore 0:
  29.7 42.2 all-gather.1

commit v2 on v0

v2 whole, which is shorter than its diff:
```python
import jax
import jax.numpy as jnp
from jax import lax
from jax.experimental import pallas as pl
from jax.experimental.pallas import tpu as pltpu
from jax.sharding import PartitionSpec as P

NX, NY, NZ = 4, 8, 8
STEP = 256
VMEM = 48 * 1024 * 1024

Z_GROUPS = [[NX * z + x for z in range(NZ)] for x in range(NX)]


def along_x(shift):
    return [(NX * z + x, NX * z + (x + shift) % NX) for z in range(NZ) for x in range(NX)]


def check_weights(total, start, count):
    index = (start + jnp.arange(count, dtype=jnp.int32)).astype(jnp.float32)
    flat = jnp.full((count,), 1.0, jnp.float32) / jnp.sqrt(jnp.float32(total))
    ramp = (index + 0.5) / total * jnp.sqrt(jnp.float32(3.0) / total)
    return jnp.stack([flat, ramp], 0)


def halves(value):
    high = value.astype(jnp.bfloat16)
    return high, (value - high.astype(jnp.float32)).astype(jnp.bfloat16)


def dot(left, right, contract=((1,), (0,))):
    return lax.dot_general(left, right, (contract, ((), ())), preferred_element_type=jnp.float32)


def three(left, right, contract=((1,), (0,))):
    (lh, ll), (rh, rl) = left, right
    return dot(lh, rh, contract) + (dot(ll, rh, contract) + dot(lh, rl, contract))


def product_kernel(place, t, e0, e1, e2, e3, u, v, main, rows, cols, eh, el):
    @pl.when(pl.program_id(0) == 0)
    def _():
        for d, part in enumerate((e0, e1, e2, e3)):
            x = lax.rem(place[0] + d, NX)
            for z in range(NZ):
                at = pl.ds(pl.multiple_of((NX * z + x) * 64, 64), 64)
                eh[at, :], el[at, :] = halves(part[z, :64, :])
        rows[...] = three(halves(u[...]), (eh[...], el[...]))

    th, tl = halves(jnp.concatenate([t[k] for k in range(t.shape[0])], 1))
    main[...] = three((th, tl), (eh[...], el[...]))
    cols[...] = three(halves(v[...]), (th, tl), ((1,), (1,)))


def product(place, t, parts, u, v):
    blocks, m, wide = t.shape
    whole = lambda a: pl.BlockSpec(a.shape, lambda i, s: (0,) * a.ndim)
    depth = blocks * wide
    return pl.pallas_call(
        product_kernel,
        out_shape=(
            jax.ShapeDtypeStruct((m, 256), jnp.float32),
            jax.ShapeDtypeStruct((2, 256), jnp.float32),
            jax.ShapeDtypeStruct((2, m), jnp.float32),
        ),
        grid_spec=pltpu.PrefetchScalarGridSpec(
            num_scalar_prefetch=1,
            grid=(m // STEP,),
            in_specs=[pl.BlockSpec((blocks, STEP, wide), lambda i, s: (0, i, 0))]
            + [whole(a) for a in (*parts, u, v)],
            out_specs=[
                pl.BlockSpec((STEP, 256), lambda i, s: (i, 0)),
                pl.BlockSpec((2, 256), lambda i, s: (0, 0)),
                pl.BlockSpec((2, STEP), lambda i, s: (0, i)),
            ],
            scratch_shapes=[pltpu.VMEM((depth, 256), jnp.bfloat16)] * 2,
        ),
        compiler_params=pltpu.CompilerParams(vmem_limit_bytes=VMEM),
    )(place, t, *parts, u, v)


def to_all(value, axis, count, groups=None):
    copies = jnp.broadcast_to(value[None], (count,) + value.shape)
    return lax.all_to_all(copies, axis, split_axis=0, concat_axis=0, axis_index_groups=groups)


def on_device(transfer, emissions):
    highest = lax.Precision.HIGHEST
    row, col = lax.axis_index("row"), lax.axis_index("col")
    x = lax.rem(row, NX)
    m_local, s_local = transfer.shape[0], emissions.shape[1]

    whole = lax.all_gather(transfer, "col", axis=0)

    receptor = check_weights(m_local * lax.axis_size("row"), row * m_local, m_local)
    u = jnp.dot(receptor, transfer, precision=highest, preferred_element_type=jnp.float32)
    sent = jnp.concatenate([emissions, jnp.pad(u, ((0, 6), (0, s_local - u.shape[1])))], 0)
    near = to_all(sent, "row", NZ, Z_GROUPS)
    parts = [near] + [lax.ppermute(near, "row", along_x(-d)) for d in (1, 2, 3)]
    u = sum(part[:, 64:66, :128].sum(0) for part in parts)
    u = to_all(u, "col", 2 * NY).transpose(1, 0, 2).reshape(2, -1)

    scenario = check_weights(s_local * lax.axis_size("col"), col * s_local, s_local)
    v = jnp.einsum("js,ks->jk", scenario, emissions, precision=highest, preferred_element_type=jnp.float32)
    v = to_all(v, "col", 2 * NY).sum(0)
    v = to_all(v, "row", NX * NZ).transpose(1, 0, 2).reshape(2, -1)

    place = jnp.stack([x]).astype(jnp.int32)
    return tuple(product(place, whole, parts, u, v))


def solution(mesh):
    placed = (P("row", "col"), P("row", "col"))
    return jax.shard_map(
        on_device,
        mesh=mesh,
        in_specs=placed,
        out_specs=(P("row", "col"), P(None, "col"), P(None, "row")),
        check_vma=False,
    )
```

time: 283 us -> 112 us (0.40)
  the two profiles are of different devices: /device:TPU:32 before, /device:TPU:1 now
where the time goes in v2:
time: 112 us
  blocking collectives  45.3 us (40%)
  starting transfers between devices  19.4 us (17%)
  waiting for transfers between devices  15.6 us (14%)
  between operations  14.2 us (13%)
  Pallas kernels  10.3 us (9%)
  matrix products  2.38 us (2%)
  other arithmetic  2.33 us (2%)
  local copies, waits for them, and re-layouts  2.25 us (2%)
    all_to_all x2, blocking collectives, to_all(): lax.all_to_all(copies, axis, split_axis=0, concat_axis=0, axis_index_grou...  45.3 us
    all_to_all x2, waiting for transfers between devices, to_all(): lax.all_to_all(copies, axis, split_axis=0, concat_axis=0, axis_index_grou...  14.9 us
    ppermute x3, starting transfers between devices, on_device(): parts = [near] + [lax.ppermute(near, 'row', along_x(-d)) for d in (1, 2, 3)]  10.5 us
    pallas_call x1, Pallas kernels, product(): pl.pallas_call(product_kernel, out_shape=(jax.ShapeDtypeStruct((m, 256),...  10.3 us
    all_to_all x2, starting transfers between devices, to_all(): lax.all_to_all(copies, axis, split_axis=0, concat_axis=0, axis_index_grou...  8.86 us
  transfers between devices with their start and end apart: 6, of which 2 were waited for; matrix products, arithmetic and copies ran while one was open for 6% of the time, Pallas kernels for 0%

profile of v2, /device:TPU:1, one launch (start us, length us, event | category | flops | bytes accessed | tf_op | source)
XLA Modules:
  0.0 111.9 jit_solution(10290663970697081955)
XLA Ops:
  7.2 0.0 all-gather.3.cloned.1.call-start
  7.2 0.7 all-gather.3.cloned.1.call-update
  7.9 1.4 %fusion = f32[2,128]{1,0:T(2,128)S(1)} fusion(f32[1024,128]{1,0:T(8,128)} %param.2, f32[1,1024]{1,0:T(1,128)S(1)} %add_multiply_fusion), kind=kOutput, calls=%fused_computation.6 | convolution fusion | flops 3145728 | bytes 529408 | tf_op jit(solution)/shard_map/dot_general | solution.py:96
  9.3 0.9 select_maximum_fusion
  10.2 28.1 %all_to_all.20.e0 = f32[8,72,256]{2,1,0:T(8,128)S(1)} all-to-all(f32[8,72,256]{2,1,0:T(8,128)S(1)} %broadcast_in_dim.8), channel_id=1, replica_groups={{0,64,128,192,256,320,384,448},{16,80,144,208,272,336,400,464},{32,96,1..., dimensions={0} | all-to-all | bytes 1179648 | tf_op jit(solution)/shard_map/all_to_all | solution.py:84
  38.3 3.1 %collective-permute-start.2 = (f32[8,72,256]{2,1,0:T(8,128)S(1)}, f32[8,72,256]{2,1,0:T(8,128)S(1)}, u32[]{:S(2)}, u32[]{:S(2)}) collective-permute-start(f32[8,72,256]{2,1,0:T(8,128)S(1)} %all_to_all.20.e0), channel_id=1, source_target_pairs={{0,16},{16,32},{32,48},{48,0},{64,80},{80,96},{96,112},{112,64},{1... | collective-permute-start | bytes 1769480 | tf_op jit(solution)/shard_map/ppermute | solution.py:99
  41.4 4.4 %collective-permute-start.1 = (f32[8,72,256]{2,1,0:T(8,128)S(1)}, f32[8,72,256]{2,1,0:T(8,128)S(1)}, u32[]{:S(2)}, u32[]{:S(2)}) collective-permute-start(f32[8,72,256]{2,1,0:T(8,128)S(1)} %all_to_all.20.e0), channel_id=1, source_target_pairs={{0,32},{16,48},{32,0},{48,16},{64,96},{80,112},{96,64},{112,80},{1... | collective-permute-start | bytes 1769480 | tf_op jit(solution)/shard_map/ppermute | solution.py:99
  45.8 3.1 %collective-permute-start = (f32[8,72,256]{2,1,0:T(8,128)S(1)}, f32[8,72,256]{2,1,0:T(8,128)S(1)}, u32[]{:S(2)}, u32[]{:S(2)}) collective-permute-start(f32[8,72,256]{2,1,0:T(8,128)S(1)} %all_to_all.20.e0), channel_id=1, source_target_pairs={{0,48},{16,0},{32,16},{48,32},{64,112},{80,64},{96,80},{112,96},{1... | collective-permute-start | bytes 1769480 | tf_op jit(solution)/shard_map/ppermute | solution.py:99
  48.9 1.0 fusion.2
  49.9 0.1 reshape.61
  50.0 17.2 %all_to_all.21 = f32[16,1,128]{2,1,0:T(1,128)S(1)} all-to-all(f32[16,1,128]{2,1,0:T(1,128)S(1)} %reshape.61), channel_id=1, replica_groups=mesh['row'=32,'col'=16] {'col'}, dimensions={0} | all-to-all | bytes 16384 | tf_op jit(solution)/shard_map/all_to_all | solution.py:84
  67.3 0.5 broadcast.60
  67.8 0.7 reduce
  68.4 0.1 reshape.62
  68.6 0.7 reshape.63
  69.3 3.8 %all-to-all-start.3 = ((f32[32,1,128]{2,1,0:T(1,128)}), f32[32,1,128]{2,1,0:T(1,128)S(1)}, u32[]{:S(2)}, u32[]{:S(2)}) async-start(f32[32,1,128]{2,1,0:T(1,128)} %reshape.63), calls=%async_computation.3 | async-start | bytes 32768 | tf_op jit(solution)/shard_map/all_to_all | solution.py:84
  73.1 0.0 collective-permute-done.2.e3
  73.1 0.0 collective-permute-done.1.e2
  73.2 0.0 collective-permute-done.e1
  73.2 8.4 %all-to-all-done.3 = f32[32,1,128]{2,1,0:T(1,128)S(1)} async-done(((f32[32,1,128]{2,1,0:T(1,128)}), f32[32,1,128]{2,1,0:T(1,128)S(1)}, u32[]{:S(2)}, u32[]{:S(2)}) %all-to-all-start.3) | async-done | bytes 16416 | tf_op jit(solution)/shard_map/all_to_all | solution.py:84
  81.6 0.6 broadcast_in_dim.9
  82.2 5.0 %all-to-all-start.1 = ((f32[16,2,128]{2,1,0:T(2,128)}), f32[16,2,128]{2,1,0:T(2,128)S(1)}, u32[]{:S(2)}, u32[]{:S(2)}) async-start(f32[16,2,128]{2,1,0:T(2,128)} %broadcast_in_dim.9), calls=%async_computation.1 | async-start | bytes 32768 | tf_op jit(solution)/shard_map/all_to_all | solution.py:84
  87.3 0.7 reduce.1
  87.9 0.1 reshape.64
  88.0 0.1 reshape.59.v
  88.1 6.5 %all-to-all-done.1 = f32[16,2,128]{2,1,0:T(2,128)S(1)} async-done(((f32[16,2,128]{2,1,0:T(2,128)}), f32[16,2,128]{2,1,0:T(2,128)S(1)}, u32[]{:S(2)}, u32[]{:S(2)}) %all-to-all-start.1) | async-done | bytes 16416 | tf_op jit(solution)/shard_map/all_to_all | solution.py:84
  94.7 0.0 all-gather.3.cloned.1.call-done
  94.7 10.3 %shard_map.49 = (f32[1024,256]{1,0:T(8,128)}, f32[2,256]{1,0:T(2,128)}, f32[2,1024]{1,0:T(2,128)}) custom-call(s32[1]{0:T(128)} %bitcast.place, f32[16,1024,128]{2,1,0:T(8,128)} %bitcast.9, f32[8,72,256]{2,1,0:T(8,128)S(1)} %all_to_all.20.e0, f32[8,72,256]{2,1,0:T(8,128)S(1)} %collective-permute-done.e1, f32[8,72,256]{2,1,0:T(8,128)S(1)} %collective-permute-done.1.e2, ...), custom_call_target="tpu_custom_call" | custom-call | tf_op jit(solution)/shard_map/pallas_call | solution.py:59
  (12 shorter events, 0.2 us)
Async XLA Ops:
  7.2 87.5 %all-gather.3.cloned.1.call-start = ((), (), s32[]{:S(2)}) async-start(), calls=%async_computation.4 | async-start | bytes 8912896 | tf_op jit(solution)/shard_map/all_gather | solution.py:93
  38.3 34.8 %collective-permute-start.2 = (f32[8,72,256]{2,1,0:T(8,128)S(1)}, f32[8,72,256]{2,1,0:T(8,128)S(1)}, u32[]{:S(2)}, u32[]{:S(2)}) collective-permute-start(f32[8,72,256]{2,1,0:T(8,128)S(1)} %all_to_all.20.e0), channel_id=1, source_target_pairs={{0,16},{16,32},{32,48},{48,0},{64,80},{80,96},{96,112},{112,64},{1... | collective-permute-start | bytes 1769480 | tf_op jit(solution)/shard_map/ppermute | solution.py:99
  41.4 31.7 %collective-permute-start.1 = (f32[8,72,256]{2,1,0:T(8,128)S(1)}, f32[8,72,256]{2,1,0:T(8,128)S(1)}, u32[]{:S(2)}, u32[]{:S(2)}) collective-permute-start(f32[8,72,256]{2,1,0:T(8,128)S(1)} %all_to_all.20.e0), channel_id=1, source_target_pairs={{0,32},{16,48},{32,0},{48,16},{64,96},{80,112},{96,64},{112,80},{1... | collective-permute-start | bytes 1769480 | tf_op jit(solution)/shard_map/ppermute | solution.py:99
  45.8 27.4 %collective-permute-start = (f32[8,72,256]{2,1,0:T(8,128)S(1)}, f32[8,72,256]{2,1,0:T(8,128)S(1)}, u32[]{:S(2)}, u32[]{:S(2)}) collective-permute-start(f32[8,72,256]{2,1,0:T(8,128)S(1)} %all_to_all.20.e0), channel_id=1, source_target_pairs={{0,48},{16,0},{32,16},{48,32},{64,112},{80,64},{96,80},{112,96},{1... | collective-permute-start | bytes 1769480 | tf_op jit(solution)/shard_map/ppermute | solution.py:99
  69.3 12.4 %all-to-all-start.3 = ((f32[32,1,128]{2,1,0:T(1,128)}), f32[32,1,128]{2,1,0:T(1,128)S(1)}, u32[]{:S(2)}, u32[]{:S(2)}) async-start(f32[32,1,128]{2,1,0:T(1,128)} %reshape.63), calls=%async_computation.3 | async-start | bytes 32768 | tf_op jit(solution)/shard_map/all_to_all | solution.py:84
  82.2 12.4 %all-to-all-start.1 = ((f32[16,2,128]{2,1,0:T(2,128)}), f32[16,2,128]{2,1,0:T(2,128)S(1)}, u32[]{:S(2)}, u32[]{:S(2)}) async-start(f32[16,2,128]{2,1,0:T(2,128)} %broadcast_in_dim.9), calls=%async_computation.1 | async-start | bytes 32768 | tf_op jit(solution)/shard_map/all_to_all | solution.py:84
Sparse Core Ops, SparseCore 0:
  10.1 64.2 all-gather.2

commit v3 on v2

v3 whole, which is shorter than its diff:
```python
import jax
import jax.numpy as jnp
from jax import lax
from jax.experimental import pallas as pl
from jax.experimental.pallas import tpu as pltpu
from jax.sharding import PartitionSpec as P

NX, NY, NZ = 4, 8, 8
STEP = 256
PAD = 16
VMEM = 48 * 1024 * 1024
Z_ORDER = (0, 4, 2, 6, 1, 5, 3, 7)

RING = [(2 * y + c, 2 * ((y + 1 - 2 * c) % NY) + c) for y in range(NY) for c in range(2)]
SIBLING = [(j, j ^ 1) for j in range(2 * NY)]


def from_plane(dz, dx):
    return [
        (NX * ((z + dz) % NZ) + (x + dx) % NX, NX * z + x) for z in range(NZ) for x in range(NX)
    ]


def check_weights(total, start, count):
    index = (start + jnp.arange(count, dtype=jnp.int32)).astype(jnp.float32)
    flat = jnp.full((count,), 1.0, jnp.float32) / jnp.sqrt(jnp.float32(total))
    ramp = (index + 0.5) / total * jnp.sqrt(jnp.float32(3.0) / total)
    return jnp.stack([flat, ramp], 0)


def halves(value):
    high = value.astype(jnp.bfloat16)
    return high, (value - high.astype(jnp.float32)).astype(jnp.bfloat16)


def dot(left, right, contract=((1,), (0,))):
    return lax.dot_general(left, right, (contract, ((), ())), preferred_element_type=jnp.float32)


def product_kernel(place, *refs):
    blocks, (pair, four), parts, (u, v, main, rows, cols, eh, el, us, vs) = (
        refs[:10], refs[10:12], refs[12:16], refs[16:],
    )
    x, y, z, c = place[0], place[1], place[2], place[3]
    way = 2 * c - 1

    @pl.when(pl.program_id(0) == 0)
    def _():
        for d, part in enumerate(parts):
            from_x = lax.rem(x + d, NX)
            other = jnp.where(from_x // 2 == c, 0, 1)
            for i, dz in enumerate(Z_ORDER):
                away = lax.rem(way * (z + dz - y) + 4 * NY, NY)
                at = pl.multiple_of((2 * away + other) * 128 + lax.rem(from_x, 2) * 64, 64)
                eh[pl.ds(at, 64), :], el[pl.ds(at, 64), :] = halves(part[i * 64 : (i + 1) * 64, :])
        us[...] = jnp.zeros_like(us)
        for n in range(2 * NY):
            j = 2 * lax.rem(y + way * (n // 2) + NY, NY) + lax.rem(c + n, 2)
            us[:2, n * 128 : (n + 1) * 128] = u[j]
            vs[:, n * 128 : (n + 1) * 128] = v[j]

    t = [b[...] for b in blocks] + [pair[1], pair[0], four[3], four[2], four[1], four[0]]
    sums = []
    for w in range(2):
        total = t[0] * vs[w : w + 1, :128]
        for n in range(1, 2 * NY):
            total += t[n] * vs[w : w + 1, n * 128 : (n + 1) * 128]
        th, tl = halves(total)
        ones = jnp.ones((PAD, 128), jnp.bfloat16)
        lanes = ((1,), (1,))
        sums.append((dot(ones, th, lanes) + dot(ones, tl, lanes))[:1])
    cols[...] = jnp.concatenate(sums, 0)
    th, tl = halves(jnp.concatenate([jnp.concatenate(t, 1), us[...]], 0))
    out = dot(th, eh[...]) + (dot(tl, eh[...]) + dot(th, el[...]))
    main[...] = out[:STEP]
    rows[...] = out[STEP : STEP + 2]


def product(place, blocks, pair, four, parts, u, v):
    m, wide = blocks[0].shape
    whole = lambda a: pl.BlockSpec(a.shape, lambda i, s: (0,) * a.ndim)
    depth = 2 * NY * wide
    return pl.pallas_call(
        product_kernel,
        out_shape=(
            jax.ShapeDtypeStruct((m, 256), jnp.float32),
            jax.ShapeDtypeStruct((2, 256), jnp.float32),
            jax.ShapeDtypeStruct((2, m), jnp.float32),
        ),
        grid_spec=pltpu.PrefetchScalarGridSpec(
            num_scalar_prefetch=1,
            grid=(m // STEP,),
            in_specs=[pl.BlockSpec((STEP, wide), lambda i, s: (i, 0))] * 10
            + [pl.BlockSpec((a.shape[0], STEP, wide), lambda i, s: (0, i, 0)) for a in (pair, four)]
            + [whole(a) for a in (*parts, u, v)],
            out_specs=[
                pl.BlockSpec((STEP, 256), lambda i, s: (i, 0)),
                pl.BlockSpec((2, 256), lambda i, s: (0, 0)),
                pl.BlockSpec((2, STEP), lambda i, s: (0, i)),
            ],
            scratch_shapes=[pltpu.VMEM((depth, 256), jnp.bfloat16)] * 2
            + [pltpu.VMEM((PAD, depth), jnp.float32), pltpu.VMEM((2, depth), jnp.float32)],
        ),
        compiler_params=pltpu.CompilerParams(vmem_limit_bytes=VMEM),
    )(place, *blocks, pair, four, *parts, u, v)


def to_all(value, axis, count):
    copies = jnp.broadcast_to(value[None], (count,) + value.shape)
    return lax.all_to_all(copies, axis, split_axis=0, concat_axis=0)


def on_device(transfer, emissions):
    highest = lax.Precision.HIGHEST
    row, col = lax.axis_index("row"), lax.axis_index("col")
    x, z, y, c = lax.rem(row, NX), row // NX, col // 2, lax.rem(col, 2)
    m_local, s_local = transfer.shape[0], emissions.shape[1]
    pass_on = lambda a: lax.ppermute(a, "col", RING)
    swap = lambda a: lax.ppermute(a, "col", SIBLING)

    a1 = pass_on(transfer)
    s = swap(transfer)
    b1 = pass_on(s)

    receptor = check_weights(m_local * lax.axis_size("row"), row * m_local, m_local)
    u = jnp.dot(receptor, transfer, precision=highest, preferred_element_type=jnp.float32)
    scenario = check_weights(s_local * lax.axis_size("col"), col * s_local, s_local)
    v = jnp.einsum("js,ks->jk", scenario, emissions, precision=highest, preferred_element_type=jnp.float32)
    both = to_all(jnp.concatenate([u, v, jnp.zeros_like(v)], 1), "col", 2 * NY)
    v = both[:, :, 128:].sum(0)

    near = emissions
    for dz in (4, 2, 1):
        near = jnp.concatenate([near, lax.ppermute(near, "row", from_plane(dz, 0))], 0)
    parts = [near] + [lax.ppermute(near, "row", from_plane(0, d)) for d in (1, 2, 3)]

    both = to_all(jnp.concatenate([both[:, :, :128], v[None]], 0), "row", NX * NZ)
    u = both[:, : 2 * NY].sum(0)
    v = both[:, 2 * NY, :, :64].reshape(2 * NY, 2, 2, 64).transpose(0, 2, 1, 3).reshape(2 * NY, 2, 128)

    a2, b2 = pass_on(a1), pass_on(b1)
    a3, b3 = pass_on(a2), pass_on(b2)
    a4 = pass_on(a3)
    four = swap(jnp.stack([a1, b1, a2, b2]))
    pair = swap(jnp.stack([a3, b3]))
    b4 = swap(a4)
    place = jnp.stack([x, y, z, c]).astype(jnp.int32)
    return tuple(product(place, [transfer, s, a1, b1, a2, b2, a3, b3, a4, b4], pair, four, parts, u, v))


def solution(mesh):
    placed = (P("row", "col"), P("row", "col"))
    return jax.shard_map(
        on_device,
        mesh=mesh,
        in_specs=placed,
        out_specs=(P("row", "col"), P(None, "col"), P(None, "row")),
        check_vma=False,
    )
```

time: 112 us -> 126 us (1.12)
  starting transfers between devices: 19.4 us -> 78.6 us
  blocking collectives: 45.3 us -> 0 us
  between operations: 14.2 us -> 0.98 us
  local copies, waits for them, and re-layouts: 2.25 us -> 8.02 us
  waiting for transfers between devices: 15.6 us -> 19.6 us
  other arithmetic: 2.33 us -> 5.62 us
    ppermute x3 -> x17, starting transfers between devices: 10.5 us -> 65.5 us  [the longest x7 20.7 us: on_device(): pass_on = lambda a: lax.ppermute(a, 'col', RING)]
    all_to_all x2 -> x0, blocking collectives: 45.3 us -> none  [to_all(): lax.all_to_all(copies, axis, split_axis=0, concat_axis=0, axis_index_grou...]
    ppermute x3 -> x17, waiting for transfers between devices: 0.01 us -> 19.6 us  [the longest x3 17.4 us: on_device(): lax.ppermute(near, 'row', from_plane(0, d))]
    all_to_all x2, waiting for transfers between devices: 14.9 us -> 0.01 us  [to_all(): return lax.all_to_all(copies, axis, split_axis=0, concat_axis=0)]
    all_to_all x2, starting transfers between devices: 8.86 us -> 13.1 us  [to_all(): return lax.all_to_all(copies, axis, split_axis=0, concat_axis=0)]
    another operation x0 -> x3, other arithmetic: none -> 3.63 us  [the longest x1 2.51 us: on_device(): four = swap(jnp.stack([a1, b1, a2, b2]))]
    unnamed x4 -> x14, local copies, waits for them, and re-layouts: 0.96 us -> 3.81 us
    concatenate x0 -> x2, local copies, waits for them, and re-layouts: none -> 1.75 us  [the longest x1 1.68 us: on_device(): jnp.concatenate([near, lax.ppermute(near, 'row', from_plane(dz, 0))], 0)]
  transfers between devices with their start and end apart: 6 -> 19, of which waited for: 2 -> 4; matrix products, arithmetic and copies ran while one was open for 6% -> 12% of each run, Pallas kernels for 0% -> 0%
where the time goes in v3:
time: 126 us; the launch traced here: 125 us
  starting transfers between devices  78.6 us (62%)
  waiting for transfers between devices  19.6 us (16%)
  Pallas kernels  9.39 us (7%)
  local copies, waits for them, and re-layouts  8.02 us (6%)
  other arithmetic  5.62 us (4%)
  matrix products  2.38 us (2%)
    ppermute x7, starting transfers between devices, on_device(): pass_on = lambda a: lax.ppermute(a, 'col', RING)  20.7 us
    ppermute x4, starting transfers between devices, on_device(): swap = lambda a: lax.ppermute(a, 'col', SIBLING)  18.9 us
    ppermute x3, waiting for transfers between devices, on_device(): lax.ppermute(near, 'row', from_plane(0, d))  17.4 us
    ppermute x3, starting transfers between devices, on_device(): lax.ppermute(near, 'row', from_plane(dz, 0))  15.7 us
    all_to_all x2, starting transfers between devices, to_all(): return lax.all_to_all(copies, axis, split_axis=0, concat_axis=0)  13.1 us
    ppermute x3, starting transfers between devices, on_device(): lax.ppermute(near, 'row', from_plane(0, d))  10.3 us
    pallas_call x1, Pallas kernels, product(): pl.pallas_call(product_kernel, out_shape=(jax.ShapeDtypeStruct((m, 256),...  9.39 us
    unnamed x14, local copies, waits for them, and re-layouts  3.81 us
  transfers between devices with their start and end apart: 19, of which 4 were waited for; matrix products, arithmetic and copies ran while one was open for 12% of the time, Pallas kernels for 0%

profile of v3, /device:TPU:1, one launch (start us, length us, event | category | flops | bytes accessed | tf_op | source)
XLA Modules:
  0.0 124.6 jit_solution(2622700962916715035)
XLA Ops:
  0.6 8.8 %collective-permute-start = (f32[1024,128]{1,0:T(8,128)}, f32[1024,128]{1,0:T(8,128)S(1)}, u32[]{:S(2)}, u32[]{:S(2)}) collective-permute-start(f32[1024,128]{1,0:T(8,128)} %refs_0_.1), channel_id=1, source_target_pairs={{0,1},{1,0},{2,3},{3,2},{4,5},{5,4},{6,7},{7,6},{8,9},{9,8},{10,11... | collective-permute-start | bytes 1572872 | tf_op jit(solution)/shard_map/ppermute | solution.py:119
  9.4 1.9 %collective-permute-start.1 = (f32[1024,128]{1,0:T(8,128)}, f32[1024,128]{1,0:T(8,128)S(1)}, u32[]{:S(2)}, u32[]{:S(2)}) collective-permute-start(f32[1024,128]{1,0:T(8,128)} %refs_0_.1), channel_id=1, source_target_pairs={{0,2},{1,15},{2,4},{3,1},{4,6},{5,3},{6,8},{7,5},{8,10},{9,7},{10,... | collective-permute-start | bytes 1572872 | tf_op jit(solution)/shard_map/ppermute | solution.py:118
  11.4 1.9 %collective-permute-start.2 = (f32[1024,128]{1,0:T(8,128)S(1)}, f32[1024,128]{1,0:T(8,128)S(1)}, u32[]{:S(2)}, u32[]{:S(2)}) collective-permute-start(f32[1024,128]{1,0:T(8,128)S(1)} %collective-permute-done.refs_1_), channel_id=1, source_target_pairs={{0,2},{1,15},{2,4},{3,1},{4,6},{5,3},{6,8},{7,5},{8,10},{9,7},{10,... | collective-permute-start | bytes 1572872 | tf_op jit(solution)/shard_map/ppermute | solution.py:118
  13.3 9.5 %collective-permute-start.11 = (f32[64,256]{1,0:T(8,128)}, f32[64,256]{1,0:T(8,128)S(1)}, u32[]{:S(2)}, u32[]{:S(2)}) collective-permute-start(f32[64,256]{1,0:T(8,128)} %param.3), channel_id=1, source_target_pairs={{256,0},{272,16},{288,32},{304,48},{320,64},{336,80},{352,96},{368... | collective-permute-start | bytes 196616 | tf_op jit(solution)/shard_map/ppermute | solution.py:134
  22.9 1.4 %fusion = f32[2,128]{1,0:T(2,128)S(1)} fusion(f32[1024,128]{1,0:T(8,128)} %refs_0_.1, f32[1,1024]{1,0:T(1,128)S(1)} %add_multiply_fusion), kind=kOutput, calls=%fused_computation.11 | convolution fusion | flops 3145728 | bytes 529408 | tf_op jit(solution)/shard_map/dot_general | solution.py:126
  24.3 3.0 %collective-permute-start.3 = (f32[1024,128]{1,0:T(8,128)S(1)}, f32[1024,128]{1,0:T(8,128)S(1)}, u32[]{:S(2)}, u32[]{:S(2)}) collective-permute-start(f32[1024,128]{1,0:T(8,128)S(1)} %collective-permute-done.1.refs_2_), channel_id=1, source_target_pairs={{0,2},{1,15},{2,4},{3,1},{4,6},{5,3},{6,8},{7,5},{8,10},{9,7},{10,... | collective-permute-start | bytes 1572872 | tf_op jit(solution)/shard_map/ppermute | solution.py:118
  27.3 3.0 %collective-permute-start.4 = (f32[1024,128]{1,0:T(8,128)S(1)}, f32[1024,128]{1,0:T(8,128)}, u32[]{:S(2)}, u32[]{:S(2)}) collective-permute-start(f32[1024,128]{1,0:T(8,128)S(1)} %collective-permute-done.2.refs_3_), channel_id=1, source_target_pairs={{0,2},{1,15},{2,4},{3,1},{4,6},{5,3},{6,8},{7,5},{8,10},{9,7},{10,... | collective-permute-start | bytes 1572872 | tf_op jit(solution)/shard_map/ppermute | solution.py:118
  30.3 1.0 fusion.2
  32.0 4.7 %all-to-all-start = ((f32[16,2,256]{2,1,0:T(2,128)}), f32[16,2,256]{2,1,0:T(2,128)S(1)}, u32[]{:S(2)}, u32[]{:S(2)}) async-start(f32[16,2,256]{2,1,0:T(2,128)} %broadcast_in_dim.9), calls=%async_computation | async-start | bytes 65536 | tf_op jit(solution)/shard_map/all_to_all | solution.py:110
  36.7 1.5 %constant_dynamic-update-slice_fusion.3 = f32[512,256]{1,0:T(8,128)} fusion(f32[64,256]{1,0:T(8,128)} %param.3), kind=kLoop, calls=%fused_computation.10 | loop fusion | bytes 131072
  38.1 2.2 %collective-permute-done.4.refs_5_ = f32[1024,128]{1,0:T(8,128)} collective-permute-done((f32[1024,128]{1,0:T(8,128)S(1)}, f32[1024,128]{1,0:T(8,128)}, u32[]{:S(2)}, u32[]{:S(2)}) %collective-permute-start.4) | collective-permute-done | bytes 524320 | tf_op jit(solution)/shard_map/ppermute | solution.py:118
  40.3 2.5 %pad_maximum_fusion = f32[4,1024,128]{2,1,0:T(8,128)} fusion(f32[1,1024,128]{2,1,0:T(8,128)} %bitcast.9, f32[1,1024,128]{2,1,0:T(8,128)S(1)} %bitcast.22, f32[1,1024,128]{2,1,0:T(8,128)S(1)} %bitcast.21, f32[1,1024,128]{2,1,0:T(8,128)S(1)} %bitcast.20), kind=kLoop, calls=%fused_computation | loop fusion | flops 1572864 | bytes 4194304 | tf_op jit(solution)/shard_map/stack | solution.py:144
  42.9 3.2 %collective-permute-start.10 = (f32[4,1024,128]{2,1,0:T(8,128)}, f32[4,1024,128]{2,1,0:T(8,128)}, u32[]{:S(2)}, u32[]{:S(2)}) collective-permute-start(f32[4,1024,128]{2,1,0:T(8,128)} %pad_maximum_fusion), channel_id=1, source_target_pairs={{0,1},{1,0},{2,3},{3,2},{4,5},{5,4},{6,7},{7,6},{8,9},{9,8},{10,11... | collective-permute-start | bytes 6291464 | tf_op jit(solution)/shard_map/ppermute | solution.py:119
  46.1 4.0 %collective-permute-start.12 = (f32[128,256]{1,0:T(8,128)S(1)}, f32[128,256]{1,0:T(8,128)S(1)}, u32[]{:S(2)}, u32[]{:S(2)}) collective-permute-start(f32[128,256]{1,0:T(8,128)S(1)} %pad_maximum_fusion.3), channel_id=1, source_target_pairs={{128,0},{144,16},{160,32},{176,48},{192,64},{208,80},{224,96},{240... | collective-permute-start | bytes 393224 | tf_op jit(solution)/shard_map/ppermute | solution.py:134
  50.2 4.8 %collective-permute-start.5 = (f32[1024,128]{1,0:T(8,128)S(1)}, f32[1024,128]{1,0:T(8,128)S(1)}, u32[]{:S(2)}, u32[]{:S(2)}) collective-permute-start(f32[1024,128]{1,0:T(8,128)S(1)} %collective-permute-done.3.refs_4_), channel_id=1, source_target_pairs={{0,2},{1,15},{2,4},{3,1},{4,6},{5,3},{6,8},{7,5},{8,10},{9,7},{10,... | collective-permute-start | bytes 1572872 | tf_op jit(solution)/shard_map/ppermute | solution.py:118
  54.9 3.1 %collective-permute-start.6 = (f32[1024,128]{1,0:T(8,128)}, f32[1024,128]{1,0:T(8,128)S(1)}, u32[]{:S(2)}, u32[]{:S(2)}) collective-permute-start(f32[1024,128]{1,0:T(8,128)} %collective-permute-done.4.refs_5_), channel_id=1, source_target_pairs={{0,2},{1,15},{2,4},{3,1},{4,6},{5,3},{6,8},{7,5},{8,10},{9,7},{10,... | collective-permute-start | bytes 1572872 | tf_op jit(solution)/shard_map/ppermute | solution.py:118
  58.8 2.2 %collective-permute-start.13 = (f32[256,256]{1,0:T(8,128)}, f32[256,256]{1,0:T(8,128)}, u32[]{:S(2)}, u32[]{:S(2)}) collective-permute-start(f32[256,256]{1,0:T(8,128)} %pad_maximum_fusion.2), channel_id=1, source_target_pairs={{64,0},{80,16},{96,32},{112,48},{128,64},{144,80},{160,96},{176,11... | collective-permute-start | bytes 786440 | tf_op jit(solution)/shard_map/ppermute | solution.py:134
  61.9 8.4 %all-to-all-start.1 = ((f32[32,17,2,128]{3,2,1,0:T(2,128)}), f32[32,17,2,128]{3,2,1,0:T(2,128)}, u32[]{:S(2)}, u32[]{:S(2)}) async-start(f32[32,17,2,128]{3,2,1,0:T(2,128)} %broadcast_in_dim.21), calls=%async_computation.1 | async-start | bytes 1114112 | tf_op jit(solution)/shard_map/all_to_all | solution.py:110
  71.7 1.7 %constant_dynamic-update-slice_fusion.refs_12_ = f32[512,256]{1,0:T(8,128)} fusion(f32[512,256]{1,0:T(8,128)} %constant_dynamic-update-slice_fusion.1, f32[256,256]{1,0:T(8,128)} %collective-permute-done.13), kind=kLoop, calls=%fused_computation.7 | loop fusion | bytes 524288 | tf_op jit(solution)/shard_map/concatenate | solution.py:134
  73.3 4.3 %collective-permute-start.14 = (f32[512,256]{1,0:T(8,128)}, f32[512,256]{1,0:T(8,128)S(1)}, u32[]{:S(2)}, u32[]{:S(2)}) collective-permute-start(f32[512,256]{1,0:T(8,128)} %constant_dynamic-update-slice_fusion.refs_12_), channel_id=1, source_target_pairs={{16,0},{32,16},{48,32},{0,48},{80,64},{96,80},{112,96},{64,112},{1... | collective-permute-start | bytes 1572872 | tf_op jit(solution)/shard_map/ppermute | solution.py:135
  77.6 3.0 %collective-permute-start.7 = (f32[1024,128]{1,0:T(8,128)S(1)}, f32[1024,128]{1,0:T(8,128)}, u32[]{:S(2)}, u32[]{:S(2)}) collective-permute-start(f32[1024,128]{1,0:T(8,128)S(1)} %collective-permute-done.5.refs_6_), channel_id=1, source_target_pairs={{0,2},{1,15},{2,4},{3,1},{4,6},{5,3},{6,8},{7,5},{8,10},{9,7},{10,... | collective-permute-start | bytes 1572872 | tf_op jit(solution)/shard_map/ppermute | solution.py:118
  80.7 1.0 pad_maximum_fusion.1
  81.7 3.7 %collective-permute-start.9 = (f32[2,1024,128]{2,1,0:T(8,128)}, f32[2,1024,128]{2,1,0:T(8,128)}, u32[]{:S(2)}, u32[]{:S(2)}) collective-permute-start(f32[2,1024,128]{2,1,0:T(8,128)} %pad_maximum_fusion.1), channel_id=1, source_target_pairs={{0,1},{1,0},{2,3},{3,2},{4,5},{5,4},{6,7},{7,6},{8,9},{9,8},{10,11... | collective-permute-start | bytes 3145736 | tf_op jit(solution)/shard_map/ppermute | solution.py:119
  85.4 2.5 %collective-permute-start.15 = (f32[512,256]{1,0:T(8,128)}, f32[512,256]{1,0:T(8,128)}, u32[]{:S(2)}, u32[]{:S(2)}) collective-permute-start(f32[512,256]{1,0:T(8,128)} %constant_dynamic-update-slice_fusion.refs_12_), channel_id=1, source_target_pairs={{32,0},{48,16},{0,32},{16,48},{96,64},{112,80},{64,96},{80,112},{1... | collective-permute-start | bytes 1572872 | tf_op jit(solution)/shard_map/ppermute | solution.py:135
  87.9 4.7 %collective-permute-done.14.refs_13_ = f32[512,256]{1,0:T(8,128)S(1)} collective-permute-done((f32[512,256]{1,0:T(8,128)}, f32[512,256]{1,0:T(8,128)S(1)}, u32[]{:S(2)}, u32[]{:S(2)}) %collective-permute-start.14) | collective-permute-done | bytes 524320 | tf_op jit(solution)/shard_map/ppermute | solution.py:135
  92.6 3.5 %collective-permute-start.16 = (f32[512,256]{1,0:T(8,128)}, f32[512,256]{1,0:T(8,128)}, u32[]{:S(2)}, u32[]{:S(2)}) collective-permute-start(f32[512,256]{1,0:T(8,128)} %constant_dynamic-update-slice_fusion.refs_12_), channel_id=1, source_target_pairs={{48,0},{0,16},{16,32},{32,48},{112,64},{64,80},{80,96},{96,112},{1... | collective-permute-start | bytes 1572872 | tf_op jit(solution)/shard_map/ppermute | solution.py:135
  96.1 3.2 %collective-permute-start.8 = (f32[1024,128]{1,0:T(8,128)}, f32[1024,128]{1,0:T(8,128)}, u32[]{:S(2)}, u32[]{:S(2)}) collective-permute-start(f32[1024,128]{1,0:T(8,128)} %collective-permute-done.7.refs_8_), channel_id=1, source_target_pairs={{0,1},{1,0},{2,3},{3,2},{4,5},{5,4},{6,7},{7,6},{8,9},{9,8},{10,11... | collective-permute-start | bytes 1572872 | tf_op jit(solution)/shard_map/ppermute | solution.py:119
  100.3 1.2 slice_reduce_fusion.refs_16_
  101.5 1.2 collective-permute-done.15.refs_14_
  102.7 11.5 %collective-permute-done.16.refs_15_ = f32[512,256]{1,0:T(8,128)} collective-permute-done((f32[512,256]{1,0:T(8,128)}, f32[512,256]{1,0:T(8,128)}, u32[]{:S(2)}, u32[]{:S(2)}) %collective-permute-start.16) | collective-permute-done | bytes 524320 | tf_op jit(solution)/shard_map/ppermute | solution.py:135
  114.2 1.0 copy-done.2
  115.2 9.4 %shard_map.49 = (f32[1024,256]{1,0:T(8,128)}, f32[2,256]{1,0:T(2,128)}, f32[2,1024]{1,0:T(2,128)}) custom-call(s32[4]{0:T(128)S(1)} %pad_add_fusion.place, f32[1024,128]{1,0:T(8,128)S(1)} %copy-done, f32[1024,128]{1,0:T(8,128)S(1)} %copy-done.2, f32[1024,128]{1,0:T(8,128)S(1)} %collective-permute-done.1.refs_2_, ...), custom_call_target="tpu_custom_call" | custom-call | tf_op jit(solution)/shard_map/pallas_call | solution.py:83
  (42 shorter events, 4.8 us)
Async XLA Ops:
  0.6 10.7 %collective-permute-start = (f32[1024,128]{1,0:T(8,128)}, f32[1024,128]{1,0:T(8,128)S(1)}, u32[]{:S(2)}, u32[]{:S(2)}) collective-permute-start(f32[1024,128]{1,0:T(8,128)} %refs_0_.1), channel_id=1, source_target_pairs={{0,1},{1,0},{2,3},{3,2},{4,5},{5,4},{6,7},{7,6},{8,9},{9,8},{10,11... | collective-permute-start | bytes 1572872 | tf_op jit(solution)/shard_map/ppermute | solution.py:119
  9.4 14.9 %collective-permute-start.1 = (f32[1024,128]{1,0:T(8,128)}, f32[1024,128]{1,0:T(8,128)S(1)}, u32[]{:S(2)}, u32[]{:S(2)}) collective-permute-start(f32[1024,128]{1,0:T(8,128)} %refs_0_.1), channel_id=1, source_target_pairs={{0,2},{1,15},{2,4},{3,1},{4,6},{5,3},{6,8},{7,5},{8,10},{9,7},{10,... | collective-permute-start | bytes 1572872 | tf_op jit(solution)/shard_map/ppermute | solution.py:118
  11.4 31.5 %copy-start.1 = (f32[1024,128]{1,0:T(8,128)}, f32[1024,128]{1,0:T(8,128)S(1)}, u32[]{:S(2)}) copy-start(f32[1024,128]{1,0:T(8,128)S(1)} %collective-permute-done.refs_1_) | copy-start | bytes 1572868
  11.4 15.9 %collective-permute-start.2 = (f32[1024,128]{1,0:T(8,128)S(1)}, f32[1024,128]{1,0:T(8,128)S(1)}, u32[]{:S(2)}, u32[]{:S(2)}) collective-permute-start(f32[1024,128]{1,0:T(8,128)S(1)} %collective-permute-done.refs_1_), channel_id=1, source_target_pairs={{0,2},{1,15},{2,4},{3,1},{4,6},{5,3},{6,8},{7,5},{8,10},{9,7},{10,... | collective-permute-start | bytes 1572872 | tf_op jit(solution)/shard_map/ppermute | solution.py:118
  13.3 32.8 %collective-permute-start.11 = (f32[64,256]{1,0:T(8,128)}, f32[64,256]{1,0:T(8,128)S(1)}, u32[]{:S(2)}, u32[]{:S(2)}) collective-permute-start(f32[64,256]{1,0:T(8,128)} %param.3), channel_id=1, source_target_pairs={{256,0},{272,16},{288,32},{304,48},{320,64},{336,80},{352,96},{368... | collective-permute-start | bytes 196616 | tf_op jit(solution)/shard_map/ppermute | solution.py:134
  24.3 13.8 %collective-permute-start.3 = (f32[1024,128]{1,0:T(8,128)S(1)}, f32[1024,128]{1,0:T(8,128)S(1)}, u32[]{:S(2)}, u32[]{:S(2)}) collective-permute-start(f32[1024,128]{1,0:T(8,128)S(1)} %collective-permute-done.1.refs_2_), channel_id=1, source_target_pairs={{0,2},{1,15},{2,4},{3,1},{4,6},{5,3},{6,8},{7,5},{8,10},{9,7},{10,... | collective-permute-start | bytes 1572872 | tf_op jit(solution)/shard_map/ppermute | solution.py:118
  27.3 13.0 %collective-permute-start.4 = (f32[1024,128]{1,0:T(8,128)S(1)}, f32[1024,128]{1,0:T(8,128)}, u32[]{:S(2)}, u32[]{:S(2)}) collective-permute-start(f32[1024,128]{1,0:T(8,128)S(1)} %collective-permute-done.2.refs_3_), channel_id=1, source_target_pairs={{0,2},{1,15},{2,4},{3,1},{4,6},{5,3},{6,8},{7,5},{8,10},{9,7},{10,... | collective-permute-start | bytes 1572872 | tf_op jit(solution)/shard_map/ppermute | solution.py:118
  32.0 18.2 %all-to-all-start = ((f32[16,2,256]{2,1,0:T(2,128)}), f32[16,2,256]{2,1,0:T(2,128)S(1)}, u32[]{:S(2)}, u32[]{:S(2)}) async-start(f32[16,2,256]{2,1,0:T(2,128)} %broadcast_in_dim.9), calls=%async_computation | async-start | bytes 65536 | tf_op jit(solution)/shard_map/all_to_all | solution.py:110
  40.3 5.8 %copy-start.3 = (f32[64,256]{1,0:T(8,128)S(1)}, f32[64,256]{1,0:T(8,128)}, u32[]{:S(2)}) copy-start(f32[64,256]{1,0:T(8,128)} %param.3) | copy-start | bytes 196612
  42.9 71.3 %collective-permute-start.10 = (f32[4,1024,128]{2,1,0:T(8,128)}, f32[4,1024,128]{2,1,0:T(8,128)}, u32[]{:S(2)}, u32[]{:S(2)}) collective-permute-start(f32[4,1024,128]{2,1,0:T(8,128)} %pad_maximum_fusion), channel_id=1, source_target_pairs={{0,1},{1,0},{2,3},{3,2},{4,5},{5,4},{6,7},{7,6},{8,9},{9,8},{10,11... | collective-permute-start | bytes 6291464 | tf_op jit(solution)/shard_map/ppermute | solution.py:119
  46.1 11.9 %collective-permute-start.12 = (f32[128,256]{1,0:T(8,128)S(1)}, f32[128,256]{1,0:T(8,128)S(1)}, u32[]{:S(2)}, u32[]{:S(2)}) collective-permute-start(f32[128,256]{1,0:T(8,128)S(1)} %pad_maximum_fusion.3), channel_id=1, source_target_pairs={{128,0},{144,16},{160,32},{176,48},{192,64},{208,80},{224,96},{240... | collective-permute-start | bytes 393224 | tf_op jit(solution)/shard_map/ppermute | solution.py:134
  50.2 27.5 %collective-permute-start.5 = (f32[1024,128]{1,0:T(8,128)S(1)}, f32[1024,128]{1,0:T(8,128)S(1)}, u32[]{:S(2)}, u32[]{:S(2)}) collective-permute-start(f32[1024,128]{1,0:T(8,128)S(1)} %collective-permute-done.3.refs_4_), channel_id=1, source_target_pairs={{0,2},{1,15},{2,4},{3,1},{4,6},{5,3},{6,8},{7,5},{8,10},{9,7},{10,... | collective-permute-start | bytes 1572872 | tf_op jit(solution)/shard_map/ppermute | solution.py:118
  54.9 25.7 %collective-permute-start.6 = (f32[1024,128]{1,0:T(8,128)}, f32[1024,128]{1,0:T(8,128)S(1)}, u32[]{:S(2)}, u32[]{:S(2)}) collective-permute-start(f32[1024,128]{1,0:T(8,128)} %collective-permute-done.4.refs_5_), channel_id=1, source_target_pairs={{0,2},{1,15},{2,4},{3,1},{4,6},{5,3},{6,8},{7,5},{8,10},{9,7},{10,... | collective-permute-start | bytes 1572872 | tf_op jit(solution)/shard_map/ppermute | solution.py:118
  58.8 12.9 %collective-permute-start.13 = (f32[256,256]{1,0:T(8,128)}, f32[256,256]{1,0:T(8,128)}, u32[]{:S(2)}, u32[]{:S(2)}) collective-permute-start(f32[256,256]{1,0:T(8,128)} %pad_maximum_fusion.2), channel_id=1, source_target_pairs={{64,0},{80,16},{96,32},{112,48},{128,64},{144,80},{160,96},{176,11... | collective-permute-start | bytes 786440 | tf_op jit(solution)/shard_map/ppermute | solution.py:134
  61.9 37.5 %all-to-all-start.1 = ((f32[32,17,2,128]{3,2,1,0:T(2,128)}), f32[32,17,2,128]{3,2,1,0:T(2,128)}, u32[]{:S(2)}, u32[]{:S(2)}) async-start(f32[32,17,2,128]{3,2,1,0:T(2,128)} %broadcast_in_dim.21), calls=%async_computation.1 | async-start | bytes 1114112 | tf_op jit(solution)/shard_map/all_to_all | solution.py:110
  70.4 43.8 %copy-start = (f32[1024,128]{1,0:T(8,128)S(1)}, f32[1024,128]{1,0:T(8,128)}, u32[]{:S(2)}) copy-start(f32[1024,128]{1,0:T(8,128)} %refs_0_.1) | copy-start | bytes 1572868
  73.3 19.2 %collective-permute-start.14 = (f32[512,256]{1,0:T(8,128)}, f32[512,256]{1,0:T(8,128)S(1)}, u32[]{:S(2)}, u32[]{:S(2)}) collective-permute-start(f32[512,256]{1,0:T(8,128)} %constant_dynamic-update-slice_fusion.refs_12_), channel_id=1, source_target_pairs={{16,0},{32,16},{48,32},{0,48},{80,64},{96,80},{112,96},{64,112},{1... | collective-permute-start | bytes 1572872 | tf_op jit(solution)/shard_map/ppermute | solution.py:135
  77.6 18.5 %collective-permute-start.7 = (f32[1024,128]{1,0:T(8,128)S(1)}, f32[1024,128]{1,0:T(8,128)}, u32[]{:S(2)}, u32[]{:S(2)}) collective-permute-start(f32[1024,128]{1,0:T(8,128)S(1)} %collective-permute-done.5.refs_6_), channel_id=1, source_target_pairs={{0,2},{1,15},{2,4},{3,1},{4,6},{5,3},{6,8},{7,5},{8,10},{9,7},{10,... | collective-permute-start | bytes 1572872 | tf_op jit(solution)/shard_map/ppermute | solution.py:118
  81.7 32.5 %collective-permute-start.9 = (f32[2,1024,128]{2,1,0:T(8,128)}, f32[2,1024,128]{2,1,0:T(8,128)}, u32[]{:S(2)}, u32[]{:S(2)}) collective-permute-start(f32[2,1024,128]{2,1,0:T(8,128)} %pad_maximum_fusion.1), channel_id=1, source_target_pairs={{0,1},{1,0},{2,3},{3,2},{4,5},{5,4},{6,7},{7,6},{8,9},{9,8},{10,11... | collective-permute-start | bytes 3145736 | tf_op jit(solution)/shard_map/ppermute | solution.py:119
  85.4 17.3 %collective-permute-start.15 = (f32[512,256]{1,0:T(8,128)}, f32[512,256]{1,0:T(8,128)}, u32[]{:S(2)}, u32[]{:S(2)}) collective-permute-start(f32[512,256]{1,0:T(8,128)} %constant_dynamic-update-slice_fusion.refs_12_), channel_id=1, source_target_pairs={{32,0},{48,16},{0,32},{16,48},{96,64},{112,80},{64,96},{80,112},{1... | collective-permute-start | bytes 1572872 | tf_op jit(solution)/shard_map/ppermute | solution.py:135
  92.6 3.6 %copy-start.4 = (f32[512,256]{1,0:T(8,128)}, f32[512,256]{1,0:T(8,128)S(1)}, u32[]{:S(2)}) copy-start(f32[512,256]{1,0:T(8,128)S(1)} %collective-permute-done.14.refs_13_) | copy-start | bytes 1572868
  92.6 21.6 %collective-permute-start.16 = (f32[512,256]{1,0:T(8,128)}, f32[512,256]{1,0:T(8,128)}, u32[]{:S(2)}, u32[]{:S(2)}) collective-permute-start(f32[512,256]{1,0:T(8,128)} %constant_dynamic-update-slice_fusion.refs_12_), channel_id=1, source_target_pairs={{48,0},{0,16},{16,32},{32,48},{112,64},{64,80},{80,96},{96,112},{1... | collective-permute-start | bytes 1572872 | tf_op jit(solution)/shard_map/ppermute | solution.py:135
  96.1 18.0 %collective-permute-start.8 = (f32[1024,128]{1,0:T(8,128)}, f32[1024,128]{1,0:T(8,128)}, u32[]{:S(2)}, u32[]{:S(2)}) collective-permute-start(f32[1024,128]{1,0:T(8,128)} %collective-permute-done.7.refs_8_), channel_id=1, source_target_pairs={{0,1},{1,0},{2,3},{3,2},{4,5},{5,4},{6,7},{7,6},{8,9},{9,8},{10,11... | collective-permute-start | bytes 1572872 | tf_op jit(solution)/shard_map/ppermute | solution.py:119
  114.2 1.0 copy-start.2

commit v4 on v3

v4 whole, which is shorter than its diff:
```python
import jax
import jax.numpy as jnp
from jax import lax
from jax.experimental import pallas as pl
from jax.experimental.pallas import tpu as pltpu
from jax.sharding import PartitionSpec as P

NX, NY, NZ = 4, 8, 8
STEP = 256
PAD = 16
VMEM = 48 * 1024 * 1024
Z_ORDER = (0, 4, 2, 6, 1, 5, 3, 7)


def from_plane(dz, dx):
    return [
        (NX * ((z + dz) % NZ) + (x + dx) % NX, NX * z + x) for z in range(NZ) for x in range(NX)
    ]


def check_weights(total, start, count):
    index = (start + jnp.arange(count, dtype=jnp.int32)).astype(jnp.float32)
    flat = jnp.full((count,), 1.0, jnp.float32) / jnp.sqrt(jnp.float32(total))
    ramp = (index + 0.5) / total * jnp.sqrt(jnp.float32(3.0) / total)
    return jnp.stack([flat, ramp], 0)


def halves(value):
    high = value.astype(jnp.bfloat16)
    return high, (value - high.astype(jnp.float32)).astype(jnp.bfloat16)


def dot(left, right, contract=((1,), (0,))):
    return lax.dot_general(left, right, (contract, ((), ())), preferred_element_type=jnp.float32)


def product_kernel(place, t, e0, e1, e2, e3, u, v, main, rows, cols, eh, el, us):
    @pl.when(pl.program_id(0) == 0)
    def _():
        for d, part in enumerate((e0, e1, e2, e3)):
            x = lax.rem(place[0] + d, NX)
            for i, dz in enumerate(Z_ORDER):
                z = lax.rem(place[1] + dz, NZ)
                at = pl.ds(pl.multiple_of((NX * z + x) * 64, 64), 64)
                eh[at, :], el[at, :] = halves(part[i * 64 : (i + 1) * 64, :])
        us[...] = jnp.zeros_like(us)
        for n in range(2 * NY):
            us[:2, n * 128 : (n + 1) * 128] = u[n]

    blocks = [t[n] for n in range(2 * NY)]
    sums = []
    for w in range(2):
        total = blocks[0] * v[0, w : w + 1, :]
        for n in range(1, 2 * NY):
            total += blocks[n] * v[n, w : w + 1, :]
        th, tl = halves(total)
        ones = jnp.ones((PAD, 128), jnp.bfloat16)
        lanes = ((1,), (1,))
        sums.append((dot(ones, th, lanes) + dot(ones, tl, lanes))[:1])
    cols[...] = jnp.concatenate(sums, 0)
    th, tl = halves(jnp.concatenate([jnp.concatenate(blocks, 1), us[...]], 0))
    out = dot(th, eh[...]) + (dot(tl, eh[...]) + dot(th, el[...]))
    main[...] = out[:STEP]
    rows[...] = out[STEP : STEP + 2]


def product(place, t, parts, u, v):
    blocks, m, wide = t.shape
    whole = lambda a: pl.BlockSpec(a.shape, lambda i, s: (0,) * a.ndim)
    depth = blocks * wide
    return pl.pallas_call(
        product_kernel,
        out_shape=(
            jax.ShapeDtypeStruct((m, 256), jnp.float32),
            jax.ShapeDtypeStruct((2, 256), jnp.float32),
            jax.ShapeDtypeStruct((2, m), jnp.float32),
        ),
        grid_spec=pltpu.PrefetchScalarGridSpec(
            num_scalar_prefetch=1,
            grid=(m // STEP,),
            in_specs=[pl.BlockSpec((blocks, STEP, wide), lambda i, s: (0, i, 0))]
            + [whole(a) for a in (*parts, u, v)],
            out_specs=[
                pl.BlockSpec((STEP, 256), lambda i, s: (i, 0)),
                pl.BlockSpec((2, 256), lambda i, s: (0, 0)),
                pl.BlockSpec((2, STEP), lambda i, s: (0, i)),
            ],
            scratch_shapes=[pltpu.VMEM((depth, 256), jnp.bfloat16)] * 2
            + [pltpu.VMEM((PAD, depth), jnp.float32)],
        ),
        compiler_params=pltpu.CompilerParams(vmem_limit_bytes=VMEM),
    )(place, t, *parts, u, v)


def to_all(value, axis, count):
    copies = jnp.broadcast_to(value[None], (count,) + value.shape)
    return lax.all_to_all(copies, axis, split_axis=0, concat_axis=0)


def on_device(transfer, emissions):
    highest = lax.Precision.HIGHEST
    row, col = lax.axis_index("row"), lax.axis_index("col")
    x, z = lax.rem(row, NX), row // NX
    m_local, s_local = transfer.shape[0], emissions.shape[1]
    whole = lax.all_gather(transfer, "col", axis=0)

    receptor = check_weights(m_local * lax.axis_size("row"), row * m_local, m_local)
    u = jnp.dot(receptor, transfer, precision=highest, preferred_element_type=jnp.float32)
    scenario = check_weights(s_local * lax.axis_size("col"), col * s_local, s_local)
    v = jnp.einsum("js,ks->jk", scenario, emissions, precision=highest, preferred_element_type=jnp.float32)
    both = to_all(jnp.concatenate([u, v, jnp.zeros_like(v)], 1), "col", 2 * NY)
    v = both[:, :, 128:].sum(0)

    near = emissions
    for dz in (4, 2, 1):
        near = jnp.concatenate([near, lax.ppermute(near, "row", from_plane(dz, 0))], 0)
    parts = [near] + [lax.ppermute(near, "row", from_plane(0, d)) for d in (1, 2, 3)]

    both = to_all(jnp.concatenate([both[:, :, :128], v[None]], 0), "row", NX * NZ)
    u = both[:, : 2 * NY].sum(0)
    v = both[:, 2 * NY, :, :64].reshape(2 * NY, 2, 2, 64).transpose(0, 2, 1, 3).reshape(2 * NY, 2, 128)

    place = jnp.stack([x, z]).astype(jnp.int32)
    return tuple(product(place, whole, parts, u, v))


def solution(mesh):
    placed = (P("row", "col"), P("row", "col"))
    return jax.shard_map(
        on_device,
        mesh=mesh,
        in_specs=placed,
        out_specs=(P("row", "col"), P(None, "col"), P(None, "row")),
        check_vma=False,
    )
```

time: 126 us -> 116 us (0.921)
  starting transfers between devices: 78.6 us -> 46.6 us
  waiting for transfers between devices: 19.6 us -> 38.8 us
  between operations: 0.98 us -> 14.2 us
  local copies, waits for them, and re-layouts: 8.02 us -> 2.65 us
  other arithmetic: 5.62 us -> 1.98 us
    ppermute x11 -> x0, starting transfers between devices: 39.6 us -> none  [the longest x7 20.7 us: on_device(): pass_on = lambda a: lax.ppermute(a, 'col', RING)]
    ppermute x3, waiting for transfers between devices: 0.01 us -> 14.8 us  [on_device(): lax.ppermute(near, 'row', from_plane(dz, 0))]
    ppermute x3, starting transfers between devices: 15.7 us -> 22.8 us  [on_device(): lax.ppermute(near, 'row', from_plane(dz, 0))]
    ppermute x3, waiting for transfers between devices: 17.4 us -> 23.3 us  [on_device(): lax.ppermute(near, 'row', from_plane(0, d))]
    another operation x3 -> x1, other arithmetic: 3.63 us -> 0.08 us  [on_device(): place = jnp.stack([x, z]).astype(jnp.int32)]
    unnamed x14 -> x4, local copies, waits for them, and re-layouts: 3.81 us -> 0.87 us
    ppermute x11 -> x0, waiting for transfers between devices: 2.23 us -> none  [the longest x7 2.22 us: on_device(): pass_on = lambda a: lax.ppermute(a, 'col', RING)]
    concatenate x1, local copies, waits for them, and re-layouts: 1.68 us -> 0.02 us  [on_device(): jnp.concatenate([near, lax.ppermute(near, 'row', from_plane(dz, 0))], 0)]
  transfers between devices with their start and end apart: 19 -> 9, of which waited for: 4 -> 5; matrix products, arithmetic and copies ran while one was open for 12% -> 6% of each run, Pallas kernels for 0% -> 0%
where the time goes in v4:
time: 116 us
  starting transfers between devices  46.6 us (40%)
  waiting for transfers between devices  38.8 us (33%)
  between operations  14.2 us (12%)
  Pallas kernels  9.05 us (8%)
  local copies, waits for them, and re-layouts  2.65 us (2%)
  matrix products  2.41 us (2%)
  other arithmetic  1.98 us (2%)
    ppermute x3, waiting for transfers between devices, on_device(): lax.ppermute(near, 'row', from_plane(0, d))  23.3 us
    ppermute x3, starting transfers between devices, on_device(): lax.ppermute(near, 'row', from_plane(dz, 0))  22.8 us
    ppermute x3, waiting for transfers between devices, on_device(): lax.ppermute(near, 'row', from_plane(dz, 0))  14.8 us
    all_to_all x2, starting transfers between devices, to_all(): return lax.all_to_all(copies, axis, split_axis=0, concat_axis=0)  14.6 us
    ppermute x3, starting transfers between devices, on_device(): lax.ppermute(near, 'row', from_plane(0, d))  9.19 us
    pallas_call x1, Pallas kernels, product(): pl.pallas_call(product_kernel, out_shape=(jax.ShapeDtypeStruct((m, 256),...  9.05 us
  transfers between devices with their start and end apart: 9, of which 5 were waited for; matrix products, arithmetic and copies ran while one was open for 6% of the time, Pallas kernels for 0%

profile of v4, /device:TPU:1, one launch (start us, length us, event | category | flops | bytes accessed | tf_op | source)
XLA Modules:
  0.0 115.7 jit_solution(15076994544672519945)
XLA Ops:
  7.2 0.0 all-gather.3.cloned.1.call-start
  7.2 0.7 all-gather.3.cloned.1.call-update
  7.9 0.1 pad.6.clone
  8.0 1.0 fusion.2
  9.0 1.4 %fusion = f32[2,128]{1,0:T(2,128)S(1)} fusion(f32[1024,128]{1,0:T(8,128)} %param.2, f32[1,1024]{1,0:T(1,128)S(1)} %add_multiply_fusion), kind=kOutput, calls=%fused_computation.9 | convolution fusion | flops 3145728 | bytes 529408 | tf_op jit(solution)/shard_map/dot_general | solution.py:108
  10.4 0.6 broadcast_in_dim.9
  11.1 10.2 %all-to-all-start = ((f32[16,2,256]{2,1,0:T(2,128)}), f32[16,2,256]{2,1,0:T(2,128)S(1)}, u32[]{:S(2)}, u32[]{:S(2)}) async-start(f32[16,2,256]{2,1,0:T(2,128)} %broadcast_in_dim.9), calls=%async_computation | async-start | bytes 65536 | tf_op jit(solution)/shard_map/all_to_all | solution.py:97
  21.2 9.1 %collective-permute-start = (f32[64,256]{1,0:T(8,128)}, f32[64,256]{1,0:T(8,128)S(1)}, u32[]{:S(2)}, u32[]{:S(2)}) collective-permute-start(f32[64,256]{1,0:T(8,128)} %param.3), channel_id=1, source_target_pairs={{256,0},{272,16},{288,32},{304,48},{320,64},{336,80},{352,96},{368... | collective-permute-start | bytes 196616 | tf_op jit(solution)/shard_map/ppermute | solution.py:116
  30.4 0.0 all-to-all-done
  30.4 2.5 %collective-permute-done = f32[64,256]{1,0:T(8,128)S(1)} collective-permute-done((f32[64,256]{1,0:T(8,128)}, f32[64,256]{1,0:T(8,128)S(1)}, u32[]{:S(2)}, u32[]{:S(2)}) %collective-permute-start) | collective-permute-done | bytes 65568 | tf_op jit(solution)/shard_map/ppermute | solution.py:116
  32.9 0.8 pad_maximum_fusion.1
  33.7 8.8 %collective-permute-start.1 = (f32[128,256]{1,0:T(8,128)S(1)}, f32[128,256]{1,0:T(8,128)S(1)}, u32[]{:S(2)}, u32[]{:S(2)}) collective-permute-start(f32[128,256]{1,0:T(8,128)S(1)} %pad_maximum_fusion.1), channel_id=1, source_target_pairs={{128,0},{144,16},{160,32},{176,48},{192,64},{208,80},{224,96},{240... | collective-permute-start | bytes 393224 | tf_op jit(solution)/shard_map/ppermute | solution.py:116
  42.5 0.9 broadcast_in_dim.21
  43.5 4.4 %all-to-all-start.1 = ((f32[32,17,2,128]{3,2,1,0:T(2,128)}), f32[32,17,2,128]{3,2,1,0:T(2,128)S(1)}, u32[]{:S(2)}, u32[]{:S(2)}) async-start(f32[32,17,2,128]{3,2,1,0:T(2,128)} %broadcast_in_dim.21), calls=%async_computation.1 | async-start | bytes 1114112 | tf_op jit(solution)/shard_map/all_to_all | solution.py:97
  47.9 0.0 collective-permute-done.1
  47.9 0.9 pad_maximum_fusion
  48.8 4.9 %collective-permute-start.2 = (f32[256,256]{1,0:T(8,128)S(1)}, f32[256,256]{1,0:T(8,128)S(1)}, u32[]{:S(2)}, u32[]{:S(2)}) collective-permute-start(f32[256,256]{1,0:T(8,128)S(1)} %pad_maximum_fusion), channel_id=1, source_target_pairs={{64,0},{80,16},{96,32},{112,48},{128,64},{144,80},{160,96},{176,11... | collective-permute-start | bytes 786440 | tf_op jit(solution)/shard_map/ppermute | solution.py:116
  53.7 0.8 constant_dynamic-update-slice_fusion.3
  54.6 12.3 %collective-permute-done.2 = f32[256,256]{1,0:T(8,128)S(1)} collective-permute-done((f32[256,256]{1,0:T(8,128)S(1)}, f32[256,256]{1,0:T(8,128)S(1)}, u32[]{:S(2)}, u32[]{:S(2)}) %collective-permute-start.2) | collective-permute-done | bytes 262176 | tf_op jit(solution)/shard_map/ppermute | solution.py:116
  66.9 4.4 %collective-permute-start.3 = (f32[512,256]{1,0:T(8,128)S(1)}, f32[512,256]{1,0:T(8,128)S(1)}, u32[]{:S(2)}, u32[]{:S(2)}) collective-permute-start(f32[512,256]{1,0:T(8,128)S(1)} %constant_dynamic-update-slice_fusion.e0), channel_id=1, source_target_pairs={{16,0},{32,16},{48,32},{0,48},{80,64},{96,80},{112,96},{64,112},{1... | collective-permute-start | bytes 1572872 | tf_op jit(solution)/shard_map/ppermute | solution.py:117
  71.3 2.3 %collective-permute-start.4 = (f32[512,256]{1,0:T(8,128)S(1)}, f32[512,256]{1,0:T(8,128)S(1)}, u32[]{:S(2)}, u32[]{:S(2)}) collective-permute-start(f32[512,256]{1,0:T(8,128)S(1)} %constant_dynamic-update-slice_fusion.e0), channel_id=1, source_target_pairs={{32,0},{48,16},{0,32},{16,48},{96,64},{112,80},{64,96},{80,112},{1... | collective-permute-start | bytes 1572872 | tf_op jit(solution)/shard_map/ppermute | solution.py:117
  73.6 2.5 %collective-permute-start.5 = (f32[512,256]{1,0:T(8,128)S(1)}, f32[512,256]{1,0:T(8,128)S(1)}, u32[]{:S(2)}, u32[]{:S(2)}) collective-permute-start(f32[512,256]{1,0:T(8,128)S(1)} %constant_dynamic-update-slice_fusion.e0), channel_id=1, source_target_pairs={{48,0},{0,16},{16,32},{32,48},{112,64},{64,80},{80,96},{96,112},{1... | collective-permute-start | bytes 1572872 | tf_op jit(solution)/shard_map/ppermute | solution.py:117
  76.1 0.1 pad_add_fusion.place
  76.2 0.0 all-to-all-done.1
  76.2 0.1 reshape.45
  76.3 0.1 slice_reduce_fusion.u
  76.5 5.5 %collective-permute-done.3.e1 = f32[512,256]{1,0:T(8,128)S(1)} collective-permute-done((f32[512,256]{1,0:T(8,128)S(1)}, f32[512,256]{1,0:T(8,128)S(1)}, u32[]{:S(2)}, u32[]{:S(2)}) %collective-permute-start.3) | collective-permute-done | bytes 524320 | tf_op jit(solution)/shard_map/ppermute | solution.py:117
  82.0 4.5 %collective-permute-done.4.e2 = f32[512,256]{1,0:T(8,128)S(1)} collective-permute-done((f32[512,256]{1,0:T(8,128)S(1)}, f32[512,256]{1,0:T(8,128)S(1)}, u32[]{:S(2)}, u32[]{:S(2)}) %collective-permute-start.4) | collective-permute-done | bytes 524320 | tf_op jit(solution)/shard_map/ppermute | solution.py:117
  86.4 13.3 %collective-permute-done.5.e3 = f32[512,256]{1,0:T(8,128)S(1)} collective-permute-done((f32[512,256]{1,0:T(8,128)S(1)}, f32[512,256]{1,0:T(8,128)S(1)}, u32[]{:S(2)}, u32[]{:S(2)}) %collective-permute-start.5) | collective-permute-done | bytes 524320 | tf_op jit(solution)/shard_map/ppermute | solution.py:117
  99.8 0.0 all-gather.3.cloned.1.call-done
  99.8 9.0 %shard_map.49 = (f32[1024,256]{1,0:T(8,128)}, f32[2,256]{1,0:T(2,128)}, f32[2,1024]{1,0:T(2,128)}) custom-call(s32[2]{0:T(128)S(1)} %pad_add_fusion.place, f32[16,1024,128]{2,1,0:T(8,128)} %bitcast.11, f32[512,256]{1,0:T(8,128)S(1)} %constant_dynamic-update-slice_fusion.e0, f32[512,256]{1,0:T(8,128)S(1)} %collective-permute-done.3.e1, ...), custom_call_target="tpu_custom_call" | custom-call | tf_op jit(solution)/shard_map/pallas_call | solution.py:71
  (12 shorter events, 0.1 us)
Async XLA Ops:
  7.2 92.6 %all-gather.3.cloned.1.call-start = ((), (), s32[]{:S(2)}) async-start(), calls=%async_computation.2 | async-start | bytes 8912896 | tf_op jit(solution)/shard_map/all_gather | solution.py:105
  11.1 19.3 %all-to-all-start = ((f32[16,2,256]{2,1,0:T(2,128)}), f32[16,2,256]{2,1,0:T(2,128)S(1)}, u32[]{:S(2)}, u32[]{:S(2)}) async-start(f32[16,2,256]{2,1,0:T(2,128)} %broadcast_in_dim.9), calls=%async_computation | async-start | bytes 65536 | tf_op jit(solution)/shard_map/all_to_all | solution.py:97
  21.2 11.6 %collective-permute-start = (f32[64,256]{1,0:T(8,128)}, f32[64,256]{1,0:T(8,128)S(1)}, u32[]{:S(2)}, u32[]{:S(2)}) collective-permute-start(f32[64,256]{1,0:T(8,128)} %param.3), channel_id=1, source_target_pairs={{256,0},{272,16},{288,32},{304,48},{320,64},{336,80},{352,96},{368... | collective-permute-start | bytes 196616 | tf_op jit(solution)/shard_map/ppermute | solution.py:116
  33.7 14.2 %collective-permute-start.1 = (f32[128,256]{1,0:T(8,128)S(1)}, f32[128,256]{1,0:T(8,128)S(1)}, u32[]{:S(2)}, u32[]{:S(2)}) collective-permute-start(f32[128,256]{1,0:T(8,128)S(1)} %pad_maximum_fusion.1), channel_id=1, source_target_pairs={{128,0},{144,16},{160,32},{176,48},{192,64},{208,80},{224,96},{240... | collective-permute-start | bytes 393224 | tf_op jit(solution)/shard_map/ppermute | solution.py:116
  43.5 32.7 %all-to-all-start.1 = ((f32[32,17,2,128]{3,2,1,0:T(2,128)}), f32[32,17,2,128]{3,2,1,0:T(2,128)S(1)}, u32[]{:S(2)}, u32[]{:S(2)}) async-start(f32[32,17,2,128]{3,2,1,0:T(2,128)} %broadcast_in_dim.21), calls=%async_computation.1 | async-start | bytes 1114112 | tf_op jit(solution)/shard_map/all_to_all | solution.py:97
  48.8 18.1 %collective-permute-start.2 = (f32[256,256]{1,0:T(8,128)S(1)}, f32[256,256]{1,0:T(8,128)S(1)}, u32[]{:S(2)}, u32[]{:S(2)}) collective-permute-start(f32[256,256]{1,0:T(8,128)S(1)} %pad_maximum_fusion), channel_id=1, source_target_pairs={{64,0},{80,16},{96,32},{112,48},{128,64},{144,80},{160,96},{176,11... | collective-permute-start | bytes 786440 | tf_op jit(solution)/shard_map/ppermute | solution.py:116
  66.9 15.1 %collective-permute-start.3 = (f32[512,256]{1,0:T(8,128)S(1)}, f32[512,256]{1,0:T(8,128)S(1)}, u32[]{:S(2)}, u32[]{:S(2)}) collective-permute-start(f32[512,256]{1,0:T(8,128)S(1)} %constant_dynamic-update-slice_fusion.e0), channel_id=1, source_target_pairs={{16,0},{32,16},{48,32},{0,48},{80,64},{96,80},{112,96},{64,112},{1... | collective-permute-start | bytes 1572872 | tf_op jit(solution)/shard_map/ppermute | solution.py:117
  71.3 15.1 %collective-permute-start.4 = (f32[512,256]{1,0:T(8,128)S(1)}, f32[512,256]{1,0:T(8,128)S(1)}, u32[]{:S(2)}, u32[]{:S(2)}) collective-permute-start(f32[512,256]{1,0:T(8,128)S(1)} %constant_dynamic-update-slice_fusion.e0), channel_id=1, source_target_pairs={{32,0},{48,16},{0,32},{16,48},{96,64},{112,80},{64,96},{80,112},{1... | collective-permute-start | bytes 1572872 | tf_op jit(solution)/shard_map/ppermute | solution.py:117
  73.6 26.2 %collective-permute-start.5 = (f32[512,256]{1,0:T(8,128)S(1)}, f32[512,256]{1,0:T(8,128)S(1)}, u32[]{:S(2)}, u32[]{:S(2)}) collective-permute-start(f32[512,256]{1,0:T(8,128)S(1)} %constant_dynamic-update-slice_fusion.e0), channel_id=1, source_target_pairs={{48,0},{0,16},{16,32},{32,48},{112,64},{64,80},{80,96},{96,112},{1... | collective-permute-start | bytes 1572872 | tf_op jit(solution)/shard_map/ppermute | solution.py:117
Sparse Core Ops, SparseCore 0:
  10.1 64.1 all-gather.2

commit v5 on v4

--- a/solution.py
+++ b/solution.py
@@ -9,13 +9,13 @@
 STEP = 256
 PAD = 16
 VMEM = 48 * 1024 * 1024
-Z_ORDER = (0, 4, 2, 6, 1, 5, 3, 7)
+DEPTH = 64 * NZ
+
+Z_GROUPS = [[NX * z + x for z in range(NZ)] for x in range(NX)]
 
 
-def from_plane(dz, dx):
-    return [
-        (NX * ((z + dz) % NZ) + (x + dx) % NX, NX * z + x) for z in range(NZ) for x in range(NX)
-    ]
+def from_x(dx):
+    return [(NX * z + (x + dx) % NX, NX * z + x) for z in range(NZ) for x in range(NX)]
 
 
 def check_weights(total, start, count):
@@ -34,18 +34,27 @@
     return lax.dot_general(left, right, (contract, ((), ())), preferred_element_type=jnp.float32)
 
 
-def product_kernel(place, t, e0, e1, e2, e3, u, v, main, rows, cols, eh, el, us):
+def product_kernel(place, t, e0, e1, e2, e3, main, rows, cols, eh, el, us, v):
     @pl.when(pl.program_id(0) == 0)
     def _():
+        v[...] = jnp.zeros_like(v)
+        upper = lax.broadcasted_iota(jnp.int32, (1, 128), 1) // 64
         for d, part in enumerate((e0, e1, e2, e3)):
             x = lax.rem(place[0] + d, NX)
-            for i, dz in enumerate(Z_ORDER):
-                z = lax.rem(place[1] + dz, NZ)
+            here = upper == lax.rem(x, 2)
+            for z in range(NZ):
                 at = pl.ds(pl.multiple_of((NX * z + x) * 64, 64), 64)
-                eh[at, :], el[at, :] = halves(part[i * 64 : (i + 1) * 64, :])
+                eh[at, :], el[at, :] = halves(part[z * 64 : (z + 1) * 64, :])
+                own = part[DEPTH + 16 + z : DEPTH + 17 + z, :]
+                both = jnp.concatenate([own[:, :128], own[:, 128:]], 0)
+                v[2 * z + x // 2] += jnp.where(here, both, 0.0)
         us[...] = jnp.zeros_like(us)
+        total = (e0[DEPTH : DEPTH + 16, :] + e1[DEPTH : DEPTH + 16, :]) + (
+            e2[DEPTH : DEPTH + 16, :] + e3[DEPTH : DEPTH + 16, :]
+        )
         for n in range(2 * NY):
-            us[:2, n * 128 : (n + 1) * 128] = u[n]
+            for w in range(2):
+                us[w : w + 1, n * 128 : (n + 1) * 128] = total[n : n + 1, w * 128 : (w + 1) * 128]
 
     blocks = [t[n] for n in range(2 * NY)]
     sums = []
@@ -64,7 +73,7 @@
     rows[...] = out[STEP : STEP + 2]
 
 
-def product(place, t, parts, u, v):
+def product(place, t, parts):
     blocks, m, wide = t.shape
     whole = lambda a: pl.BlockSpec(a.shape, lambda i, s: (0,) * a.ndim)
     depth = blocks * wide
@@ -79,28 +88,28 @@
             num_scalar_prefetch=1,
             grid=(m // STEP,),
             in_specs=[pl.BlockSpec((blocks, STEP, wide), lambda i, s: (0, i, 0))]
-            + [whole(a) for a in (*parts, u, v)],
+            + [whole(a) for a in parts],
             out_specs=[
                 pl.BlockSpec((STEP, 256), lambda i, s: (i, 0)),
                 pl.BlockSpec((2, 256), lambda i, s: (0, 0)),
                 pl.BlockSpec((2, STEP), lambda i, s: (0, i)),
             ],
             scratch_shapes=[pltpu.VMEM((depth, 256), jnp.bfloat16)] * 2
-            + [pltpu.VMEM((PAD, depth), jnp.float32)],
+            + [pltpu.VMEM((PAD, depth), jnp.float32), pltpu.VMEM((blocks, 2, wide), jnp.float32)],
         ),
         compiler_params=pltpu.CompilerParams(vmem_limit_bytes=VMEM),
-    )(place, t, *parts, u, v)
+    )(place, t, *parts)
 
 
-def to_all(value, axis, count):
+def to_all(value, axis, count, groups=None):
     copies = jnp.broadcast_to(value[None], (count,) + value.shape)
-    return lax.all_to_all(copies, axis, split_axis=0, concat_axis=0)
+    return lax.all_to_all(copies, axis, split_axis=0, concat_axis=0, axis_index_groups=groups)
 
 
 def on_device(transfer, emissions):
     highest = lax.Precision.HIGHEST
     row, col = lax.axis_index("row"), lax.axis_index("col")
-    x, z = lax.rem(row, NX), row // NX
+    x = lax.rem(row, NX)
     m_local, s_local = transfer.shape[0], emissions.shape[1]
     whole = lax.all_gather(transfer, "col", axis=0)
 
@@ -109,19 +118,18 @@
     scenario = check_weights(s_local * lax.axis_size("col"), col * s_local, s_local)
     v = jnp.einsum("js,ks->jk", scenario, emissions, precision=highest, preferred_element_type=jnp.float32)
     both = to_all(jnp.concatenate([u, v, jnp.zeros_like(v)], 1), "col", 2 * NY)
-    v = both[:, :, 128:].sum(0)
+    v = both[:, :, 128:192].sum(0)
+    v = jnp.concatenate([v[:1], v[:1], v[1:], v[1:]], 1)
+    sent = jnp.concatenate(
+        [emissions, both[:, :, :128].reshape(2 * NY, s_local), v, jnp.zeros((7, s_local), jnp.float32)], 0
+    )
 
-    near = emissions
-    for dz in (4, 2, 1):
-        near = jnp.concatenate([near, lax.ppermute(near, "row", from_plane(dz, 0))], 0)
-    parts = [near] + [lax.ppermute(near, "row", from_plane(0, d)) for d in (1, 2, 3)]
+    near = to_all(sent, "row", NZ, Z_GROUPS)
+    near = jnp.concatenate([near[:, :64].reshape(DEPTH, s_local), near[:, 64:80].sum(0), near[:, 80]], 0)
+    parts = [near] + [lax.ppermute(near, "row", from_x(d)) for d in (1, 2, 3)]
 
-    both = to_all(jnp.concatenate([both[:, :, :128], v[None]], 0), "row", NX * NZ)
-    u = both[:, : 2 * NY].sum(0)
-    v = both[:, 2 * NY, :, :64].reshape(2 * NY, 2, 2, 64).transpose(0, 2, 1, 3).reshape(2 * NY, 2, 128)
-
-    place = jnp.stack([x, z]).astype(jnp.int32)
-    return tuple(product(place, whole, parts, u, v))
+    place = jnp.stack([x]).astype(jnp.int32)
+    return tuple(product(place, whole, parts))
 
 
 def solution(mesh):

time: 116 us -> 107 us (0.922); the launches traced: 116 us -> 105 us
  blocking collectives: 0 us -> 29 us
  starting transfers between devices: 46.6 us -> 20.7 us
  waiting for transfers between devices: 38.8 us -> 28.2 us
  local copies, waits for them, and re-layouts: 2.65 us -> 0.9 us
    all_to_all x0 -> x1, blocking collectives: none -> 29 us  [to_all(): lax.all_to_all(copies, axis, split_axis=0, concat_axis=0, axis_index_grou...]
    ppermute x6 -> x3, starting transfers between devices: 32 us -> 10.5 us  [on_device(): parts = [near] + [lax.ppermute(near, 'row', from_x(d)) for d in (1, 2, 3)]]
    ppermute x6 -> x3, waiting for transfers between devices: 38.1 us -> 20.1 us  [on_device(): parts = [near] + [lax.ppermute(near, 'row', from_x(d)) for d in (1, 2, 3)]]
    all_to_all x2 -> x1, waiting for transfers between devices: 0.01 us -> 7.4 us  [to_all(): lax.all_to_all(copies, axis, split_axis=0, concat_axis=0, axis_index_grou...]
    all_to_all x2 -> x1, starting transfers between devices: 14.6 us -> 10.2 us  [to_all(): lax.all_to_all(copies, axis, split_axis=0, concat_axis=0, axis_index_grou...]
  transfers between devices with their start and end apart: 9 -> 5, of which waited for: 5 -> 4; matrix products, arithmetic and copies ran while one was open for 6% -> 4% of each run, Pallas kernels for 0% -> 0%
where the time goes in v5:
time: 107 us; the launch traced here: 105 us
  blocking collectives  29 us (27%)
  waiting for transfers between devices  28.2 us (26%)
  starting transfers between devices  20.7 us (19%)
  between operations  14.1 us (13%)
  Pallas kernels  8.61 us (8%)
  matrix products  2.41 us (2%)
    all_to_all x1, blocking collectives, to_all(): lax.all_to_all(copies, axis, split_axis=0, concat_axis=0, axis_index_grou...  29 us
    ppermute x3, waiting for transfers between devices, on_device(): parts = [near] + [lax.ppermute(near, 'row', from_x(d)) for d in (1, 2, 3)]  20.1 us
    ppermute x3, starting transfers between devices, on_device(): parts = [near] + [lax.ppermute(near, 'row', from_x(d)) for d in (1, 2, 3)]  10.5 us
    all_to_all x1, starting transfers between devices, to_all(): lax.all_to_all(copies, axis, split_axis=0, concat_axis=0, axis_index_grou...  10.2 us
    pallas_call x1, Pallas kernels, product(): pl.pallas_call(product_kernel, out_shape=(jax.ShapeDtypeStruct((m, 256),...  8.61 us
    all_to_all x1, waiting for transfers between devices, to_all(): lax.all_to_all(copies, axis, split_axis=0, concat_axis=0, axis_index_grou...  7.4 us
  transfers between devices with their start and end apart: 5, of which 4 were waited for; matrix products, arithmetic and copies ran while one was open for 4% of the time, Pallas kernels for 0%

profile of v5, /device:TPU:1, one launch (start us, length us, event | category | flops | bytes accessed | tf_op | source)
XLA Modules:
  0.0 105.1 jit_solution(13431931515555931246)
XLA Ops:
  7.2 0.0 all-gather.3.cloned.1.call-start
  7.2 0.7 all-gather.3.cloned.1.call-update
  7.9 0.1 pad.14.clone
  8.0 1.0 fusion.2
  9.0 1.4 %fusion = f32[2,128]{1,0:T(2,128)S(1)} fusion(f32[1024,128]{1,0:T(8,128)} %param.2, f32[1,1024]{1,0:T(1,128)S(1)} %add_multiply_fusion), kind=kOutput, calls=%fused_computation.6 | convolution fusion | flops 3145728 | bytes 529408 | tf_op jit(solution)/shard_map/dot_general | solution.py:117
  10.4 0.6 broadcast_in_dim.9
  11.1 10.2 %all-to-all-start = ((f32[16,2,256]{2,1,0:T(2,128)}), f32[16,2,256]{2,1,0:T(2,128)S(1)}, u32[]{:S(2)}, u32[]{:S(2)}) async-start(f32[16,2,256]{2,1,0:T(2,128)} %broadcast_in_dim.9), calls=%async_computation | async-start | bytes 65536 | tf_op jit(solution)/shard_map/all_to_all | solution.py:106
  21.2 0.1 pad.11.clone
  21.3 7.4 %all-to-all-done = f32[16,2,256]{2,1,0:T(2,128)S(1)} async-done(((f32[16,2,256]{2,1,0:T(2,128)}), f32[16,2,256]{2,1,0:T(2,128)S(1)}, u32[]{:S(2)}, u32[]{:S(2)}) %all-to-all-start) | async-done | bytes 32800 | tf_op jit(solution)/shard_map/all_to_all | solution.py:106
  28.8 0.9 maximum_maximum_fusion
  29.8 29.0 %all_to_all.10 = f32[8,88,256]{2,1,0:T(8,128)S(1)} all-to-all(f32[8,88,256]{2,1,0:T(8,128)S(1)} %broadcast_in_dim.21), channel_id=1, replica_groups={{0,64,128,192,256,320,384,448},{16,80,144,208,272,336,400,464},{32,96,1..., dimensions={0} | all-to-all | bytes 1441792 | tf_op jit(solution)/shard_map/all_to_all | solution.py:106
  58.9 3.1 %collective-permute-start.2 = (f32[536,256]{1,0:T(8,128)S(1)}, f32[536,256]{1,0:T(8,128)S(1)}, u32[]{:S(2)}, u32[]{:S(2)}) collective-permute-start(f32[536,256]{1,0:T(8,128)S(1)} %pad_maximum_fusion.e0), channel_id=1, source_target_pairs={{48,0},{0,16},{16,32},{32,48},{112,64},{64,80},{80,96},{96,112},{1... | collective-permute-start | bytes 1646600 | tf_op jit(solution)/shard_map/ppermute | solution.py:129
  62.0 4.4 %collective-permute-start.1 = (f32[536,256]{1,0:T(8,128)S(1)}, f32[536,256]{1,0:T(8,128)S(1)}, u32[]{:S(2)}, u32[]{:S(2)}) collective-permute-start(f32[536,256]{1,0:T(8,128)S(1)} %pad_maximum_fusion.e0), channel_id=1, source_target_pairs={{32,0},{48,16},{0,32},{16,48},{96,64},{112,80},{64,96},{80,112},{1... | collective-permute-start | bytes 1646600 | tf_op jit(solution)/shard_map/ppermute | solution.py:129
  66.4 3.1 %collective-permute-start = (f32[536,256]{1,0:T(8,128)S(1)}, f32[536,256]{1,0:T(8,128)S(1)}, u32[]{:S(2)}, u32[]{:S(2)}) collective-permute-start(f32[536,256]{1,0:T(8,128)S(1)} %pad_maximum_fusion.e0), channel_id=1, source_target_pairs={{16,0},{32,16},{48,32},{0,48},{80,64},{96,80},{112,96},{64,112},{1... | collective-permute-start | bytes 1646600 | tf_op jit(solution)/shard_map/ppermute | solution.py:129
  69.5 4.6 %collective-permute-done.2.e3 = f32[536,256]{1,0:T(8,128)S(1)} collective-permute-done((f32[536,256]{1,0:T(8,128)S(1)}, f32[536,256]{1,0:T(8,128)S(1)}, u32[]{:S(2)}, u32[]{:S(2)}) %collective-permute-start.2) | collective-permute-done | bytes 548896 | tf_op jit(solution)/shard_map/ppermute | solution.py:129
  74.1 12.7 %collective-permute-done.1.e2 = f32[536,256]{1,0:T(8,128)S(1)} collective-permute-done((f32[536,256]{1,0:T(8,128)S(1)}, f32[536,256]{1,0:T(8,128)S(1)}, u32[]{:S(2)}, u32[]{:S(2)}) %collective-permute-start.1) | collective-permute-done | bytes 548896 | tf_op jit(solution)/shard_map/ppermute | solution.py:129
  86.8 2.8 %collective-permute-done.e1 = f32[536,256]{1,0:T(8,128)S(1)} collective-permute-done((f32[536,256]{1,0:T(8,128)S(1)}, f32[536,256]{1,0:T(8,128)S(1)}, u32[]{:S(2)}, u32[]{:S(2)}) %collective-permute-start) | collective-permute-done | bytes 548896 | tf_op jit(solution)/shard_map/ppermute | solution.py:129
  89.6 0.0 all-gather.3.cloned.1.call-done
  89.6 8.6 %shard_map.49 = (f32[1024,256]{1,0:T(8,128)}, f32[2,256]{1,0:T(2,128)}, f32[2,1024]{1,0:T(2,128)}) custom-call(s32[1]{0:T(128)} %bitcast.place, f32[16,1024,128]{2,1,0:T(8,128)} %bitcast.12, f32[536,256]{1,0:T(8,128)S(1)} %pad_maximum_fusion.e0, f32[536,256]{1,0:T(8,128)S(1)} %collective-permute-done.e1, f32[536,256]{1,0:T(8,128)S(1)} %collective-permute-done.1.e2, ...), custom_call_target="tpu_custom_call" | custom-call | tf_op jit(solution)/shard_map/pallas_call | solution.py:80
  (15 shorter events, 0.2 us)
Async XLA Ops:
  7.2 82.4 %all-gather.3.cloned.1.call-start = ((), (), s32[]{:S(2)}) async-start(), calls=%async_computation.2 | async-start | bytes 8912896 | tf_op jit(solution)/shard_map/all_gather | solution.py:114
  11.1 17.6 %all-to-all-start = ((f32[16,2,256]{2,1,0:T(2,128)}), f32[16,2,256]{2,1,0:T(2,128)S(1)}, u32[]{:S(2)}, u32[]{:S(2)}) async-start(f32[16,2,256]{2,1,0:T(2,128)} %broadcast_in_dim.9), calls=%async_computation | async-start | bytes 65536 | tf_op jit(solution)/shard_map/all_to_all | solution.py:106
  58.9 15.2 %collective-permute-start.2 = (f32[536,256]{1,0:T(8,128)S(1)}, f32[536,256]{1,0:T(8,128)S(1)}, u32[]{:S(2)}, u32[]{:S(2)}) collective-permute-start(f32[536,256]{1,0:T(8,128)S(1)} %pad_maximum_fusion.e0), channel_id=1, source_target_pairs={{48,0},{0,16},{16,32},{32,48},{112,64},{64,80},{80,96},{96,112},{1... | collective-permute-start | bytes 1646600 | tf_op jit(solution)/shard_map/ppermute | solution.py:129
  62.0 24.8 %collective-permute-start.1 = (f32[536,256]{1,0:T(8,128)S(1)}, f32[536,256]{1,0:T(8,128)S(1)}, u32[]{:S(2)}, u32[]{:S(2)}) collective-permute-start(f32[536,256]{1,0:T(8,128)S(1)} %pad_maximum_fusion.e0), channel_id=1, source_target_pairs={{32,0},{48,16},{0,32},{16,48},{96,64},{112,80},{64,96},{80,112},{1... | collective-permute-start | bytes 1646600 | tf_op jit(solution)/shard_map/ppermute | solution.py:129
  66.4 23.2 %collective-permute-start = (f32[536,256]{1,0:T(8,128)S(1)}, f32[536,256]{1,0:T(8,128)S(1)}, u32[]{:S(2)}, u32[]{:S(2)}) collective-permute-start(f32[536,256]{1,0:T(8,128)S(1)} %pad_maximum_fusion.e0), channel_id=1, source_target_pairs={{16,0},{32,16},{48,32},{0,48},{80,64},{96,80},{112,96},{64,112},{1... | collective-permute-start | bytes 1646600 | tf_op jit(solution)/shard_map/ppermute | solution.py:129
Sparse Core Ops, SparseCore 0:
  10.1 64.1 all-gather.2

commit v6 on v5

v6 whole, which is shorter than its diff:
```python
import jax
import jax.numpy as jnp
from jax import lax
from jax.experimental import pallas as pl
from jax.experimental.pallas import tpu as pltpu
from jax.sharding import PartitionSpec as P

NX, NY, NZ = 4, 8, 8
STEP = 256
PAD = 16
VMEM = 40 * 1024 * 1024
DEPTH = 64 * NZ

Z_GROUPS = [[NX * z + x for z in range(NZ)] for x in range(NX)]


def from_x(dx):
    return [(NX * z + (x + dx) % NX, NX * z + x) for z in range(NZ) for x in range(NX)]


def check_weights(total, start, count):
    index = (start + jnp.arange(count, dtype=jnp.int32)).astype(jnp.float32)
    flat = jnp.full((count,), 1.0, jnp.float32) / jnp.sqrt(jnp.float32(total))
    ramp = (index + 0.5) / total * jnp.sqrt(jnp.float32(3.0) / total)
    return jnp.stack([flat, ramp], 0)


def halves(value):
    high = value.astype(jnp.bfloat16)
    return high, (value - high.astype(jnp.float32)).astype(jnp.bfloat16)


def dot(left, right, contract=((1,), (0,))):
    return lax.dot_general(left, right, (contract, ((), ())), preferred_element_type=jnp.float32)


def split_kernel(t, high, low):
    high[...], low[...] = halves(jnp.concatenate([t[n] for n in range(t.shape[0])], 1))


def split(t):
    blocks, m, wide = t.shape
    shape = jax.ShapeDtypeStruct((m, blocks * wide), jnp.bfloat16)
    return pl.pallas_call(
        split_kernel,
        out_shape=(shape, shape),
        grid=(m // STEP,),
        in_specs=[pl.BlockSpec((blocks, STEP, wide), lambda i: (0, i, 0))],
        out_specs=[pl.BlockSpec((STEP, blocks * wide), lambda i: (i, 0))] * 2,
        compiler_params=pltpu.CompilerParams(vmem_limit_bytes=VMEM),
    )(t)


def product_kernel(place, th, tl, e0, e1, e2, e3, main, rows, cols, mv, eh, el, v, gone):
    v[...] = jnp.zeros_like(v)
    upper = lax.broadcasted_iota(jnp.int32, (1, 128), 1) // 64
    for d, part in enumerate((e0, e1, e2, e3)):
        x = lax.rem(place[0] + d, NX)
        here = upper == lax.rem(x, 2)
        for z in range(NZ):
            at = pl.ds(pl.multiple_of((NX * z + x) * 64, 64), 64)
            eh[at, :], el[at, :] = halves(part[z * 64 : (z + 1) * 64, :])
            own = part[DEPTH + 16 + z : DEPTH + 17 + z, :]
            both = jnp.concatenate([own[:, :128], own[:, 128:]], 0)
            v[2 * z + x // 2] += jnp.where(here, both, 0.0)
    total = (e0[DEPTH : DEPTH + 16, :] + e1[DEPTH : DEPTH + 16, :]) + (
        e2[DEPTH : DEPTH + 16, :] + e3[DEPTH : DEPTH + 16, :]
    )
    us = [jnp.concatenate([total[n : n + 1, w : w + 128] for n in range(2 * NY)], 1) for w in (0, 128)]
    uh, ul = halves(jnp.concatenate(us + [jnp.zeros((PAD - 2, us[0].shape[1]), jnp.float32)], 0))
    ones = jnp.ones((PAD, 128), jnp.bfloat16)
    lanes = ((1,), (1,))

    stores = []
    for i in range(mv.shape[0]):
        at = slice(i * STEP, (i + 1) * STEP)
        left, right = th[at, :], tl[at, :]
        if i == 0:
            left, right = jnp.concatenate([left, uh], 0), jnp.concatenate([right, ul], 0)
        out = dot(left, eh[...]) + (dot(right, eh[...]) + dot(left, el[...]))
        mv[i] = out[:STEP]
        if i == 0:
            rows[...] = out[STEP : STEP + 2]
        stores.append(pltpu.make_async_copy(mv.at[i], main.at[pl.ds(i * STEP, STEP), :], gone.at[i]))
        stores[i].start()
        sums = [0.0, 0.0]
        for n in range(2 * NY):
            k = slice(n * 128, (n + 1) * 128)
            block = th[at, k].astype(jnp.float32) + tl[at, k].astype(jnp.float32)
            for w in range(2):
                sums[w] += block * v[n, w : w + 1, :]
        for w in range(2):
            sh, sl = halves(sums[w])
            cols[w : w + 1, at] = (dot(ones, sh, lanes) + dot(ones, sl, lanes))[:1]
    for store in stores:
        store.wait()


def product(place, th, tl, parts):
    m, depth = th.shape
    steps = m // STEP
    vmem = pl.BlockSpec(memory_space=pltpu.VMEM)
    return pl.pallas_call(
        product_kernel,
        out_shape=(
            jax.ShapeDtypeStruct((m, 256), jnp.float32),
            jax.ShapeDtypeStruct((2, 256), jnp.float32),
            jax.ShapeDtypeStruct((2, m), jnp.float32),
        ),
        in_specs=[pl.BlockSpec(memory_space=pltpu.SMEM)] + [vmem] * 6,
        out_specs=[pl.BlockSpec(memory_space=pl.ANY), vmem, vmem],
        scratch_shapes=[
            pltpu.VMEM((steps, STEP, 256), jnp.float32),
            pltpu.VMEM((depth, 256), jnp.bfloat16),
            pltpu.VMEM((depth, 256), jnp.bfloat16),
            pltpu.VMEM((2 * NY, 2, 128), jnp.float32),
            pltpu.SemaphoreType.DMA((steps,)),
        ],
        compiler_params=pltpu.CompilerParams(vmem_limit_bytes=VMEM),
    )(place, th, tl, *parts)


def to_all(value, axis, count, groups=None):
    copies = jnp.broadcast_to(value[None], (count,) + value.shape)
    return lax.all_to_all(copies, axis, split_axis=0, concat_axis=0, axis_index_groups=groups)


def on_device(transfer, emissions):
    highest = lax.Precision.HIGHEST
    row, col = lax.axis_index("row"), lax.axis_index("col")
    x = lax.rem(row, NX)
    m_local, s_local = transfer.shape[0], emissions.shape[1]
    whole = lax.all_gather(transfer, "col", axis=0)

    receptor = check_weights(m_local * lax.axis_size("row"), row * m_local, m_local)
    u = jnp.dot(receptor, transfer, precision=highest, preferred_element_type=jnp.float32)
    scenario = check_weights(s_local * lax.axis_size("col"), col * s_local, s_local)
    v = jnp.einsum("js,ks->jk", scenario, emissions, precision=highest, preferred_element_type=jnp.float32)
    both = to_all(jnp.concatenate([u, v, jnp.zeros_like(v)], 1), "col", 2 * NY)
    v = both[:, :, 128:192].sum(0)
    v = jnp.concatenate([v[:1], v[:1], v[1:], v[1:]], 1)
    sent = jnp.concatenate(
        [emissions, both[:, :, :128].reshape(2 * NY, s_local), v, jnp.zeros((7, s_local), jnp.float32)], 0
    )

    near = to_all(sent, "row", NZ, Z_GROUPS)
    near = jnp.concatenate([near[:, :64].reshape(DEPTH, s_local), near[:, 64:80].sum(0), near[:, 80]], 0)
    parts = [near] + [lax.ppermute(near, "row", from_x(d)) for d in (1, 2, 3)]

    place = jnp.stack([x]).astype(jnp.int32)
    return tuple(product(place, *split(whole), parts))


def solution(mesh):
    placed = (P("row", "col"), P("row", "col"))
    return jax.shard_map(
        on_device,
        mesh=mesh,
        in_specs=placed,
        out_specs=(P("row", "col"), P(None, "col"), P(None, "row")),
        check_vma=False,
    )
```

time: 107 us -> 105 us (0.981)
  waiting for transfers between devices: 28.2 us -> 23.6 us
  Pallas kernels: 8.61 us -> 11.6 us
    ppermute x3, waiting for transfers between devices: 20.1 us -> 10.7 us  [on_device(): parts = [near] + [lax.ppermute(near, 'row', from_x(d)) for d in (1, 2, 3)]]
    all_gather x1, waiting for transfers between devices: 0.01 us -> 4.82 us  [on_device(): whole = lax.all_gather(transfer, 'col', axis=0)]
    pallas_call x0 -> x1, Pallas kernels: none -> 4.65 us  [split(): pl.pallas_call(split_kernel, out_shape=(shape, shape), grid=(m // STEP,),...]
    pallas_call x1, Pallas kernels: 8.61 us -> 6.93 us  [product(): pl.pallas_call(product_kernel, out_shape=(jax.ShapeDtypeStruct((m, 256),...]
  transfers between devices with their start and end apart: 5 -> 5, of which waited for: 4 -> 4; matrix products, arithmetic and copies ran while one was open for 4% -> 4% of each run, Pallas kernels for 0% -> 4%
where the time goes in v6:
time: 105 us; the launch traced here: 103 us
  blocking collectives  29 us (28%)
  waiting for transfers between devices  23.6 us (22%)
  starting transfers between devices  20.7 us (20%)
  between operations  14.2 us (14%)
  Pallas kernels  11.6 us (11%)
  matrix products  2.41 us (2%)
    all_to_all x1, blocking collectives, to_all(): lax.all_to_all(copies, axis, split_axis=0, concat_axis=0, axis_index_grou...  29 us
    ppermute x3, waiting for transfers between devices, on_device(): parts = [near] + [lax.ppermute(near, 'row', from_x(d)) for d in (1, 2, 3)]  10.7 us
    ppermute x3, starting transfers between devices, on_device(): parts = [near] + [lax.ppermute(near, 'row', from_x(d)) for d in (1, 2, 3)]  10.5 us
    all_to_all x1, starting transfers between devices, to_all(): lax.all_to_all(copies, axis, split_axis=0, concat_axis=0, axis_index_grou...  10.2 us
    all_to_all x1, waiting for transfers between devices, to_all(): lax.all_to_all(copies, axis, split_axis=0, concat_axis=0, axis_index_grou...  7.4 us
    pallas_call x1, Pallas kernels, product(): pl.pallas_call(product_kernel, out_shape=(jax.ShapeDtypeStruct((m, 256),...  6.93 us
    all_gather x1, waiting for transfers between devices, on_device(): whole = lax.all_gather(transfer, 'col', axis=0)  4.82 us
    pallas_call x1, Pallas kernels, split(): pl.pallas_call(split_kernel, out_shape=(shape, shape), grid=(m // STEP,),...  4.65 us
  transfers between devices with their start and end apart: 5, of which 4 were waited for; matrix products, arithmetic and copies ran while one was open for 4% of the time, Pallas kernels for 4%

profile of v6, /device:TPU:1, one launch (start us, length us, event | category | flops | bytes accessed | tf_op | source)
XLA Modules:
  0.0 103.4 jit_solution(8236891630507349134)
XLA Ops:
  7.2 0.0 all-gather.3.cloned.1.call-start
  7.2 0.7 all-gather.3.cloned.1.call-update
  7.9 0.1 pad.14.clone
  8.0 1.0 fusion.2
  9.0 1.4 %fusion = f32[2,128]{1,0:T(2,128)S(1)} fusion(f32[1024,128]{1,0:T(8,128)} %param.2, f32[1,1024]{1,0:T(1,128)S(1)} %add_multiply_fusion), kind=kOutput, calls=%fused_computation.6 | convolution fusion | flops 3145728 | bytes 529408 | tf_op jit(solution)/shard_map/dot_general | solution.py:136
  10.4 0.6 broadcast_in_dim.9
  11.1 10.2 %all-to-all-start = ((f32[16,2,256]{2,1,0:T(2,128)}), f32[16,2,256]{2,1,0:T(2,128)S(1)}, u32[]{:S(2)}, u32[]{:S(2)}) async-start(f32[16,2,256]{2,1,0:T(2,128)} %broadcast_in_dim.9), calls=%async_computation | async-start | bytes 65536 | tf_op jit(solution)/shard_map/all_to_all | solution.py:125
  21.2 0.1 pad.11.clone
  21.3 7.4 %all-to-all-done = f32[16,2,256]{2,1,0:T(2,128)S(1)} async-done(((f32[16,2,256]{2,1,0:T(2,128)}), f32[16,2,256]{2,1,0:T(2,128)S(1)}, u32[]{:S(2)}, u32[]{:S(2)}) %all-to-all-start) | async-done | bytes 32800 | tf_op jit(solution)/shard_map/all_to_all | solution.py:125
  28.8 0.9 maximum_maximum_fusion
  29.8 29.0 %all_to_all.10 = f32[8,88,256]{2,1,0:T(8,128)S(1)} all-to-all(f32[8,88,256]{2,1,0:T(8,128)S(1)} %broadcast_in_dim.21), channel_id=1, replica_groups={{0,64,128,192,256,320,384,448},{16,80,144,208,272,336,400,464},{32,96,1..., dimensions={0} | all-to-all | bytes 1441792 | tf_op jit(solution)/shard_map/all_to_all | solution.py:125
  58.9 3.1 %collective-permute-start.2 = (f32[536,256]{1,0:T(8,128)S(1)}, f32[536,256]{1,0:T(8,128)S(1)}, u32[]{:S(2)}, u32[]{:S(2)}) collective-permute-start(f32[536,256]{1,0:T(8,128)S(1)} %pad_maximum_fusion.e0), channel_id=1, source_target_pairs={{48,0},{0,16},{16,32},{32,48},{112,64},{64,80},{80,96},{96,112},{1... | collective-permute-start | bytes 1646600 | tf_op jit(solution)/shard_map/ppermute | solution.py:148
  62.0 4.4 %collective-permute-start.1 = (f32[536,256]{1,0:T(8,128)S(1)}, f32[536,256]{1,0:T(8,128)S(1)}, u32[]{:S(2)}, u32[]{:S(2)}) collective-permute-start(f32[536,256]{1,0:T(8,128)S(1)} %pad_maximum_fusion.e0), channel_id=1, source_target_pairs={{32,0},{48,16},{0,32},{16,48},{96,64},{112,80},{64,96},{80,112},{1... | collective-permute-start | bytes 1646600 | tf_op jit(solution)/shard_map/ppermute | solution.py:148
  66.4 3.1 %collective-permute-start = (f32[536,256]{1,0:T(8,128)S(1)}, f32[536,256]{1,0:T(8,128)S(1)}, u32[]{:S(2)}, u32[]{:S(2)}) collective-permute-start(f32[536,256]{1,0:T(8,128)S(1)} %pad_maximum_fusion.e0), channel_id=1, source_target_pairs={{16,0},{32,16},{48,32},{0,48},{80,64},{96,80},{112,96},{64,112},{1... | collective-permute-start | bytes 1646600 | tf_op jit(solution)/shard_map/ppermute | solution.py:148
  69.5 4.8 %all-gather.3.cloned.1.call-done = f32[16384,128]{1,0:T(8,128)} async-done(((f32[1024,128]{1,0:T(8,128)}), f32[16384,128]{1,0:T(8,128)}) %all-gather.3.cloned.1.call-update) | async-done | bytes 8388624 | tf_op jit(solution)/shard_map/all_gather | solution.py:133
  74.3 4.6 %shard_map.49 = (bf16[1024,2048]{1,0:T(8,128)(2,1)S(1)}, bf16[1024,2048]{1,0:T(8,128)(2,1)S(1)}) custom-call(f32[16,1024,128]{2,1,0:T(8,128)} %bitcast.12), custom_call_target="tpu_custom_call" | custom-call | tf_op jit(solution)/shard_map/pallas_call | solution.py:44
  78.9 0.0 collective-permute-done.2.e3
  78.9 7.9 %collective-permute-done.1.e2 = f32[536,256]{1,0:T(8,128)S(1)} collective-permute-done((f32[536,256]{1,0:T(8,128)S(1)}, f32[536,256]{1,0:T(8,128)S(1)}, u32[]{:S(2)}, u32[]{:S(2)}) %collective-permute-start.1) | collective-permute-done | bytes 548896 | tf_op jit(solution)/shard_map/ppermute | solution.py:148
  86.8 2.8 %collective-permute-done.e1 = f32[536,256]{1,0:T(8,128)S(1)} collective-permute-done((f32[536,256]{1,0:T(8,128)S(1)}, f32[536,256]{1,0:T(8,128)S(1)}, u32[]{:S(2)}, u32[]{:S(2)}) %collective-permute-start) | collective-permute-done | bytes 548896 | tf_op jit(solution)/shard_map/ppermute | solution.py:148
  89.6 6.9 %shard_map.50 = (f32[1024,256]{1,0:T(8,128)}, f32[2,256]{1,0:T(2,128)}, f32[2,1024]{1,0:T(2,128)}) custom-call(s32[1]{0:T(128)} %bitcast.place, bf16[1024,2048]{1,0:T(8,128)(2,1)S(1)} %get-tuple-element.5.th, bf16[1024,2048]{1,0:T(8,128)(2,1)S(1)} %get-tuple-element.6.tl, f32[536,256]{1,0:T(8,128)S(1)} %pad_maximum_fusion.e0, ...), custom_call_target="tpu_custom_call" | custom-call | tf_op jit(solution)/shard_map/pallas_call | solution.py:103
  (15 shorter events, 0.2 us)
Async XLA Ops:
  7.2 67.1 %all-gather.3.cloned.1.call-start = ((), (), s32[]{:S(2)}) async-start(), calls=%async_computation.2 | async-start | bytes 8912896 | tf_op jit(solution)/shard_map/all_gather | solution.py:133
  11.1 17.6 %all-to-all-start = ((f32[16,2,256]{2,1,0:T(2,128)}), f32[16,2,256]{2,1,0:T(2,128)S(1)}, u32[]{:S(2)}, u32[]{:S(2)}) async-start(f32[16,2,256]{2,1,0:T(2,128)} %broadcast_in_dim.9), calls=%async_computation | async-start | bytes 65536 | tf_op jit(solution)/shard_map/all_to_all | solution.py:125
  58.9 20.0 %collective-permute-start.2 = (f32[536,256]{1,0:T(8,128)S(1)}, f32[536,256]{1,0:T(8,128)S(1)}, u32[]{:S(2)}, u32[]{:S(2)}) collective-permute-start(f32[536,256]{1,0:T(8,128)S(1)} %pad_maximum_fusion.e0), channel_id=1, source_target_pairs={{48,0},{0,16},{16,32},{32,48},{112,64},{64,80},{80,96},{96,112},{1... | collective-permute-start | bytes 1646600 | tf_op jit(solution)/shard_map/ppermute | solution.py:148
  62.0 24.8 %collective-permute-start.1 = (f32[536,256]{1,0:T(8,128)S(1)}, f32[536,256]{1,0:T(8,128)S(1)}, u32[]{:S(2)}, u32[]{:S(2)}) collective-permute-start(f32[536,256]{1,0:T(8,128)S(1)} %pad_maximum_fusion.e0), channel_id=1, source_target_pairs={{32,0},{48,16},{0,32},{16,48},{96,64},{112,80},{64,96},{80,112},{1... | collective-permute-start | bytes 1646600 | tf_op jit(solution)/shard_map/ppermute | solution.py:148
  66.4 23.2 %collective-permute-start = (f32[536,256]{1,0:T(8,128)S(1)}, f32[536,256]{1,0:T(8,128)S(1)}, u32[]{:S(2)}, u32[]{:S(2)}) collective-permute-start(f32[536,256]{1,0:T(8,128)S(1)} %pad_maximum_fusion.e0), channel_id=1, source_target_pairs={{16,0},{32,16},{48,32},{0,48},{80,64},{96,80},{112,96},{64,112},{1... | collective-permute-start | bytes 1646600 | tf_op jit(solution)/shard_map/ppermute | solution.py:148
Sparse Core Ops, SparseCore 0:
  10.1 64.1 all-gather.2

commit v7 on v5

--- a/solution.py
+++ b/solution.py
@@ -9,7 +9,6 @@
 STEP = 256
 PAD = 16
 VMEM = 48 * 1024 * 1024
-DEPTH = 64 * NZ
 
 Z_GROUPS = [[NX * z + x for z in range(NZ)] for x in range(NX)]
 
@@ -34,27 +33,21 @@
     return lax.dot_general(left, right, (contract, ((), ())), preferred_element_type=jnp.float32)
 
 
-def product_kernel(place, t, e0, e1, e2, e3, main, rows, cols, eh, el, us, v):
+def product_kernel(place, t, e0, e1, e2, e3, both, main, rows, cols, eh, el, us, v):
     @pl.when(pl.program_id(0) == 0)
     def _():
-        v[...] = jnp.zeros_like(v)
-        upper = lax.broadcasted_iota(jnp.int32, (1, 128), 1) // 64
         for d, part in enumerate((e0, e1, e2, e3)):
             x = lax.rem(place[0] + d, NX)
-            here = upper == lax.rem(x, 2)
             for z in range(NZ):
                 at = pl.ds(pl.multiple_of((NX * z + x) * 64, 64), 64)
-                eh[at, :], el[at, :] = halves(part[z * 64 : (z + 1) * 64, :])
-                own = part[DEPTH + 16 + z : DEPTH + 17 + z, :]
-                both = jnp.concatenate([own[:, :128], own[:, 128:]], 0)
-                v[2 * z + x // 2] += jnp.where(here, both, 0.0)
+                eh[at, :], el[at, :] = halves(part[z])
         us[...] = jnp.zeros_like(us)
-        total = (e0[DEPTH : DEPTH + 16, :] + e1[DEPTH : DEPTH + 16, :]) + (
-            e2[DEPTH : DEPTH + 16, :] + e3[DEPTH : DEPTH + 16, :]
-        )
+        u = both[0, : 2 * NY]
+        for r in range(1, NX * NZ):
+            u += both[r, : 2 * NY]
         for n in range(2 * NY):
-            for w in range(2):
-                us[w : w + 1, n * 128 : (n + 1) * 128] = total[n : n + 1, w * 128 : (w + 1) * 128]
+            us[:2, n * 128 : (n + 1) * 128] = u[n]
+            v[n] = jnp.concatenate([both[2 * n + k, 2 * NY, :, :64] for k in range(2)], 1)
 
     blocks = [t[n] for n in range(2 * NY)]
     sums = []
@@ -73,7 +66,7 @@
     rows[...] = out[STEP : STEP + 2]
 
 
-def product(place, t, parts):
+def product(place, t, parts, both):
     blocks, m, wide = t.shape
     whole = lambda a: pl.BlockSpec(a.shape, lambda i, s: (0,) * a.ndim)
     depth = blocks * wide
@@ -88,7 +81,7 @@
             num_scalar_prefetch=1,
             grid=(m // STEP,),
             in_specs=[pl.BlockSpec((blocks, STEP, wide), lambda i, s: (0, i, 0))]
-            + [whole(a) for a in parts],
+            + [whole(a) for a in (*parts, both)],
             out_specs=[
                 pl.BlockSpec((STEP, 256), lambda i, s: (i, 0)),
                 pl.BlockSpec((2, 256), lambda i, s: (0, 0)),
@@ -98,7 +91,7 @@
             + [pltpu.VMEM((PAD, depth), jnp.float32), pltpu.VMEM((blocks, 2, wide), jnp.float32)],
         ),
         compiler_params=pltpu.CompilerParams(vmem_limit_bytes=VMEM),
-    )(place, t, *parts)
+    )(place, t, *parts, both)
 
 
 def to_all(value, axis, count, groups=None):
@@ -113,23 +106,22 @@
     m_local, s_local = transfer.shape[0], emissions.shape[1]
     whole = lax.all_gather(transfer, "col", axis=0)
 
+    near = to_all(emissions, "row", NZ, Z_GROUPS)
+    parts = [near] + [lax.ppermute(near, "row", from_x(d)) for d in (1, 2, 3)]
+
     receptor = check_weights(m_local * lax.axis_size("row"), row * m_local, m_local)
     u = jnp.dot(receptor, transfer, precision=highest, preferred_element_type=jnp.float32)
     scenario = check_weights(s_local * lax.axis_size("col"), col * s_local, s_local)
     v = jnp.einsum("js,ks->jk", scenario, emissions, precision=highest, preferred_element_type=jnp.float32)
-    both = to_all(jnp.concatenate([u, v, jnp.zeros_like(v)], 1), "col", 2 * NY)
-    v = both[:, :, 128:192].sum(0)
-    v = jnp.concatenate([v[:1], v[:1], v[1:], v[1:]], 1)
-    sent = jnp.concatenate(
-        [emissions, both[:, :, :128].reshape(2 * NY, s_local), v, jnp.zeros((7, s_local), jnp.float32)], 0
-    )
-
-    near = to_all(sent, "row", NZ, Z_GROUPS)
-    near = jnp.concatenate([near[:, :64].reshape(DEPTH, s_local), near[:, 64:80].sum(0), near[:, 80]], 0)
-    parts = [near] + [lax.ppermute(near, "row", from_x(d)) for d in (1, 2, 3)]
+    small = jnp.concatenate([u, v, jnp.zeros_like(v)], 1)
+    small, near = lax.optimization_barrier((small, near))
+    both = to_all(small, "col", 2 * NY)
+    both = jnp.concatenate([both[:, :, :128], both[:, :, 128:].sum(0)[None]], 0)
+    both, parts[1], parts[3] = lax.optimization_barrier((both, parts[1], parts[3]))
+    both = to_all(both, "row", NX * NZ)
 
     place = jnp.stack([x]).astype(jnp.int32)
-    return tuple(product(place, whole, parts))
+    return tuple(product(place, whole, parts, both))
 
 
 def solution(mesh):

time: 107 us -> 104 us (0.972); the launches traced: 105 us -> 104 us
  blocking collectives: 29 us -> 15.6 us
  waiting for transfers between devices: 28.2 us -> 34.1 us
  starting transfers between devices: 20.7 us -> 25.8 us
  local copies, waits for them, and re-layouts: 0.9 us -> 2.71 us
    all_to_all x1, blocking collectives: 29 us -> 15.6 us  [to_all(): lax.all_to_all(copies, axis, split_axis=0, concat_axis=0, axis_index_grou...]
    all_to_all x1 -> x2, waiting for transfers between devices: 7.4 us -> 15.4 us  [to_all(): lax.all_to_all(copies, axis, split_axis=0, concat_axis=0, axis_index_grou...]
    all_to_all x1 -> x2, starting transfers between devices: 10.2 us -> 14.8 us  [to_all(): lax.all_to_all(copies, axis, split_axis=0, concat_axis=0, axis_index_grou...]
    ppermute x3, waiting for transfers between devices: 20.1 us -> 18 us  [on_device(): parts = [near] + [lax.ppermute(near, 'row', from_x(d)) for d in (1, 2, 3)]]
    broadcast_in_dim x2 -> x3, local copies, waits for them, and re-layouts: 0.68 us -> 2.64 us  [to_all(): copies = jnp.broadcast_to(value[None], (count,) + value.shape)]
  transfers between devices with their start and end apart: 5 -> 6, of which waited for: 4 -> 2; matrix products, arithmetic and copies ran while one was open for 4% -> 5% of each run, Pallas kernels for 0% -> 0%
where the time goes in v7:
time: 104 us
  waiting for transfers between devices  34.1 us (33%)
  starting transfers between devices  25.8 us (25%)
  blocking collectives  15.6 us (15%)
  between operations  14.1 us (14%)
  Pallas kernels  8.69 us (8%)
  local copies, waits for them, and re-layouts  2.71 us (3%)
  matrix products  2.41 us (2%)
    ppermute x3, waiting for transfers between devices, on_device(): parts = [near] + [lax.ppermute(near, 'row', from_x(d)) for d in (1, 2, 3)]  18 us
    all_to_all x1, blocking collectives, to_all(): lax.all_to_all(copies, axis, split_axis=0, concat_axis=0, axis_index_grou...  15.6 us
    all_to_all x2, waiting for transfers between devices, to_all(): lax.all_to_all(copies, axis, split_axis=0, concat_axis=0, axis_index_grou...  15.4 us
    all_to_all x2, starting transfers between devices, to_all(): lax.all_to_all(copies, axis, split_axis=0, concat_axis=0, axis_index_grou...  14.8 us
    ppermute x3, starting transfers between devices, on_device(): parts = [near] + [lax.ppermute(near, 'row', from_x(d)) for d in (1, 2, 3)]  11 us
    pallas_call x1, Pallas kernels, product(): pl.pallas_call(product_kernel, out_shape=(jax.ShapeDtypeStruct((m, 256),...  8.69 us
    broadcast_in_dim x3, local copies, waits for them, and re-layouts, to_all(): copies = jnp.broadcast_to(value[None], (count,) + value.shape)  2.64 us
  transfers between devices with their start and end apart: 6, of which 2 were waited for; matrix products, arithmetic and copies ran while one was open for 5% of the time, Pallas kernels for 0%

profile of v7, /device:TPU:1, one launch (start us, length us, event | category | flops | bytes accessed | tf_op | source)
XLA Modules:
  0.0 103.5 jit_solution(358287276624289162)
XLA Ops:
  7.2 0.0 all-gather.3.cloned.1.call-start
  7.2 0.7 all-gather.3.cloned.1.call-update
  7.9 1.7 %broadcast_in_dim.10 = f32[8,64,256]{2,1,0:T(8,128)} broadcast(f32[64,256]{1,0:T(8,128)} %param.3), dimensions={1,2} | broadcast | bytes 589824 | tf_op jit(solution)/shard_map/broadcast_in_dim | solution.py:98
  9.6 10.9 %all-to-all-start = ((f32[8,64,256]{2,1,0:T(8,128)}), f32[8,64,256]{2,1,0:T(8,128)S(1)}, u32[]{:S(2)}, u32[]{:S(2)}) async-start(f32[8,64,256]{2,1,0:T(8,128)} %broadcast_in_dim.10), calls=%async_computation | async-start | bytes 1048576 | tf_op jit(solution)/shard_map/all_to_all | solution.py:99
  20.4 0.1 pad.6.clone
  20.5 1.0 fusion.2
  21.5 1.4 %fusion = f32[2,128]{1,0:T(2,128)S(1)} fusion(f32[1024,128]{1,0:T(8,128)} %param.2, f32[1,1024]{1,0:T(1,128)S(1)} %add_multiply_fusion), kind=kOutput, calls=%fused_computation.2 | convolution fusion | flops 3145728 | bytes 529408 | tf_op jit(solution)/shard_map/dot_general | solution.py:113
  23.0 15.4 %all-to-all-done.e0 = f32[8,64,256]{2,1,0:T(8,128)S(1)} async-done(((f32[8,64,256]{2,1,0:T(8,128)}), f32[8,64,256]{2,1,0:T(8,128)S(1)}, u32[]{:S(2)}, u32[]{:S(2)}) %all-to-all-start) | async-done | bytes 524320 | tf_op jit(solution)/shard_map/all_to_all | solution.py:99
  38.4 3.1 %collective-permute-start.1 = (f32[8,64,256]{2,1,0:T(8,128)S(1)}, f32[8,64,256]{2,1,0:T(8,128)S(1)}, u32[]{:S(2)}, u32[]{:S(2)}) collective-permute-start(f32[8,64,256]{2,1,0:T(8,128)S(1)} %all-to-all-done.e0), channel_id=1, source_target_pairs={{48,0},{0,16},{16,32},{32,48},{112,64},{64,80},{80,96},{96,112},{1... | collective-permute-start | bytes 1572872 | tf_op jit(solution)/shard_map/ppermute | solution.py:110
  41.5 3.4 %collective-permute-start = (f32[8,64,256]{2,1,0:T(8,128)S(1)}, f32[8,64,256]{2,1,0:T(8,128)S(1)}, u32[]{:S(2)}, u32[]{:S(2)}) collective-permute-start(f32[8,64,256]{2,1,0:T(8,128)S(1)} %all-to-all-done.e0), channel_id=1, source_target_pairs={{16,0},{32,16},{48,32},{0,48},{80,64},{96,80},{112,96},{64,112},{1... | collective-permute-start | bytes 1572872 | tf_op jit(solution)/shard_map/ppermute | solution.py:110
  44.9 15.6 %all_to_all.15 = f32[16,2,256]{2,1,0:T(2,128)S(1)} all-to-all(f32[16,2,256]{2,1,0:T(2,128)S(1)} %broadcast_in_dim.12), channel_id=1, replica_groups=mesh['row'=32,'col'=16] {'col'}, dimensions={0} | all-to-all | bytes 65536 | tf_op jit(solution)/shard_map/all_to_all | solution.py:99
  60.6 0.0 collective-permute-done.1.e3
  60.6 0.0 collective-permute-done.e1
  60.6 0.9 broadcast_in_dim.28
  61.6 3.9 %all-to-all-start.2 = ((f32[32,17,2,128]{3,2,1,0:T(2,128)}), f32[32,17,2,128]{3,2,1,0:T(2,128)S(1)}, u32[]{:S(2)}, u32[]{:S(2)}) async-start(f32[32,17,2,128]{3,2,1,0:T(2,128)} %broadcast_in_dim.28), calls=%async_computation.2 | async-start | bytes 1114112 | tf_op jit(solution)/shard_map/all_to_all | solution.py:99
  65.5 4.5 %collective-permute-start.2 = (f32[8,64,256]{2,1,0:T(8,128)S(1)}, f32[8,64,256]{2,1,0:T(8,128)S(1)}, u32[]{:S(2)}, u32[]{:S(2)}) collective-permute-start(f32[8,64,256]{2,1,0:T(8,128)S(1)} %all-to-all-done.e0), channel_id=1, source_target_pairs={{32,0},{48,16},{0,32},{16,48},{96,64},{112,80},{64,96},{80,112},{1... | collective-permute-start | bytes 1572872 | tf_op jit(solution)/shard_map/ppermute | solution.py:110
  70.0 17.9 %collective-permute-done.2.e2 = f32[8,64,256]{2,1,0:T(8,128)S(1)} collective-permute-done((f32[8,64,256]{2,1,0:T(8,128)S(1)}, f32[8,64,256]{2,1,0:T(8,128)S(1)}, u32[]{:S(2)}, u32[]{:S(2)}) %collective-permute-start.2) | collective-permute-done | bytes 524320 | tf_op jit(solution)/shard_map/ppermute | solution.py:110
  88.0 0.0 all-to-all-done.2.both
  88.0 0.0 all-gather.3.cloned.1.call-done
  88.0 8.7 %shard_map.49 = (f32[1024,256]{1,0:T(8,128)}, f32[2,256]{1,0:T(2,128)}, f32[2,1024]{1,0:T(2,128)}) custom-call(s32[1]{0:T(128)} %bitcast.place, f32[16,1024,128]{2,1,0:T(8,128)} %bitcast.5, f32[8,64,256]{2,1,0:T(8,128)S(1)} %all-to-all-done.e0, f32[8,64,256]{2,1,0:T(8,128)S(1)} %collective-permute-done.e1, f32[8,64,256]{2,1,0:T(8,128)S(1)} %collective-permute-done.2.e2, ...), custom_call_target="tpu_custom_call" | custom-call | tf_op jit(solution)/shard_map/pallas_call | solution.py:73
  (7 shorter events, 0.1 us)
Async XLA Ops:
  7.2 80.8 %all-gather.3.cloned.1.call-start = ((), (), s32[]{:S(2)}) async-start(), calls=%async_computation.3 | async-start | bytes 8912896 | tf_op jit(solution)/shard_map/all_gather | solution.py:107
  9.6 28.8 %all-to-all-start = ((f32[8,64,256]{2,1,0:T(8,128)}), f32[8,64,256]{2,1,0:T(8,128)S(1)}, u32[]{:S(2)}, u32[]{:S(2)}) async-start(f32[8,64,256]{2,1,0:T(8,128)} %broadcast_in_dim.10), calls=%async_computation | async-start | bytes 1048576 | tf_op jit(solution)/shard_map/all_to_all | solution.py:99
  38.4 22.2 %collective-permute-start.1 = (f32[8,64,256]{2,1,0:T(8,128)S(1)}, f32[8,64,256]{2,1,0:T(8,128)S(1)}, u32[]{:S(2)}, u32[]{:S(2)}) collective-permute-start(f32[8,64,256]{2,1,0:T(8,128)S(1)} %all-to-all-done.e0), channel_id=1, source_target_pairs={{48,0},{0,16},{16,32},{32,48},{112,64},{64,80},{80,96},{96,112},{1... | collective-permute-start | bytes 1572872 | tf_op jit(solution)/shard_map/ppermute | solution.py:110
  41.5 19.1 %collective-permute-start = (f32[8,64,256]{2,1,0:T(8,128)S(1)}, f32[8,64,256]{2,1,0:T(8,128)S(1)}, u32[]{:S(2)}, u32[]{:S(2)}) collective-permute-start(f32[8,64,256]{2,1,0:T(8,128)S(1)} %all-to-all-done.e0), channel_id=1, source_target_pairs={{16,0},{32,16},{48,32},{0,48},{80,64},{96,80},{112,96},{64,112},{1... | collective-permute-start | bytes 1572872 | tf_op jit(solution)/shard_map/ppermute | solution.py:110
  61.6 26.4 %all-to-all-start.2 = ((f32[32,17,2,128]{3,2,1,0:T(2,128)}), f32[32,17,2,128]{3,2,1,0:T(2,128)S(1)}, u32[]{:S(2)}, u32[]{:S(2)}) async-start(f32[32,17,2,128]{3,2,1,0:T(2,128)} %broadcast_in_dim.28), calls=%async_computation.2 | async-start | bytes 1114112 | tf_op jit(solution)/shard_map/all_to_all | solution.py:99
  65.5 22.5 %collective-permute-start.2 = (f32[8,64,256]{2,1,0:T(8,128)S(1)}, f32[8,64,256]{2,1,0:T(8,128)S(1)}, u32[]{:S(2)}, u32[]{:S(2)}) collective-permute-start(f32[8,64,256]{2,1,0:T(8,128)S(1)} %all-to-all-done.e0), channel_id=1, source_target_pairs={{32,0},{48,16},{0,32},{16,48},{96,64},{112,80},{64,96},{80,112},{1... | collective-permute-start | bytes 1572872 | tf_op jit(solution)/shard_map/ppermute | solution.py:110
Sparse Core Ops, SparseCore 0:
  10.1 64.8 all-gather.2

commit v8 on v7

--- a/solution.py
+++ b/solution.py
@@ -33,14 +33,14 @@
     return lax.dot_general(left, right, (contract, ((), ())), preferred_element_type=jnp.float32)
 
 
-def product_kernel(place, t, e0, e1, e2, e3, both, main, rows, cols, eh, el, us, v):
+def product_kernel(place, t, e0, e1, e2, e2_more, e3, both, main, rows, cols, eh, el, us, v):
     @pl.when(pl.program_id(0) == 0)
     def _():
-        for d, part in enumerate((e0, e1, e2, e3)):
+        for d, part in enumerate(((e0,), (e1,), (e2, e2_more), (e3,))):
             x = lax.rem(place[0] + d, NX)
             for z in range(NZ):
                 at = pl.ds(pl.multiple_of((NX * z + x) * 64, 64), 64)
-                eh[at, :], el[at, :] = halves(part[z])
+                eh[at, :], el[at, :] = halves(part[z * len(part) // NZ][z % (NZ // len(part))])
         us[...] = jnp.zeros_like(us)
         u = both[0, : 2 * NY]
         for r in range(1, NX * NZ):
@@ -107,7 +107,7 @@
     whole = lax.all_gather(transfer, "col", axis=0)
 
     near = to_all(emissions, "row", NZ, Z_GROUPS)
-    parts = [near] + [lax.ppermute(near, "row", from_x(d)) for d in (1, 2, 3)]
+    after, before = [lax.ppermute(near, "row", from_x(d)) for d in (1, 3)]
 
     receptor = check_weights(m_local * lax.axis_size("row"), row * m_local, m_local)
     u = jnp.dot(receptor, transfer, precision=highest, preferred_element_type=jnp.float32)
@@ -117,8 +117,14 @@
     small, near = lax.optimization_barrier((small, near))
     both = to_all(small, "col", 2 * NY)
     both = jnp.concatenate([both[:, :, :128], both[:, :, 128:].sum(0)[None]], 0)
-    both, parts[1], parts[3] = lax.optimization_barrier((both, parts[1], parts[3]))
+    both, after, before = lax.optimization_barrier((both, after, before))
     both = to_all(both, "row", NX * NZ)
+
+    two = [
+        lax.ppermute(after[: NZ // 2], "row", from_x(1)),
+        lax.ppermute(before[NZ // 2 :], "row", from_x(3)),
+    ]
+    parts = [near, after, *two, before]
 
     place = jnp.stack([x]).astype(jnp.int32)
     return tuple(product(place, whole, parts, both))

time: 104 us -> 98.9 us (0.951)
  waiting for transfers between devices: 34.1 us -> 26.8 us
  starting transfers between devices: 25.8 us -> 27.8 us
    ppermute x3 -> x4, waiting for transfers between devices: 18 us -> 8.45 us  [the longest x1 8.27 us: on_device(): lax.ppermute(before[NZ // 2:], 'row', from_x(3))]
    all_to_all x2, waiting for transfers between devices: 15.4 us -> 17.7 us  [to_all(): lax.all_to_all(copies, axis, split_axis=0, concat_axis=0, axis_index_grou...]
    ppermute x3 -> x4, starting transfers between devices: 11 us -> 13 us  [the longest x2 6.48 us: on_device(): after, before = [lax.ppermute(near, 'row', from_x(d)) for d in (1, 3)]]
  transfers between devices with their start and end apart: 6 -> 7, of which waited for: 2 -> 4; matrix products, arithmetic and copies ran while one was open for 5% -> 5% of each run, Pallas kernels for 0% -> 0%
where the time goes in v8:
time: 98.9 us; the launch traced here: 98.3 us
  starting transfers between devices  27.8 us (28%)
  waiting for transfers between devices  26.8 us (27%)
  blocking collectives  15.6 us (16%)
  between operations  14.1 us (14%)
  Pallas kernels  8.68 us (9%)
  local copies, waits for them, and re-layouts  2.75 us (3%)
  matrix products  2.41 us (2%)
    all_to_all x2, waiting for transfers between devices, to_all(): lax.all_to_all(copies, axis, split_axis=0, concat_axis=0, axis_index_grou...  17.7 us
    all_to_all x1, blocking collectives, to_all(): lax.all_to_all(copies, axis, split_axis=0, concat_axis=0, axis_index_grou...  15.6 us
    all_to_all x2, starting transfers between devices, to_all(): lax.all_to_all(copies, axis, split_axis=0, concat_axis=0, axis_index_grou...  14.8 us
    pallas_call x1, Pallas kernels, product(): pl.pallas_call(product_kernel, out_shape=(jax.ShapeDtypeStruct((m, 256),...  8.68 us
    ppermute x1, waiting for transfers between devices, on_device(): lax.ppermute(before[NZ // 2:], 'row', from_x(3))  8.27 us
    ppermute x2, starting transfers between devices, on_device(): after, before = [lax.ppermute(near, 'row', from_x(d)) for d in (1, 3)]  6.48 us
    ppermute x1, starting transfers between devices, on_device(): lax.ppermute(after[:NZ // 2], 'row', from_x(1))  3.47 us
    ppermute x1, starting transfers between devices, on_device(): lax.ppermute(before[NZ // 2:], 'row', from_x(3))  3.03 us
  transfers between devices with their start and end apart: 7, of which 4 were waited for; matrix products, arithmetic and copies ran while one was open for 5% of the time, Pallas kernels for 0%

profile of v8, /device:TPU:1, one launch (start us, length us, event | category | flops | bytes accessed | tf_op | source)
XLA Modules:
  0.0 98.3 jit_solution(1813261511936044972)
XLA Ops:
  7.2 0.0 all-gather.3.cloned.1.call-start
  7.2 0.7 all-gather.3.cloned.1.call-update
  7.9 1.7 %broadcast_in_dim.11 = f32[8,64,256]{2,1,0:T(8,128)} broadcast(f32[64,256]{1,0:T(8,128)} %param.3), dimensions={1,2} | broadcast | bytes 589824 | tf_op jit(solution)/shard_map/broadcast_in_dim | solution.py:98
  9.6 10.9 %all-to-all-start = ((f32[8,64,256]{2,1,0:T(8,128)}), f32[8,64,256]{2,1,0:T(8,128)S(1)}, u32[]{:S(2)}, u32[]{:S(2)}) async-start(f32[8,64,256]{2,1,0:T(8,128)} %broadcast_in_dim.11), calls=%async_computation | async-start | bytes 1048576 | tf_op jit(solution)/shard_map/all_to_all | solution.py:99
  20.4 0.1 pad.6.clone
  20.5 1.0 fusion.2
  21.5 1.4 %fusion = f32[2,128]{1,0:T(2,128)S(1)} fusion(f32[1024,128]{1,0:T(8,128)} %param.2, f32[1,1024]{1,0:T(1,128)S(1)} %add_multiply_fusion), kind=kOutput, calls=%fused_computation.2 | convolution fusion | flops 3145728 | bytes 529408 | tf_op jit(solution)/shard_map/dot_general | solution.py:113
  23.0 15.4 %all-to-all-done.e0 = f32[8,64,256]{2,1,0:T(8,128)S(1)} async-done(((f32[8,64,256]{2,1,0:T(8,128)}), f32[8,64,256]{2,1,0:T(8,128)S(1)}, u32[]{:S(2)}, u32[]{:S(2)}) %all-to-all-start) | async-done | bytes 524320 | tf_op jit(solution)/shard_map/all_to_all | solution.py:99
  38.4 3.1 %collective-permute-start.1 = (f32[8,64,256]{2,1,0:T(8,128)S(1)}, f32[8,64,256]{2,1,0:T(8,128)S(1)}, u32[]{:S(2)}, u32[]{:S(2)}) collective-permute-start(f32[8,64,256]{2,1,0:T(8,128)S(1)} %all-to-all-done.e0), channel_id=1, source_target_pairs={{48,0},{0,16},{16,32},{32,48},{112,64},{64,80},{80,96},{96,112},{1... | collective-permute-start | bytes 1572872 | tf_op jit(solution)/shard_map/ppermute | solution.py:110
  41.5 3.4 %collective-permute-start = (f32[8,64,256]{2,1,0:T(8,128)S(1)}, f32[8,64,256]{2,1,0:T(8,128)S(1)}, u32[]{:S(2)}, u32[]{:S(2)}) collective-permute-start(f32[8,64,256]{2,1,0:T(8,128)S(1)} %all-to-all-done.e0), channel_id=1, source_target_pairs={{16,0},{32,16},{48,32},{0,48},{80,64},{96,80},{112,96},{64,112},{1... | collective-permute-start | bytes 1572872 | tf_op jit(solution)/shard_map/ppermute | solution.py:110
  44.9 15.6 %all_to_all.15 = f32[16,2,256]{2,1,0:T(2,128)S(1)} all-to-all(f32[16,2,256]{2,1,0:T(2,128)S(1)} %broadcast_in_dim.12), channel_id=1, replica_groups=mesh['row'=32,'col'=16] {'col'}, dimensions={0} | all-to-all | bytes 65536 | tf_op jit(solution)/shard_map/all_to_all | solution.py:99
  60.6 0.0 collective-permute-done.1.e3
  60.6 0.0 collective-permute-done.e1
  60.6 0.9 broadcast_in_dim.28
  61.6 3.9 %all-to-all-start.2 = ((f32[32,17,2,128]{3,2,1,0:T(2,128)}), f32[32,17,2,128]{3,2,1,0:T(2,128)S(1)}, u32[]{:S(2)}, u32[]{:S(2)}) async-start(f32[32,17,2,128]{3,2,1,0:T(2,128)} %broadcast_in_dim.28), calls=%async_computation.2 | async-start | bytes 1114112 | tf_op jit(solution)/shard_map/all_to_all | solution.py:99
  65.5 3.0 %collective-permute-start.3 = (f32[4,64,256]{2,1,0:T(8,128)S(1)}, f32[4,64,256]{2,1,0:T(8,128)S(1)}, u32[]{:S(2)}, u32[]{:S(2)}) collective-permute-start(f32[4,64,256]{2,1,0:T(8,128)S(1)} %slice.15), channel_id=1, source_target_pairs={{48,0},{0,16},{16,32},{32,48},{112,64},{64,80},{80,96},{96,112},{1... | collective-permute-start | bytes 786440 | tf_op jit(solution)/shard_map/ppermute | solution.py:125
  68.6 3.5 %collective-permute-start.2 = (f32[4,64,256]{2,1,0:T(8,128)S(1)}, f32[4,64,256]{2,1,0:T(8,128)S(1)}, u32[]{:S(2)}, u32[]{:S(2)}) collective-permute-start(f32[4,64,256]{2,1,0:T(8,128)S(1)} %slice.14), channel_id=1, source_target_pairs={{16,0},{32,16},{48,32},{0,48},{80,64},{96,80},{112,96},{64,112},{1... | collective-permute-start | bytes 786440 | tf_op jit(solution)/shard_map/ppermute | solution.py:124
  72.0 8.3 %collective-permute-done.3.e2_more = f32[4,64,256]{2,1,0:T(8,128)S(1)} collective-permute-done((f32[4,64,256]{2,1,0:T(8,128)S(1)}, f32[4,64,256]{2,1,0:T(8,128)S(1)}, u32[]{:S(2)}, u32[]{:S(2)}) %collective-permute-start.3) | collective-permute-done | bytes 262176 | tf_op jit(solution)/shard_map/ppermute | solution.py:125
  80.3 0.2 collective-permute-done.2.e2
  80.5 2.2 %all-to-all-done.2.both = f32[32,17,2,128]{3,2,1,0:T(2,128)S(1)} async-done(((f32[32,17,2,128]{3,2,1,0:T(2,128)}), f32[32,17,2,128]{3,2,1,0:T(2,128)S(1)}, u32[]{:S(2)}, u32[]{:S(2)}) %all-to-all-start.2) | async-done | bytes 557088 | tf_op jit(solution)/shard_map/all_to_all | solution.py:99
  82.7 0.0 all-gather.3.cloned.1.call-done
  82.7 8.7 %shard_map.49 = (f32[1024,256]{1,0:T(8,128)}, f32[2,256]{1,0:T(2,128)}, f32[2,1024]{1,0:T(2,128)}) custom-call(s32[1]{0:T(128)} %bitcast.place, f32[16,1024,128]{2,1,0:T(8,128)} %bitcast.5, f32[8,64,256]{2,1,0:T(8,128)S(1)} %all-to-all-done.e0, f32[8,64,256]{2,1,0:T(8,128)S(1)} %collective-permute-done.e1, f32[4,64,256]{2,1,0:T(8,128)S(1)} %collective-permute-done.2.e2, ...), custom_call_target="tpu_custom_call" | custom-call | tf_op jit(solution)/shard_map/pallas_call | solution.py:73
  (9 shorter events, 0.1 us)
Async XLA Ops:
  7.2 75.6 %all-gather.3.cloned.1.call-start = ((), (), s32[]{:S(2)}) async-start(), calls=%async_computation.3 | async-start | bytes 8912896 | tf_op jit(solution)/shard_map/all_gather | solution.py:107
  9.6 28.8 %all-to-all-start = ((f32[8,64,256]{2,1,0:T(8,128)}), f32[8,64,256]{2,1,0:T(8,128)S(1)}, u32[]{:S(2)}, u32[]{:S(2)}) async-start(f32[8,64,256]{2,1,0:T(8,128)} %broadcast_in_dim.11), calls=%async_computation | async-start | bytes 1048576 | tf_op jit(solution)/shard_map/all_to_all | solution.py:99
  38.4 22.2 %collective-permute-start.1 = (f32[8,64,256]{2,1,0:T(8,128)S(1)}, f32[8,64,256]{2,1,0:T(8,128)S(1)}, u32[]{:S(2)}, u32[]{:S(2)}) collective-permute-start(f32[8,64,256]{2,1,0:T(8,128)S(1)} %all-to-all-done.e0), channel_id=1, source_target_pairs={{48,0},{0,16},{16,32},{32,48},{112,64},{64,80},{80,96},{96,112},{1... | collective-permute-start | bytes 1572872 | tf_op jit(solution)/shard_map/ppermute | solution.py:110
  41.5 19.1 %collective-permute-start = (f32[8,64,256]{2,1,0:T(8,128)S(1)}, f32[8,64,256]{2,1,0:T(8,128)S(1)}, u32[]{:S(2)}, u32[]{:S(2)}) collective-permute-start(f32[8,64,256]{2,1,0:T(8,128)S(1)} %all-to-all-done.e0), channel_id=1, source_target_pairs={{16,0},{32,16},{48,32},{0,48},{80,64},{96,80},{112,96},{64,112},{1... | collective-permute-start | bytes 1572872 | tf_op jit(solution)/shard_map/ppermute | solution.py:110
  61.6 21.2 %all-to-all-start.2 = ((f32[32,17,2,128]{3,2,1,0:T(2,128)}), f32[32,17,2,128]{3,2,1,0:T(2,128)S(1)}, u32[]{:S(2)}, u32[]{:S(2)}) async-start(f32[32,17,2,128]{3,2,1,0:T(2,128)} %broadcast_in_dim.28), calls=%async_computation.2 | async-start | bytes 1114112 | tf_op jit(solution)/shard_map/all_to_all | solution.py:99
  65.5 14.8 %collective-permute-start.3 = (f32[4,64,256]{2,1,0:T(8,128)S(1)}, f32[4,64,256]{2,1,0:T(8,128)S(1)}, u32[]{:S(2)}, u32[]{:S(2)}) collective-permute-start(f32[4,64,256]{2,1,0:T(8,128)S(1)} %slice.15), channel_id=1, source_target_pairs={{48,0},{0,16},{16,32},{32,48},{112,64},{64,80},{80,96},{96,112},{1... | collective-permute-start | bytes 786440 | tf_op jit(solution)/shard_map/ppermute | solution.py:125
  68.6 11.9 %collective-permute-start.2 = (f32[4,64,256]{2,1,0:T(8,128)S(1)}, f32[4,64,256]{2,1,0:T(8,128)S(1)}, u32[]{:S(2)}, u32[]{:S(2)}) collective-permute-start(f32[4,64,256]{2,1,0:T(8,128)S(1)} %slice.14), channel_id=1, source_target_pairs={{16,0},{32,16},{48,32},{0,48},{80,64},{96,80},{112,96},{64,112},{1... | collective-permute-start | bytes 786440 | tf_op jit(solution)/shard_map/ppermute | solution.py:124
Sparse Core Ops, SparseCore 0:
  10.1 64.8 all-gather.2

commit v9 on v8

--- a/solution.py
+++ b/solution.py
@@ -42,12 +42,12 @@
                 at = pl.ds(pl.multiple_of((NX * z + x) * 64, 64), 64)
                 eh[at, :], el[at, :] = halves(part[z * len(part) // NZ][z % (NZ // len(part))])
         us[...] = jnp.zeros_like(us)
-        u = both[0, : 2 * NY]
+        u = both[0, : 4 * NY]
         for r in range(1, NX * NZ):
-            u += both[r, : 2 * NY]
+            u += both[r, : 4 * NY]
         for n in range(2 * NY):
-            us[:2, n * 128 : (n + 1) * 128] = u[n]
-            v[n] = jnp.concatenate([both[2 * n + k, 2 * NY, :, :64] for k in range(2)], 1)
+            us[:2, n * 128 : (n + 1) * 128] = u[2 * n : 2 * n + 2]
+            v[n] = jnp.concatenate([both[2 * n + k, 4 * NY :, :64] for k in range(2)], 1)
 
     blocks = [t[n] for n in range(2 * NY)]
     sums = []
@@ -118,7 +118,7 @@
     both = to_all(small, "col", 2 * NY)
     both = jnp.concatenate([both[:, :, :128], both[:, :, 128:].sum(0)[None]], 0)
     both, after, before = lax.optimization_barrier((both, after, before))
-    both = to_all(both, "row", NX * NZ)
+    both = to_all(both.reshape(-1, both.shape[-1]), "row", NX * NZ)
 
     two = [
         lax.ppermute(after[: NZ // 2], "row", from_x(1)),

time: 98.9 us -> 101 us (1.021)
  waiting for transfers between devices: 26.8 us -> 28.6 us
    ppermute x1, waiting for transfers between devices: 0.17 us -> 1.34 us  [on_device(): lax.ppermute(after[:NZ // 2], 'row', from_x(1))]
    broadcast_in_dim x3 -> x4, local copies, waits for them, and re-layouts: 2.64 us -> 2.58 us  [to_all(): copies = jnp.broadcast_to(value[None], (count,) + value.shape)]
where the time goes in v9:
time: 101 us; the launch traced here: 100 us
  waiting for transfers between devices  28.6 us (28%)
  starting transfers between devices  27.8 us (28%)
  blocking collectives  15.6 us (15%)
  between operations  14.1 us (14%)
  Pallas kernels  8.62 us (9%)
  local copies, waits for them, and re-layouts  2.7 us (3%)
  matrix products  2.41 us (2%)
    all_to_all x2, waiting for transfers between devices, to_all(): lax.all_to_all(copies, axis, split_axis=0, concat_axis=0, axis_index_grou...  18.6 us
    all_to_all x1, blocking collectives, to_all(): lax.all_to_all(copies, axis, split_axis=0, concat_axis=0, axis_index_grou...  15.6 us
    all_to_all x2, starting transfers between devices, to_all(): lax.all_to_all(copies, axis, split_axis=0, concat_axis=0, axis_index_grou...  14.8 us
    pallas_call x1, Pallas kernels, product(): pl.pallas_call(product_kernel, out_shape=(jax.ShapeDtypeStruct((m, 256),...  8.62 us
    ppermute x1, waiting for transfers between devices, on_device(): lax.ppermute(before[NZ // 2:], 'row', from_x(3))  8 us
    ppermute x2, starting transfers between devices, on_device(): after, before = [lax.ppermute(near, 'row', from_x(d)) for d in (1, 3)]  6.48 us
    ppermute x1, starting transfers between devices, on_device(): lax.ppermute(after[:NZ // 2], 'row', from_x(1))  3.47 us
    ppermute x1, starting transfers between devices, on_device(): lax.ppermute(before[NZ // 2:], 'row', from_x(3))  3.03 us
  transfers between devices with their start and end apart: 7, of which 4 were waited for; matrix products, arithmetic and copies ran while one was open for 5% of the time, Pallas kernels for 0%

profile of v9, /device:TPU:1, one launch (start us, length us, event | category | flops | bytes accessed | tf_op | source)
XLA Modules:
  0.0 100.0 jit_solution(9076829921954737063)
XLA Ops:
  7.2 0.0 all-gather.3.cloned.1.call-start
  7.2 0.7 all-gather.3.cloned.1.call-update
  7.9 1.7 %broadcast_in_dim.26 = f32[8,64,256]{2,1,0:T(8,128)} broadcast(f32[64,256]{1,0:T(8,128)} %param.3), dimensions={1,2} | broadcast | bytes 589824 | tf_op jit(solution)/shard_map/broadcast_in_dim | solution.py:98
  9.6 10.9 %all-to-all-start = ((f32[8,64,256]{2,1,0:T(8,128)}), f32[8,64,256]{2,1,0:T(8,128)S(1)}, u32[]{:S(2)}, u32[]{:S(2)}) async-start(f32[8,64,256]{2,1,0:T(8,128)} %broadcast_in_dim.26), calls=%async_computation | async-start | bytes 1048576 | tf_op jit(solution)/shard_map/all_to_all | solution.py:99
  20.4 0.1 pad.6.clone
  20.5 1.0 fusion.2
  21.5 1.4 %fusion = f32[2,128]{1,0:T(2,128)S(1)} fusion(f32[1024,128]{1,0:T(8,128)} %param.2, f32[1,1024]{1,0:T(1,128)S(1)} %add_multiply_fusion), kind=kOutput, calls=%fused_computation.2 | convolution fusion | flops 3145728 | bytes 529408 | tf_op jit(solution)/shard_map/dot_general | solution.py:113
  23.0 15.4 %all-to-all-done.e0 = f32[8,64,256]{2,1,0:T(8,128)S(1)} async-done(((f32[8,64,256]{2,1,0:T(8,128)}), f32[8,64,256]{2,1,0:T(8,128)S(1)}, u32[]{:S(2)}, u32[]{:S(2)}) %all-to-all-start) | async-done | bytes 524320 | tf_op jit(solution)/shard_map/all_to_all | solution.py:99
  38.4 3.1 %collective-permute-start.1 = (f32[8,64,256]{2,1,0:T(8,128)S(1)}, f32[8,64,256]{2,1,0:T(8,128)S(1)}, u32[]{:S(2)}, u32[]{:S(2)}) collective-permute-start(f32[8,64,256]{2,1,0:T(8,128)S(1)} %all-to-all-done.e0), channel_id=1, source_target_pairs={{48,0},{0,16},{16,32},{32,48},{112,64},{64,80},{80,96},{96,112},{1... | collective-permute-start | bytes 1572872 | tf_op jit(solution)/shard_map/ppermute | solution.py:110
  41.5 3.4 %collective-permute-start = (f32[8,64,256]{2,1,0:T(8,128)S(1)}, f32[8,64,256]{2,1,0:T(8,128)S(1)}, u32[]{:S(2)}, u32[]{:S(2)}) collective-permute-start(f32[8,64,256]{2,1,0:T(8,128)S(1)} %all-to-all-done.e0), channel_id=1, source_target_pairs={{16,0},{32,16},{48,32},{0,48},{80,64},{96,80},{112,96},{64,112},{1... | collective-permute-start | bytes 1572872 | tf_op jit(solution)/shard_map/ppermute | solution.py:110
  44.9 15.6 %all_to_all.15 = f32[16,2,256]{2,1,0:T(2,128)S(1)} all-to-all(f32[16,2,256]{2,1,0:T(2,128)S(1)} %broadcast_in_dim.27), channel_id=1, replica_groups=mesh['row'=32,'col'=16] {'col'}, dimensions={0} | all-to-all | bytes 65536 | tf_op jit(solution)/shard_map/all_to_all | solution.py:99
  60.6 0.0 collective-permute-done.1.e3
  60.6 0.0 collective-permute-done.e1
  60.6 0.9 broadcast_in_dim.30
  61.5 3.9 %all-to-all-start.2 = ((f32[32,34,128]{2,1,0:T(8,128)}), f32[32,34,128]{2,1,0:T(8,128)S(1)}, u32[]{:S(2)}, u32[]{:S(2)}) async-start(f32[32,34,128]{2,1,0:T(8,128)} %broadcast_in_dim.30), calls=%async_computation.2 | async-start | bytes 1310720 | tf_op jit(solution)/shard_map/all_to_all | solution.py:99
  65.5 3.0 %collective-permute-start.3 = (f32[4,64,256]{2,1,0:T(8,128)S(1)}, f32[4,64,256]{2,1,0:T(8,128)S(1)}, u32[]{:S(2)}, u32[]{:S(2)}) collective-permute-start(f32[4,64,256]{2,1,0:T(8,128)S(1)} %slice.15), channel_id=1, source_target_pairs={{48,0},{0,16},{16,32},{32,48},{112,64},{64,80},{80,96},{96,112},{1... | collective-permute-start | bytes 786440 | tf_op jit(solution)/shard_map/ppermute | solution.py:125
  68.5 3.5 %collective-permute-start.2 = (f32[4,64,256]{2,1,0:T(8,128)S(1)}, f32[4,64,256]{2,1,0:T(8,128)S(1)}, u32[]{:S(2)}, u32[]{:S(2)}) collective-permute-start(f32[4,64,256]{2,1,0:T(8,128)S(1)} %slice.14), channel_id=1, source_target_pairs={{16,0},{32,16},{48,32},{0,48},{80,64},{96,80},{112,96},{64,112},{1... | collective-permute-start | bytes 786440 | tf_op jit(solution)/shard_map/ppermute | solution.py:124
  72.0 8.0 %collective-permute-done.3.e2_more = f32[4,64,256]{2,1,0:T(8,128)S(1)} collective-permute-done((f32[4,64,256]{2,1,0:T(8,128)S(1)}, f32[4,64,256]{2,1,0:T(8,128)S(1)}, u32[]{:S(2)}, u32[]{:S(2)}) %collective-permute-start.3) | collective-permute-done | bytes 262176 | tf_op jit(solution)/shard_map/ppermute | solution.py:125
  80.0 1.3 %collective-permute-done.2.e2 = f32[4,64,256]{2,1,0:T(8,128)S(1)} collective-permute-done((f32[4,64,256]{2,1,0:T(8,128)S(1)}, f32[4,64,256]{2,1,0:T(8,128)S(1)}, u32[]{:S(2)}, u32[]{:S(2)}) %collective-permute-start.2) | collective-permute-done | bytes 262176 | tf_op jit(solution)/shard_map/ppermute | solution.py:124
  81.3 3.2 %all-to-all-done.2.both = f32[32,34,128]{2,1,0:T(8,128)S(1)} async-done(((f32[32,34,128]{2,1,0:T(8,128)}), f32[32,34,128]{2,1,0:T(8,128)S(1)}, u32[]{:S(2)}, u32[]{:S(2)}) %all-to-all-start.2) | async-done | bytes 557088 | tf_op jit(solution)/shard_map/all_to_all | solution.py:99
  84.5 0.0 all-gather.3.cloned.1.call-done
  84.5 8.6 %shard_map.49 = (f32[1024,256]{1,0:T(8,128)}, f32[2,256]{1,0:T(2,128)}, f32[2,1024]{1,0:T(2,128)}) custom-call(s32[1]{0:T(128)} %bitcast.place, f32[16,1024,128]{2,1,0:T(8,128)} %bitcast.5, f32[8,64,256]{2,1,0:T(8,128)S(1)} %all-to-all-done.e0, f32[8,64,256]{2,1,0:T(8,128)S(1)} %collective-permute-done.e1, f32[4,64,256]{2,1,0:T(8,128)S(1)} %collective-permute-done.2.e2, ...), custom_call_target="tpu_custom_call" | custom-call | tf_op jit(solution)/shard_map/pallas_call | solution.py:73
  (10 shorter events, 0.1 us)
Async XLA Ops:
  7.2 77.3 %all-gather.3.cloned.1.call-start = ((), (), s32[]{:S(2)}) async-start(), calls=%async_computation.3 | async-start | bytes 8912896 | tf_op jit(solution)/shard_map/all_gather | solution.py:107
  9.6 28.8 %all-to-all-start = ((f32[8,64,256]{2,1,0:T(8,128)}), f32[8,64,256]{2,1,0:T(8,128)S(1)}, u32[]{:S(2)}, u32[]{:S(2)}) async-start(f32[8,64,256]{2,1,0:T(8,128)} %broadcast_in_dim.26), calls=%async_computation | async-start | bytes 1048576 | tf_op jit(solution)/shard_map/all_to_all | solution.py:99
  38.4 22.2 %collective-permute-start.1 = (f32[8,64,256]{2,1,0:T(8,128)S(1)}, f32[8,64,256]{2,1,0:T(8,128)S(1)}, u32[]{:S(2)}, u32[]{:S(2)}) collective-permute-start(f32[8,64,256]{2,1,0:T(8,128)S(1)} %all-to-all-done.e0), channel_id=1, source_target_pairs={{48,0},{0,16},{16,32},{32,48},{112,64},{64,80},{80,96},{96,112},{1... | collective-permute-start | bytes 1572872 | tf_op jit(solution)/shard_map/ppermute | solution.py:110
  41.5 19.1 %collective-permute-start = (f32[8,64,256]{2,1,0:T(8,128)S(1)}, f32[8,64,256]{2,1,0:T(8,128)S(1)}, u32[]{:S(2)}, u32[]{:S(2)}) collective-permute-start(f32[8,64,256]{2,1,0:T(8,128)S(1)} %all-to-all-done.e0), channel_id=1, source_target_pairs={{16,0},{32,16},{48,32},{0,48},{80,64},{96,80},{112,96},{64,112},{1... | collective-permute-start | bytes 1572872 | tf_op jit(solution)/shard_map/ppermute | solution.py:110
  61.5 23.0 %all-to-all-start.2 = ((f32[32,34,128]{2,1,0:T(8,128)}), f32[32,34,128]{2,1,0:T(8,128)S(1)}, u32[]{:S(2)}, u32[]{:S(2)}) async-start(f32[32,34,128]{2,1,0:T(8,128)} %broadcast_in_dim.30), calls=%async_computation.2 | async-start | bytes 1310720 | tf_op jit(solution)/shard_map/all_to_all | solution.py:99
  65.5 14.5 %collective-permute-start.3 = (f32[4,64,256]{2,1,0:T(8,128)S(1)}, f32[4,64,256]{2,1,0:T(8,128)S(1)}, u32[]{:S(2)}, u32[]{:S(2)}) collective-permute-start(f32[4,64,256]{2,1,0:T(8,128)S(1)} %slice.15), channel_id=1, source_target_pairs={{48,0},{0,16},{16,32},{32,48},{112,64},{64,80},{80,96},{96,112},{1... | collective-permute-start | bytes 786440 | tf_op jit(solution)/shard_map/ppermute | solution.py:125
  68.5 12.8 %collective-permute-start.2 = (f32[4,64,256]{2,1,0:T(8,128)S(1)}, f32[4,64,256]{2,1,0:T(8,128)S(1)}, u32[]{:S(2)}, u32[]{:S(2)}) collective-permute-start(f32[4,64,256]{2,1,0:T(8,128)S(1)} %slice.14), channel_id=1, source_target_pairs={{16,0},{32,16},{48,32},{0,48},{80,64},{96,80},{112,96},{64,112},{1... | collective-permute-start | bytes 786440 | tf_op jit(solution)/shard_map/ppermute | solution.py:124
Sparse Core Ops, SparseCore 0:
  10.1 64.8 all-gather.2

commit v10 on v8

--- a/solution.py
+++ b/solution.py
@@ -68,7 +68,6 @@
 
 def product(place, t, parts, both):
     blocks, m, wide = t.shape
-    whole = lambda a: pl.BlockSpec(a.shape, lambda i, s: (0,) * a.ndim)
     depth = blocks * wide
     return pl.pallas_call(
         product_kernel,
@@ -81,7 +80,7 @@
             num_scalar_prefetch=1,
             grid=(m // STEP,),
             in_specs=[pl.BlockSpec((blocks, STEP, wide), lambda i, s: (0, i, 0))]
-            + [whole(a) for a in (*parts, both)],
+            + [pl.BlockSpec(memory_space=pltpu.VMEM)] * (len(parts) + 1),
             out_specs=[
                 pl.BlockSpec((STEP, 256), lambda i, s: (i, 0)),
                 pl.BlockSpec((2, 256), lambda i, s: (0, 0)),

time: 98.9 us -> 98.9 us (level)
  no operation moved by 1% of the time
where the time goes in v10:
time: 98.9 us; the launch traced here: 98.3 us
  starting transfers between devices  27.8 us (28%)
  waiting for transfers between devices  26.8 us (27%)
  blocking collectives  15.6 us (16%)
  between operations  14.1 us (14%)
  Pallas kernels  8.68 us (9%)
  local copies, waits for them, and re-layouts  2.75 us (3%)
  matrix products  2.41 us (2%)
    all_to_all x2, waiting for transfers between devices, to_all(): lax.all_to_all(copies, axis, split_axis=0, concat_axis=0, axis_index_grou...  17.7 us
    all_to_all x1, blocking collectives, to_all(): lax.all_to_all(copies, axis, split_axis=0, concat_axis=0, axis_index_grou...  15.6 us
    all_to_all x2, starting transfers between devices, to_all(): lax.all_to_all(copies, axis, split_axis=0, concat_axis=0, axis_index_grou...  14.8 us
    pallas_call x1, Pallas kernels, product(): pl.pallas_call(product_kernel, out_shape=(jax.ShapeDtypeStruct((m, 256),...  8.68 us
    ppermute x1, waiting for transfers between devices, on_device(): lax.ppermute(before[NZ // 2:], 'row', from_x(3))  8.27 us
    ppermute x2, starting transfers between devices, on_device(): after, before = [lax.ppermute(near, 'row', from_x(d)) for d in (1, 3)]  6.48 us
    ppermute x1, starting transfers between devices, on_device(): lax.ppermute(after[:NZ // 2], 'row', from_x(1))  3.47 us
    ppermute x1, starting transfers between devices, on_device(): lax.ppermute(before[NZ // 2:], 'row', from_x(3))  3.03 us
  transfers between devices with their start and end apart: 7, of which 4 were waited for; matrix products, arithmetic and copies ran while one was open for 5% of the time, Pallas kernels for 0%

profile of v10, /device:TPU:1, one launch (start us, length us, event | category | flops | bytes accessed | tf_op | source)
XLA Modules:
  0.0 98.3 jit_solution(1813261511936044972)
XLA Ops:
  7.2 0.0 all-gather.3.cloned.1.call-start
  7.2 0.7 all-gather.3.cloned.1.call-update
  7.9 1.7 %broadcast_in_dim.11 = f32[8,64,256]{2,1,0:T(8,128)} broadcast(f32[64,256]{1,0:T(8,128)} %param.3), dimensions={1,2} | broadcast | bytes 589824 | tf_op jit(solution)/shard_map/broadcast_in_dim | solution.py:97
  9.6 10.9 %all-to-all-start = ((f32[8,64,256]{2,1,0:T(8,128)}), f32[8,64,256]{2,1,0:T(8,128)S(1)}, u32[]{:S(2)}, u32[]{:S(2)}) async-start(f32[8,64,256]{2,1,0:T(8,128)} %broadcast_in_dim.11), calls=%async_computation | async-start | bytes 1048576 | tf_op jit(solution)/shard_map/all_to_all | solution.py:98
  20.4 0.1 pad.6.clone
  20.5 1.0 fusion.2
  21.5 1.4 %fusion = f32[2,128]{1,0:T(2,128)S(1)} fusion(f32[1024,128]{1,0:T(8,128)} %param.2, f32[1,1024]{1,0:T(1,128)S(1)} %add_multiply_fusion), kind=kOutput, calls=%fused_computation.2 | convolution fusion | flops 3145728 | bytes 529408 | tf_op jit(solution)/shard_map/dot_general | solution.py:112
  23.0 15.4 %all-to-all-done.e0 = f32[8,64,256]{2,1,0:T(8,128)S(1)} async-done(((f32[8,64,256]{2,1,0:T(8,128)}), f32[8,64,256]{2,1,0:T(8,128)S(1)}, u32[]{:S(2)}, u32[]{:S(2)}) %all-to-all-start) | async-done | bytes 524320 | tf_op jit(solution)/shard_map/all_to_all | solution.py:98
  38.4 3.1 %collective-permute-start.1 = (f32[8,64,256]{2,1,0:T(8,128)S(1)}, f32[8,64,256]{2,1,0:T(8,128)S(1)}, u32[]{:S(2)}, u32[]{:S(2)}) collective-permute-start(f32[8,64,256]{2,1,0:T(8,128)S(1)} %all-to-all-done.e0), channel_id=1, source_target_pairs={{48,0},{0,16},{16,32},{32,48},{112,64},{64,80},{80,96},{96,112},{1... | collective-permute-start | bytes 1572872 | tf_op jit(solution)/shard_map/ppermute | solution.py:109
  41.5 3.4 %collective-permute-start = (f32[8,64,256]{2,1,0:T(8,128)S(1)}, f32[8,64,256]{2,1,0:T(8,128)S(1)}, u32[]{:S(2)}, u32[]{:S(2)}) collective-permute-start(f32[8,64,256]{2,1,0:T(8,128)S(1)} %all-to-all-done.e0), channel_id=1, source_target_pairs={{16,0},{32,16},{48,32},{0,48},{80,64},{96,80},{112,96},{64,112},{1... | collective-permute-start | bytes 1572872 | tf_op jit(solution)/shard_map/ppermute | solution.py:109
  44.9 15.6 %all_to_all.15 = f32[16,2,256]{2,1,0:T(2,128)S(1)} all-to-all(f32[16,2,256]{2,1,0:T(2,128)S(1)} %broadcast_in_dim.12), channel_id=1, replica_groups=mesh['row'=32,'col'=16] {'col'}, dimensions={0} | all-to-all | bytes 65536 | tf_op jit(solution)/shard_map/all_to_all | solution.py:98
  60.6 0.0 collective-permute-done.1.e3
  60.6 0.0 collective-permute-done.e1
  60.6 0.9 broadcast_in_dim.28
  61.6 3.9 %all-to-all-start.2 = ((f32[32,17,2,128]{3,2,1,0:T(2,128)}), f32[32,17,2,128]{3,2,1,0:T(2,128)S(1)}, u32[]{:S(2)}, u32[]{:S(2)}) async-start(f32[32,17,2,128]{3,2,1,0:T(2,128)} %broadcast_in_dim.28), calls=%async_computation.2 | async-start | bytes 1114112 | tf_op jit(solution)/shard_map/all_to_all | solution.py:98
  65.5 3.0 %collective-permute-start.3 = (f32[4,64,256]{2,1,0:T(8,128)S(1)}, f32[4,64,256]{2,1,0:T(8,128)S(1)}, u32[]{:S(2)}, u32[]{:S(2)}) collective-permute-start(f32[4,64,256]{2,1,0:T(8,128)S(1)} %slice.15), channel_id=1, source_target_pairs={{48,0},{0,16},{16,32},{32,48},{112,64},{64,80},{80,96},{96,112},{1... | collective-permute-start | bytes 786440 | tf_op jit(solution)/shard_map/ppermute | solution.py:124
  68.6 3.5 %collective-permute-start.2 = (f32[4,64,256]{2,1,0:T(8,128)S(1)}, f32[4,64,256]{2,1,0:T(8,128)S(1)}, u32[]{:S(2)}, u32[]{:S(2)}) collective-permute-start(f32[4,64,256]{2,1,0:T(8,128)S(1)} %slice.14), channel_id=1, source_target_pairs={{16,0},{32,16},{48,32},{0,48},{80,64},{96,80},{112,96},{64,112},{1... | collective-permute-start | bytes 786440 | tf_op jit(solution)/shard_map/ppermute | solution.py:123
  72.0 8.3 %collective-permute-done.3.e2_more = f32[4,64,256]{2,1,0:T(8,128)S(1)} collective-permute-done((f32[4,64,256]{2,1,0:T(8,128)S(1)}, f32[4,64,256]{2,1,0:T(8,128)S(1)}, u32[]{:S(2)}, u32[]{:S(2)}) %collective-permute-start.3) | collective-permute-done | bytes 262176 | tf_op jit(solution)/shard_map/ppermute | solution.py:124
  80.3 0.2 collective-permute-done.2.e2
  80.5 2.2 %all-to-all-done.2.both = f32[32,17,2,128]{3,2,1,0:T(2,128)S(1)} async-done(((f32[32,17,2,128]{3,2,1,0:T(2,128)}), f32[32,17,2,128]{3,2,1,0:T(2,128)S(1)}, u32[]{:S(2)}, u32[]{:S(2)}) %all-to-all-start.2) | async-done | bytes 557088 | tf_op jit(solution)/shard_map/all_to_all | solution.py:98
  82.7 0.0 all-gather.3.cloned.1.call-done
  82.7 8.7 %shard_map.49 = (f32[1024,256]{1,0:T(8,128)}, f32[2,256]{1,0:T(2,128)}, f32[2,1024]{1,0:T(2,128)}) custom-call(s32[1]{0:T(128)} %bitcast.place, f32[16,1024,128]{2,1,0:T(8,128)} %bitcast.5, f32[8,64,256]{2,1,0:T(8,128)S(1)} %all-to-all-done.e0, f32[8,64,256]{2,1,0:T(8,128)S(1)} %collective-permute-done.e1, f32[4,64,256]{2,1,0:T(8,128)S(1)} %collective-permute-done.2.e2, ...), custom_call_target="tpu_custom_call" | custom-call | tf_op jit(solution)/shard_map/pallas_call | solution.py:72
  (9 shorter events, 0.1 us)
Async XLA Ops:
  7.2 75.6 %all-gather.3.cloned.1.call-start = ((), (), s32[]{:S(2)}) async-start(), calls=%async_computation.3 | async-start | bytes 8912896 | tf_op jit(solution)/shard_map/all_gather | solution.py:106
  9.6 28.8 %all-to-all-start = ((f32[8,64,256]{2,1,0:T(8,128)}), f32[8,64,256]{2,1,0:T(8,128)S(1)}, u32[]{:S(2)}, u32[]{:S(2)}) async-start(f32[8,64,256]{2,1,0:T(8,128)} %broadcast_in_dim.11), calls=%async_computation | async-start | bytes 1048576 | tf_op jit(solution)/shard_map/all_to_all | solution.py:98
  38.4 22.2 %collective-permute-start.1 = (f32[8,64,256]{2,1,0:T(8,128)S(1)}, f32[8,64,256]{2,1,0:T(8,128)S(1)}, u32[]{:S(2)}, u32[]{:S(2)}) collective-permute-start(f32[8,64,256]{2,1,0:T(8,128)S(1)} %all-to-all-done.e0), channel_id=1, source_target_pairs={{48,0},{0,16},{16,32},{32,48},{112,64},{64,80},{80,96},{96,112},{1... | collective-permute-start | bytes 1572872 | tf_op jit(solution)/shard_map/ppermute | solution.py:109
  41.5 19.1 %collective-permute-start = (f32[8,64,256]{2,1,0:T(8,128)S(1)}, f32[8,64,256]{2,1,0:T(8,128)S(1)}, u32[]{:S(2)}, u32[]{:S(2)}) collective-permute-start(f32[8,64,256]{2,1,0:T(8,128)S(1)} %all-to-all-done.e0), channel_id=1, source_target_pairs={{16,0},{32,16},{48,32},{0,48},{80,64},{96,80},{112,96},{64,112},{1... | collective-permute-start | bytes 1572872 | tf_op jit(solution)/shard_map/ppermute | solution.py:109
  61.6 21.2 %all-to-all-start.2 = ((f32[32,17,2,128]{3,2,1,0:T(2,128)}), f32[32,17,2,128]{3,2,1,0:T(2,128)S(1)}, u32[]{:S(2)}, u32[]{:S(2)}) async-start(f32[32,17,2,128]{3,2,1,0:T(2,128)} %broadcast_in_dim.28), calls=%async_computation.2 | async-start | bytes 1114112 | tf_op jit(solution)/shard_map/all_to_all | solution.py:98
  65.5 14.8 %collective-permute-start.3 = (f32[4,64,256]{2,1,0:T(8,128)S(1)}, f32[4,64,256]{2,1,0:T(8,128)S(1)}, u32[]{:S(2)}, u32[]{:S(2)}) collective-permute-start(f32[4,64,256]{2,1,0:T(8,128)S(1)} %slice.15), channel_id=1, source_target_pairs={{48,0},{0,16},{16,32},{32,48},{112,64},{64,80},{80,96},{96,112},{1... | collective-permute-start | bytes 786440 | tf_op jit(solution)/shard_map/ppermute | solution.py:124
  68.6 11.9 %collective-permute-start.2 = (f32[4,64,256]{2,1,0:T(8,128)S(1)}, f32[4,64,256]{2,1,0:T(8,128)S(1)}, u32[]{:S(2)}, u32[]{:S(2)}) collective-permute-start(f32[4,64,256]{2,1,0:T(8,128)S(1)} %slice.14), channel_id=1, source_target_pairs={{16,0},{32,16},{48,32},{0,48},{80,64},{96,80},{112,96},{64,112},{1... | collective-permute-start | bytes 786440 | tf_op jit(solution)/shard_map/ppermute | solution.py:123
Sparse Core Ops, SparseCore 0:
  10.1 64.8 all-gather.2
